TPU v7x, 32 devices: a whole 2x2x4 slice. The times are simulated.
32 devices in a mesh: dp: 16 (over z, y, core), tensor: 2 (over x).
Axes of the slice: x: 2, y: 2, z: 4, core: 2. Of those that a mesh axis runs over, the one named last changes fastest.
Arguments:
- tokens: bfloat16 [32, 709, 768], P(('dp', 'tensor')), may hold values from -6 to 6
- text_len: int32 [32], P(('dp', 'tensor')), may hold values from 40 to 512, as said below
- box_coords: int32 [32, 2, 709], P(('dp', 'tensor')), may hold values from 0 to 1000
- w_query: bfloat16 [768, 768], P(None, 'tensor'), may hold values from -0.21875 to 0.21875
- b_query: bfloat16 [768], P('tensor'), may hold values from -3 to 3
- w_key: bfloat16 [768, 768], P(None, 'tensor'), may hold values from -0.21875 to 0.21875
- w_value: bfloat16 [768, 768], P(None, 'tensor'), may hold values from -0.21875 to 0.21875
- b_value: bfloat16 [768], P('tensor'), may hold values from -3 to 3
- w_out: bfloat16 [768, 768], P('tensor'), may hold values from -0.625 to 0.625
- b_out: bfloat16 [768], replicated, may hold values from -3 to 3
- table_seq: bfloat16 [12, 32], P('tensor'), may hold values from -3.5 to 3.5
- table_x: bfloat16 [12, 64], P('tensor'), may hold values from -3.5 to 3.5
- table_y: bfloat16 [12, 64], P('tensor'), may hold values from -3.5 to 3.5
- gain_attn: bfloat16 [768], replicated, may hold values from 0.099609375 to 1.8984375
- shift_attn: bfloat16 [768], replicated, may hold values from -1.75 to 1.75
- w_up: bfloat16 [768, 3072], P(None, 'tensor'), may hold values from -0.21875 to 0.21875
- b_up: bfloat16 [3072], P('tensor'), may hold values from -3 to 3
- w_down: bfloat16 [3072, 768], P('tensor'), may hold values from -0.21875 to 0.21875
- b_down: bfloat16 [768], replicated, may hold values from -3 to 3
- gain_ffn: bfloat16 [768], replicated, may hold values from 0.099609375 to 1.8984375
- shift_ffn: bfloat16 [768], replicated, may hold values from -1.75 to 1.75
- cotangent: bfloat16 [32, 709, 768], P(('dp', 'tensor')), may hold values from -6 to 6
Outputs:
- output: bfloat16 [32, 709, 768], P(('dp', 'tensor'))
- grad_tokens: float32 [32, 709, 768], P(('dp', 'tensor'))
- grad_w_query: float32 [768, 768], P(None, 'tensor')
- grad_b_query: float32 [768], P('tensor')
- grad_w_key: float32 [768, 768], P(None, 'tensor')
- grad_w_value: float32 [768, 768], P(None, 'tensor')
- grad_b_value: float32 [768], P('tensor')
- grad_w_out: float32 [768, 768], P('tensor')
- grad_b_out: float32 [768], replicated
- grad_table_seq: float32 [12, 32], P('tensor')
- grad_table_x: float32 [12, 64], P('tensor')
- grad_table_y: float32 [12, 64], P('tensor')
- grad_gain_attn: float32 [768], replicated
- grad_shift_attn: float32 [768], replicated
- grad_w_up: float32 [768, 3072], P(None, 'tensor')
- grad_b_up: float32 [3072], P('tensor')
- grad_w_down: float32 [3072, 768], P('tensor')
- grad_b_down: float32 [768], replicated
- grad_gain_ffn: float32 [768], replicated
- grad_shift_ffn: float32 [768], replicated
Inputs may be any that keep to these rules, and one draw needn't show every extreme that they name: `text_len`: text slots in use in each item, the rest are padding; in every draw some item uses all 512 and some only 40.
All inputs are finite; a program needn't handle non-finite values.
Results may differ from a plain program's by a relative error of at most 0.014.
The roundings to bfloat16 on the way count: a program that leaves them out, or rounds other values in their place, can miss the bound.
Values may be sent and summed in bfloat16 or wider, within the bound.
No kernel may reach another device: no remote copies, remote signals or barrier semaphores. Data moves between devices by JAX's collectives and lax.ppermute only.
A program may use at most 192 MiB of HBM per device.

v0:
```python
from functools import partial
import math

import jax
import jax.numpy as jnp
from jax import lax
from jax.sharding import PartitionSpec as P

HEAD_DIM = 64
BUCKETS = 32
MAX_DIST = 128
BUCKETS_2D = 64
MAX_DIST_2D = 256
TEXT = 512


layer_eps = 1e-05
masked_score = -1000000000.0


def bucket_edges(buckets, farthest):
    half_count = buckets // 2
    exact_count = half_count // 2
    result = list(range(1, exact_count + 1))
    for degree in range(1, exact_count):
        result.append(
            int(math.ceil(exact_count * (farthest / exact_count) ** (degree / exact_count) - 1e-09))
        )
    return result


def bucket_index(relative, buckets, farthest):
    distance = jnp.abs(relative)
    counted = (relative > 0).astype(jnp.int32) * (buckets // 2)
    for border in bucket_edges(buckets, farthest):
        counted = counted + (distance >= border).astype(jnp.int32)
    return counted


def item_buckets(box_item):
    places = jnp.arange(box_item.shape[1], dtype=jnp.int32)
    along_seq = bucket_index(places[None, :] - places[:, None], BUCKETS, MAX_DIST)
    across = box_item[0]
    along_x = bucket_index(across[None, :] - across[:, None], BUCKETS_2D, MAX_DIST_2D)
    upward = box_item[1]
    along_y = bucket_index(upward[None, :] - upward[:, None], BUCKETS_2D, MAX_DIST_2D)
    return (along_seq, along_x, along_y)


def one_hot_of(bucket, bucket_count):
    choices_all = jnp.arange(bucket_count, dtype=jnp.int32)[:, None, None]
    return (bucket[None] == choices_all).astype(jnp.bfloat16)


def item_scores(tables, query_item, key_item, length_now, box_item):
    scale_factor = query_item.shape[2] ** (-0.5)
    scores = (
        jnp.einsum("qhd,khd->hqk", query_item, key_item, preferred_element_type=jnp.float32)
        * scale_factor
    )
    bucket_sets = item_buckets(box_item)
    for bucket, bias_table in zip(bucket_sets, tables):
        scores = scores + jnp.einsum(
            "ngo,sn->sgo",
            one_hot_of(bucket, bias_table.shape[1]),
            bias_table,
            preferred_element_type=jnp.float32,
        )
    places = jnp.arange(scores.shape[2], dtype=jnp.int32)
    usable = (places < length_now) | (places >= TEXT)
    return (jnp.where(usable[None, None, :], scores, masked_score), bucket_sets)


def attend_forward(tables, packed):
    query_item, key_item, value_item, length_now, box_item = packed
    scores, bucket_sets = item_scores(tables, query_item, key_item, length_now, box_item)
    log_total = jax.nn.logsumexp(scores, axis=2)
    weights_low = jnp.exp(scores - log_total[:, :, None]).astype(jnp.bfloat16)
    context = jnp.einsum(
        "hqk,khd->qhd", weights_low, value_item, preferred_element_type=jnp.float32
    )
    return (context.astype(jnp.bfloat16), log_total)


def attend_backward(tables, packed):
    query_item, key_item, value_item, length_now, box_item, log_total, grad_context = packed
    scale_factor = query_item.shape[2] ** (-0.5)
    scores, bucket_sets = item_scores(tables, query_item, key_item, length_now, box_item)
    chances = jnp.exp(scores - log_total[:, :, None])
    grad_probs = jnp.einsum(
        "qhd,khd->hqk", grad_context, value_item, preferred_element_type=jnp.float32
    )
    grad_value = jnp.einsum(
        "hqk,qhd->khd",
        chances.astype(jnp.bfloat16),
        grad_context,
        preferred_element_type=jnp.float32,
    )
    inner_sum = jnp.sum(chances * grad_probs, axis=2, keepdims=True)
    grad_scores = (chances * (grad_probs - inner_sum)).astype(jnp.bfloat16)
    grad_query = (
        jnp.einsum("hqk,khd->qhd", grad_scores, key_item, preferred_element_type=jnp.float32)
        * scale_factor
    )
    grad_key = (
        jnp.einsum("hqk,qhd->khd", grad_scores, query_item, preferred_element_type=jnp.float32)
        * scale_factor
    )
    table_grads = []
    for bucket, bias_table in zip(bucket_sets, tables):
        table_grads.append(
            jnp.einsum(
                "fkm,pkm->pf",
                one_hot_of(bucket, bias_table.shape[1]),
                grad_scores,
                preferred_element_type=jnp.float32,
            )
        )
    return (
        grad_query.astype(jnp.bfloat16),
        grad_key.astype(jnp.bfloat16),
        grad_value.astype(jnp.bfloat16),
        table_grads[0],
        table_grads[1],
        table_grads[2],
    )


def norm_parts(values, gain, shift):
    center = values - jnp.mean(values, axis=1, keepdims=True)
    inverse = lax.rsqrt(jnp.mean(center * center, axis=1, keepdims=True) + layer_eps)
    scaled = center * inverse
    return (scaled * gain + shift, scaled, inverse)


def norm_back(grad_out, scaled, inverse, gain):
    grad_scaled = grad_out * gain
    return inverse * (
        grad_scaled
        - jnp.mean(grad_scaled, axis=1, keepdims=True)
        - scaled * jnp.mean(grad_scaled * scaled, axis=1, keepdims=True)
    )


def gelu_exact(values):
    return jax.nn.gelu(values, approximate=False)


def per_device(
    tokens,
    text_len,
    box_coords,
    w_query,
    b_query,
    w_key,
    w_value,
    b_value,
    w_out,
    b_out,
    table_seq,
    table_x,
    table_y,
    gain_attn,
    shift_attn,
    w_up,
    b_up,
    w_down,
    b_down,
    gain_ffn,
    shift_ffn,
    cotangent,
):
    own_items, seq_len, model_width = tokens.shape
    all_tokens, all_lengths, all_boxes = (
        lax.all_gather(tokens, "tensor", axis=0, tiled=True),
        lax.all_gather(text_len, "tensor", axis=0, tiled=True),
        lax.all_gather(box_coords, "tensor", axis=0, tiled=True),
    )
    pair_items = all_tokens.shape[0]
    pair_rows = pair_items * seq_len
    own_rows = own_items * seq_len
    local_width = w_query.shape[1]
    local_heads = local_width // HEAD_DIM
    head_shape = (pair_items, seq_len, local_heads, HEAD_DIM)
    tables = (table_seq, table_x, table_y)
    flat_tokens = all_tokens.reshape(pair_rows, model_width)
    query_flat = (
        jnp.dot(flat_tokens, w_query, preferred_element_type=jnp.float32) + b_query
    ).astype(jnp.bfloat16)
    key_flat = jnp.dot(flat_tokens, w_key, preferred_element_type=jnp.float32).astype(jnp.bfloat16)
    value_flat = (
        jnp.dot(flat_tokens, w_value, preferred_element_type=jnp.float32) + b_value
    ).astype(jnp.bfloat16)
    query_heads = query_flat.reshape(head_shape)
    key_heads = key_flat.reshape(head_shape)
    value_heads = value_flat.reshape(head_shape)
    context, log_totals = lax.map(
        partial(attend_forward, tables),
        (query_heads, key_heads, value_heads, all_lengths, all_boxes),
    )
    context_flat = context.reshape(pair_rows, local_width)
    piece = lax.slice_in_dim(context_flat, 0, own_rows * lax.axis_size("tensor"), axis=0)
    attn_own = (
        lax.psum_scatter(
            jnp.dot(piece, w_out, preferred_element_type=jnp.float32),
            "tensor",
            scatter_dimension=0,
            tiled=True,
        )
        + b_out
    )
    own_tokens = tokens.reshape(own_rows, model_width).astype(jnp.float32)
    normed, first_scaled, first_inverse = norm_parts(own_tokens + attn_own, gain_attn, shift_attn)
    normed_all = lax.all_gather(normed.astype(jnp.bfloat16), "tensor", axis=0, tiled=True)
    hidden_pre = jnp.dot(normed_all, w_up, preferred_element_type=jnp.float32) + b_up
    activated = gelu_exact(hidden_pre).astype(jnp.bfloat16)
    piece = lax.slice_in_dim(activated, 0, own_rows * lax.axis_size("tensor"), axis=0)
    branch = (
        lax.psum_scatter(
            jnp.dot(piece, w_down, preferred_element_type=jnp.float32),
            "tensor",
            scatter_dimension=0,
            tiled=True,
        )
        + b_down
    )
    result, second_scaled, second_inverse = norm_parts(normed + branch, gain_ffn, shift_ffn)
    output = result.astype(jnp.bfloat16).reshape(tokens.shape)
    grad_result = cotangent.reshape(own_rows, model_width).astype(jnp.float32)
    grad_gain_ffn = jnp.sum(grad_result * second_scaled, axis=0)
    grad_shift_ffn = jnp.sum(grad_result, axis=0)
    grad_mid = norm_back(grad_result, second_scaled, second_inverse, gain_ffn)
    grad_branch = grad_mid.astype(jnp.bfloat16)
    grad_b_down = jnp.sum(grad_branch.astype(jnp.float32), axis=0)
    branch_all = lax.all_gather(grad_branch, "tensor", axis=0, tiled=True)
    grad_w_down = jnp.einsum("rf,rd->fd", activated, branch_all, preferred_element_type=jnp.float32)
    grad_act = jnp.einsum("rd,fd->rf", branch_all, w_down, preferred_element_type=jnp.float32)
    gelu_pull = jax.vjp(gelu_exact, hidden_pre)[1]
    grad_hidden = gelu_pull(grad_act)[0].astype(jnp.bfloat16)
    grad_b_up = jnp.sum(grad_hidden.astype(jnp.float32), axis=0)
    grad_w_up = jnp.einsum("rd,rf->df", normed_all, grad_hidden, preferred_element_type=jnp.float32)
    piece = lax.slice_in_dim(grad_hidden, 0, own_rows * lax.axis_size("tensor"), axis=0)
    grad_normed = (
        lax.psum_scatter(
            jnp.einsum("rf,df->rd", piece, w_up, preferred_element_type=jnp.float32),
            "tensor",
            scatter_dimension=0,
            tiled=True,
        )
        + grad_mid
    )
    grad_gain_attn = jnp.sum(grad_normed * first_scaled, axis=0)
    grad_shift_attn = jnp.sum(grad_normed, axis=0)
    grad_first = norm_back(grad_normed, first_scaled, first_inverse, gain_attn)
    grad_attn = grad_first.astype(jnp.bfloat16)
    grad_b_out = jnp.sum(grad_attn.astype(jnp.float32), axis=0)
    attn_all = lax.all_gather(grad_attn, "tensor", axis=0, tiled=True)
    grad_w_out = jnp.einsum("rc,rd->cd", context_flat, attn_all, preferred_element_type=jnp.float32)
    grad_context = jnp.einsum(
        "rd,cd->rc", attn_all, w_out, preferred_element_type=jnp.float32
    ).astype(jnp.bfloat16)
    grad_q_heads, grad_k_heads, grad_v_heads, seq_parts, x_parts, y_parts = lax.map(
        partial(attend_backward, tables),
        (
            query_heads,
            key_heads,
            value_heads,
            all_lengths,
            all_boxes,
            log_totals,
            grad_context.reshape(head_shape),
        ),
    )
    grad_table_seq = jnp.sum(seq_parts, axis=0)
    grad_table_x = jnp.sum(x_parts, axis=0)
    grad_table_y = jnp.sum(y_parts, axis=0)
    grad_query_flat = grad_q_heads.reshape(pair_rows, local_width)
    grad_key_flat = grad_k_heads.reshape(pair_rows, local_width)
    grad_value_flat = grad_v_heads.reshape(pair_rows, local_width)
    grad_b_query = jnp.sum(grad_query_flat.astype(jnp.float32), axis=0)
    grad_b_value = jnp.sum(grad_value_flat.astype(jnp.float32), axis=0)
    grad_w_query = jnp.einsum(
        "rd,rc->dc", flat_tokens, grad_query_flat, preferred_element_type=jnp.float32
    )
    grad_w_key = jnp.einsum(
        "rd,rc->dc", flat_tokens, grad_key_flat, preferred_element_type=jnp.float32
    )
    grad_w_value = jnp.einsum(
        "rd,rc->dc", flat_tokens, grad_value_flat, preferred_element_type=jnp.float32
    )
    query_piece = lax.slice_in_dim(grad_query_flat, 0, own_rows * lax.axis_size("tensor"), axis=0)
    key_piece = lax.slice_in_dim(grad_key_flat, 0, own_rows * lax.axis_size("tensor"), axis=0)
    value_piece = lax.slice_in_dim(grad_value_flat, 0, own_rows * lax.axis_size("tensor"), axis=0)
    summed = jnp.einsum("rc,dc->rd", query_piece, w_query, preferred_element_type=jnp.float32)
    summed = summed + jnp.einsum("rc,dc->rd", key_piece, w_key, preferred_element_type=jnp.float32)
    grad_tokens = (
        lax.psum_scatter(
            (
                summed
                + jnp.einsum("rc,dc->rd", value_piece, w_value, preferred_element_type=jnp.float32)
            ).astype(jnp.bfloat16),
            "tensor",
            scatter_dimension=0,
            tiled=True,
        ).astype(jnp.float32)
        + grad_first
    ).reshape(tokens.shape)
    (
        grad_w_query,
        grad_b_query,
        grad_w_key,
        grad_w_value,
        grad_b_value,
        grad_w_out,
        grad_table_seq,
        grad_table_x,
        grad_table_y,
        grad_w_up,
        grad_b_up,
        grad_w_down,
    ) = lax.psum(
        (
            grad_w_query,
            grad_b_query,
            grad_w_key,
            grad_w_value,
            grad_b_value,
            grad_w_out,
            grad_table_seq,
            grad_table_x,
            grad_table_y,
            grad_w_up,
            grad_b_up,
            grad_w_down,
        ),
        "dp",
    )
    grad_b_out, grad_gain_attn, grad_shift_attn, grad_b_down, grad_gain_ffn, grad_shift_ffn = (
        lax.psum(
            (
                grad_b_out,
                grad_gain_attn,
                grad_shift_attn,
                grad_b_down,
                grad_gain_ffn,
                grad_shift_ffn,
            ),
            ("dp", "tensor"),
        )
    )
    return (
        output,
        grad_tokens,
        grad_w_query,
        grad_b_query,
        grad_w_key,
        grad_w_value,
        grad_b_value,
        grad_w_out,
        grad_b_out,
        grad_table_seq,
        grad_table_x,
        grad_table_y,
        grad_gain_attn,
        grad_shift_attn,
        grad_w_up,
        grad_b_up,
        grad_w_down,
        grad_b_down,
        grad_gain_ffn,
        grad_shift_ffn,
    )


def solution(mesh):
    placed = (
        P(("dp", "tensor"), None, None),
        P(("dp", "tensor")),
        P(("dp", "tensor"), None, None),
        P(None, "tensor"),
        P("tensor"),
        P(None, "tensor"),
        P(None, "tensor"),
        P("tensor"),
        P("tensor", None),
        P(),
        P("tensor", None),
        P("tensor", None),
        P("tensor", None),
        P(),
        P(),
        P(None, "tensor"),
        P("tensor"),
        P("tensor", None),
        P(),
        P(),
        P(),
        P(("dp", "tensor"), None, None),
    )
    return jax.shard_map(
        per_device,
        mesh=mesh,
        in_specs=placed,
        out_specs=(
            P(("dp", "tensor"), None, None),
            P(("dp", "tensor"), None, None),
            P(None, "tensor"),
            P("tensor"),
            P(None, "tensor"),
            P(None, "tensor"),
            P("tensor"),
            P("tensor", None),
            P(),
            P("tensor", None),
            P("tensor", None),
            P("tensor", None),
            P(),
            P(),
            P(None, "tensor"),
            P("tensor"),
            P("tensor", None),
            P(),
            P(),
            P(),
        ),
        check_vma=False,
    )
```

profile of v0, /device:TPU:0, one launch (start us, length us, event | category | flops | bytes accessed | tf_op | source)
XLA Modules:
  0.0 1661.8 jit_solution(2636062535177111499)
XLA Ops:
  22.4 24.1 %all-gather.8.cloned.1.call-done = bf16[2,709,768]{2,1,0:T(8,128)(2,1)} async-done(((bf16[1,709,768]{2,1,0:T(8,128)(2,1)}), bf16[2,709,768]{2,1,0:T(8,128)(2,1)}) %all-gather.8.cloned.1.call-update) | async-done | bytes 2178064 | tf_op jit(solution)/shard_map/all_gather | solution.py:175
  80.3 336.9 %while.32 = (s32[]{:T(128)}, bf16[2,709,6,64]{1,3,2,0:T(8,128)(2,1)}, f32[2,6,709]{2,1,0:T(8,128)}, bf16[2,709,6,64]{1,3,2,0:T(8,128)(2,1)}, s32[2]{0:T(128)S(1)...) while((s32[]{:T(128)}, ...), condition=%wide.region_3.4_spmd, body=%wide.region_0.3_spmd.sunk | while | flops 1970315136 | bytes 247058272 | solution.py:197
  99.0 15.3 convert_add_fusion.10
  114.3 22.8 %fusion.374 = f32[709,709,6]{1,2,0:T(8,128)} fusion(s32[709,709]{1,0:T(8,128)S(1)} %get-tuple-element.649, bf16[6,64]{1,0:T(8,128)(2,1)S(1)} %get-tuple-element.714), kind=kOutput, calls=%fused_computation.3.clone.1 | convolution fusion | flops 418230592 | bytes 14075836 | tf_op jit(solution)/shard_map/while/body/eval_jaxpr/ngo,sn->sgo/dot_general | solution.py:63
  137.1 16.4 copy.173
  153.5 13.8 fusion.376
  167.3 16.4 copy.175
  183.7 23.8 %fusion.375 = f32[709,709,6]{1,2,0:T(8,128)} fusion(s32[709,709]{1,0:T(8,128)} %get-tuple-element.650, bf16[6,64]{1,0:T(8,128)(2,1)S(1)} %get-tuple-element.713), kind=kOutput, calls=%fused_computation.2.clone.1 | convolution fusion | flops 418230592 | bytes 14075836 | tf_op jit(solution)/shard_map/while/body/eval_jaxpr/ngo,sn->sgo/dot_general | solution.py:63
  207.5 16.4 copy.174
  223.9 19.2 %fusion.378 = (f32[6,709]{1,0:T(8,128)S(1)}, f32[6,709,709]{1,2,0:T(8,128)}) fusion(f32[709,709,6]{0,1,2:T(8,128)} %copy.173, f32[709,709,6]{0,1,2:T(8,128)} %copy.174, f32[709,709,6]{0,1,2:T(8,128)} %copy.175, bf16[2,709,6,64]{1,3,2,0:T(8,128)(2,1)} %get-tuple-element.710, s32[]{:T(128)S(6)} %copy.192, ...), kind=kOutput, calls=%fused_computation.364.clone.1 | convolution fusion | flops 404151328 | bytes 52633492 | tf_op jit(solution)/shard_map/while/body/eval_jaxpr/qhd,khd->hqk/dot_general | solution.py:58
  243.1 6.7 exponential_reduce_fusion.2
  259.7 15.3 convert_add_fusion.10
  275.1 22.8 %fusion.374 = f32[709,709,6]{1,2,0:T(8,128)} fusion(s32[709,709]{1,0:T(8,128)S(1)} %get-tuple-element.649, bf16[6,64]{1,0:T(8,128)(2,1)S(1)} %get-tuple-element.714), kind=kOutput, calls=%fused_computation.3.clone.1 | convolution fusion | flops 418230592 | bytes 14075836 | tf_op jit(solution)/shard_map/while/body/eval_jaxpr/ngo,sn->sgo/dot_general | solution.py:63
  297.9 16.4 copy.173
  314.3 13.8 fusion.376
  328.1 16.4 copy.175
  344.4 23.8 %fusion.375 = f32[709,709,6]{1,2,0:T(8,128)} fusion(s32[709,709]{1,0:T(8,128)} %get-tuple-element.650, bf16[6,64]{1,0:T(8,128)(2,1)S(1)} %get-tuple-element.713), kind=kOutput, calls=%fused_computation.2.clone.1 | convolution fusion | flops 418230592 | bytes 14075836 | tf_op jit(solution)/shard_map/while/body/eval_jaxpr/ngo,sn->sgo/dot_general | solution.py:63
  368.2 16.4 copy.174
  384.6 19.0 %fusion.378 = (f32[6,709]{1,0:T(8,128)S(1)}, f32[6,709,709]{1,2,0:T(8,128)}) fusion(f32[709,709,6]{0,1,2:T(8,128)} %copy.173, f32[709,709,6]{0,1,2:T(8,128)} %copy.174, f32[709,709,6]{0,1,2:T(8,128)} %copy.175, bf16[2,709,6,64]{1,3,2,0:T(8,128)(2,1)} %get-tuple-element.710, s32[]{:T(128)S(6)} %copy.192, ...), kind=kOutput, calls=%fused_computation.364.clone.1 | convolution fusion | flops 404151328 | bytes 52633492 | tf_op jit(solution)/shard_map/while/body/eval_jaxpr/qhd,khd->hqk/dot_general | solution.py:58
  403.6 6.7 exponential_reduce_fusion.2
  428.5 54.7 %fusion = f32[712,768]{1,0:T(8,128)} fusion(f32[1418,768]{1,0:T(8,128)} %fusion.283), kind=kCustom, calls=%all-reduce-scatter | all-reduce-scatter fusion | flops 1093633 | bytes 6543872
  489.9 7.6 concatenate
  504.2 34.5 %all-gather.10.cloned.1.call-done = bf16[2,709,768]{2,1,0:T(8,128)(2,1)} async-done(((bf16[1,709,768]{2,1,0:T(8,128)(2,1)}), bf16[2,709,768]{2,1,0:T(8,128)(2,1)}) %all-gather.10.cloned.1.call-update) | async-done | bytes 2178064 | tf_op jit(solution)/shard_map/all_gather | solution.py:214
  542.1 24.7 %multiply_convert_fusion.1 = (bf16[1418,1536]{1,0:T(8,128)(2,1)S(1)}, f32[1418,1536]{1,0:T(8,128)}, f32[1418,1536]{1,0:T(8,128)}) fusion(f32[1536]{0:T(1024)} %convert_element_type.1261, bf16[1418,768]{1,0:T(8,128)(2,1)} %reshape.842, bf16[768,1536]{1,0:T(8,128)(2,1)S(1)} %copy-done), kind=kOutput, calls=%fused_computation.294 | convolution fusion | flops 3489232896 | bytes 26323968 | tf_op jit(solution)/shard_map/dot_general | solution.py:215
  573.9 54.5 %fusion.1 = f32[712,768]{1,0:T(8,128)} fusion(f32[1418,768]{1,0:T(8,128)} %fusion.284), kind=kCustom, calls=%all-reduce-scatter.1 | all-reduce-scatter fusion | flops 1093633 | bytes 6543872
  637.1 7.8 concatenate.1
  655.8 34.2 %all-gather.12.cloned.1.call-done = bf16[2,709,768]{2,1,0:T(8,128)(2,1)} async-done(((bf16[1,709,768]{2,1,0:T(8,128)(2,1)}), bf16[2,709,768]{2,1,0:T(8,128)(2,1)}) %all-gather.12.cloned.1.call-update) | async-done | bytes 2178064 | tf_op jit(solution)/shard_map/all_gather | solution.py:235
  693.5 12.5 convert_reduce_fusion
  713.1 53.6 %fusion.2 = f32[712,768]{1,0:T(8,128)S(1)} fusion(f32[1418,768]{1,0:T(8,128)} %fusion.285), kind=kCustom, calls=%all-reduce-scatter.2 | all-reduce-scatter fusion | flops 1093633 | bytes 6543872
  773.1 6.9 concatenate.2
  788.2 9.2 fusion.290
  797.4 8.0 fusion.289
  805.4 18.5 %all-gather.14.cloned.1.call-done = bf16[2,709,768]{2,1,0:T(8,128)(2,1)} async-done(((bf16[1,709,768]{2,1,0:T(8,128)(2,1)}), bf16[2,709,768]{2,1,0:T(8,128)(2,1)}) %all-gather.14.cloned.1.call-update) | async-done | bytes 2178064 | tf_op jit(solution)/shard_map/all_gather | solution.py:257
  836.7 510.8 %while.33 = (s32[]{:T(128)}, bf16[2,709,6,64]{1,3,2,0:T(8,128)(2,1)}, bf16[2,709,6,64]{1,3,2,0:T(8,128)(2,1)}, bf16[2,709,6,64]{1,3,2,0:T(8,128)(2,1)}, f32[2,6,...) while((s32[]{:T(128)}, ...), condition=%wide.region_17.18_spmd, body=%wide.region_15.17_spmd.sunk | while | flops 4181151488 | bytes 430567936 | solution.py:262
  839.3 15.4 convert_add_fusion.12
  861.4 22.8 %fusion.398 = f32[709,709,6]{1,2,0:T(8,128)} fusion(s32[709,709]{1,0:T(8,128)S(1)} %get-tuple-element.672, bf16[6,64]{1,0:T(8,128)(2,1)S(1)} %get-tuple-element.771), kind=kOutput, calls=%fused_computation.131.clone.1 | convolution fusion | flops 418230592 | bytes 14075836 | tf_op jit(solution)/shard_map/while/body/eval_jaxpr/ngo,sn->sgo/dot_general | solution.py:63
  884.2 16.4 copy.176
  900.5 24.0 %fusion.399 = f32[709,709,6]{1,2,0:T(8,128)} fusion(s32[709,709]{1,0:T(8,128)} %get-tuple-element.673, bf16[6,64]{1,0:T(8,128)(2,1)S(1)} %get-tuple-element.770), kind=kOutput, calls=%fused_computation.134.clone.1 | convolution fusion | flops 418230592 | bytes 14075836 | tf_op jit(solution)/shard_map/while/body/eval_jaxpr/ngo,sn->sgo/dot_general | solution.py:63
  924.5 16.4 copy.177
  940.9 13.0 fusion.400
  953.9 16.4 copy.178
  970.3 24.4 %multiply_reduce_fusion.7 = (f32[6,709]{1,0:T(8,128)S(1)}, f32[6,709,709]{1,2,0:T(8,128)}) fusion(f32[6,709,709]{1,2,0:T(8,128)} %fusion.396, f32[6,709]{1,0:T(8,128)S(1)} %dynamic-slice_bitcast_fusion.2, f32[709,709,6]{0,1,2:T(8,128)} %copy.176, f32[709,709,6]{0,1,2:T(8,128)} %copy.177, f32[709,709,6]{0,1,2:T(8,128)} %copy.178, ...), kind=kOutput, calls=%fused_computation.151.clone.1 | convolution fusion | flops 410183520 | bytes 65774092 | tf_op jit(solution)/shard_map/while/body/eval_jaxpr/qhd,khd->hqk/dot_general | solution.py:58
  994.7 9.9 multiply_convert_fusion.3
  1017.0 12.3 copy.179
  1029.4 24.2 %fusion.407 = f32[2,6,64]{2,1,0:T(8,128)S(1)} fusion(f32[2,6,64]{2,1,0:T(8,128)S(1)} %get-tuple-element.744, s32[]{:T(128)S(6)} %copy.205, bf16[6,709,709]{2,0,1:T(8,128)(2,1)} %copy.179, s32[709,709]{1,0:T(8,128)} %copy-done.9), kind=kOutput, calls=%fused_computation.257.clone.1 | convolution fusion | flops 418230592 | bytes 8046996 | tf_op jit(solution)/shard_map/while/body/eval_jaxpr/fkm,pkm->pf/dot_general | solution.py:112
  1053.6 23.2 %fusion.406 = f32[2,6,64]{2,1,0:T(8,128)S(1)} fusion(f32[2,6,64]{2,1,0:T(8,128)S(1)} %get-tuple-element.743, s32[]{:T(128)S(6)} %copy.205, bf16[6,709,709]{2,0,1:T(8,128)(2,1)S(1)} %copy-done.5, s32[709,709]{1,0:T(8,128)S(1)} %copy-done.8), kind=kOutput, calls=%fused_computation.255.clone.1 | convolution fusion | flops 418230592 | bytes 10903556 | tf_op jit(solution)/shard_map/while/body/eval_jaxpr/fkm,pkm->pf/dot_general | solution.py:112
  1076.8 11.7 fusion.405
  1090.9 15.4 convert_add_fusion.12
  1112.9 22.8 %fusion.398 = f32[709,709,6]{1,2,0:T(8,128)} fusion(s32[709,709]{1,0:T(8,128)S(1)} %get-tuple-element.672, bf16[6,64]{1,0:T(8,128)(2,1)S(1)} %get-tuple-element.771), kind=kOutput, calls=%fused_computation.131.clone.1 | convolution fusion | flops 418230592 | bytes 14075836 | tf_op jit(solution)/shard_map/while/body/eval_jaxpr/ngo,sn->sgo/dot_general | solution.py:63
  1135.7 16.4 copy.176
  1152.0 24.0 %fusion.399 = f32[709,709,6]{1,2,0:T(8,128)} fusion(s32[709,709]{1,0:T(8,128)} %get-tuple-element.673, bf16[6,64]{1,0:T(8,128)(2,1)S(1)} %get-tuple-element.770), kind=kOutput, calls=%fused_computation.134.clone.1 | convolution fusion | flops 418230592 | bytes 14075836 | tf_op jit(solution)/shard_map/while/body/eval_jaxpr/ngo,sn->sgo/dot_general | solution.py:63
  1176.0 16.4 copy.177
  1192.4 13.0 fusion.400
  1205.4 16.4 copy.178
  1221.8 24.3 %multiply_reduce_fusion.7 = (f32[6,709]{1,0:T(8,128)S(1)}, f32[6,709,709]{1,2,0:T(8,128)}) fusion(f32[6,709,709]{1,2,0:T(8,128)} %fusion.396, f32[6,709]{1,0:T(8,128)S(1)} %dynamic-slice_bitcast_fusion.2, f32[709,709,6]{0,1,2:T(8,128)} %copy.176, f32[709,709,6]{0,1,2:T(8,128)} %copy.177, f32[709,709,6]{0,1,2:T(8,128)} %copy.178, ...), kind=kOutput, calls=%fused_computation.151.clone.1 | convolution fusion | flops 410183520 | bytes 65774092 | tf_op jit(solution)/shard_map/while/body/eval_jaxpr/qhd,khd->hqk/dot_general | solution.py:58
  1246.2 10.1 multiply_convert_fusion.3
  1268.5 12.3 copy.179
  1280.9 24.2 %fusion.407 = f32[2,6,64]{2,1,0:T(8,128)S(1)} fusion(f32[2,6,64]{2,1,0:T(8,128)S(1)} %get-tuple-element.744, s32[]{:T(128)S(6)} %copy.205, bf16[6,709,709]{2,0,1:T(8,128)(2,1)} %copy.179, s32[709,709]{1,0:T(8,128)} %copy-done.9), kind=kOutput, calls=%fused_computation.257.clone.1 | convolution fusion | flops 418230592 | bytes 8046996 | tf_op jit(solution)/shard_map/while/body/eval_jaxpr/fkm,pkm->pf/dot_general | solution.py:112
  1305.1 23.0 %fusion.406 = f32[2,6,64]{2,1,0:T(8,128)S(1)} fusion(f32[2,6,64]{2,1,0:T(8,128)S(1)} %get-tuple-element.743, s32[]{:T(128)S(6)} %copy.205, bf16[6,709,709]{2,0,1:T(8,128)(2,1)S(1)} %copy-done.5, s32[709,709]{1,0:T(8,128)S(1)} %copy-done.8), kind=kOutput, calls=%fused_computation.255.clone.1 | convolution fusion | flops 418230592 | bytes 10903556 | tf_op jit(solution)/shard_map/while/body/eval_jaxpr/fkm,pkm->pf/dot_general | solution.py:112
  1328.1 11.7 fusion.405
  1378.9 42.1 %all-reduce.9 = (f32[768]{0:T(1024)}, f32[768]{0:T(1024)}, f32[768]{0:T(1024)}, f32[768]{0:T(1024)}, f32[768]{0:T(1024)}, /*index=5*/f32[768]{0:T(1024)}) all-reduce(f32[768]{0:T(1024)S(1)} %copy-done.44, f32[768]{0:T(1024)S(1)} %copy-done.42, f32[768]{0:T(1024)S(1)} %copy-done.43, ...), channel_id=1, replica_groups=mesh['dp'=16,'tensor'=2] {'dp','tensor'}, use_global_device_ids=true, to_apply=%region_28.29 | all-reduce | flops 4608 | bytes 36864 | tf_op jit(solution)/shard_map/psum | solution.py:339
  1426.6 30.4 %fusion.3 = bf16[712,768]{1,0:T(8,128)(2,1)} fusion(bf16[1418,768]{1,0:T(8,128)(2,1)S(1)} %add_convert_fusion.1), kind=kCustom, calls=%all-reduce-scatter.3 | all-reduce-scatter fusion | flops 1093633 | bytes 3272192
  1462.4 59.9 %all-reduce.10 = (f32[384]{0:T(512)}, f32[384]{0:T(512)}, f32[6,32]{1,0:T(8,128)}, f32[6,64]{1,0:T(8,128)}, f32[6,64]{1,0:T(8,128)}, /*index=5*/f32[1536]{0:T(1024)}) all-reduce(f32[384]{0:T(512)S(1)} %reduce_sum.211, f32[384]{0:T(512)S(1)} %reduce_sum.213, ...), channel_id=1, replica_groups=mesh['dp'=16,'tensor'=2] {'dp'}, use_global_device_ids=true, to_apply=%region_21.22 | all-reduce | flops 3264 | bytes 26112 | tf_op jit(solution)/shard_map/psum | solution.py:321
  1531.2 108.3 %all-reduce.14.cloned.1.call-done = (f32[768,384]{0,1:T(8,128)}, f32[768,384]{0,1:T(8,128)}, f32[768,384]{0,1:T(8,128)}, f32[384,768]{1,0:T(8,128)}, f32[768,1536]{1,0:T(8,128)}, /*index=5*/f32[1536,768]{1,0:T(8,128)}) async-done(((f32[768,384]{0,1:T(8,128)}, f32[768,384]{0,1:T(8,128)}, f32[768,384]{0,1:T(8,128)}, f32[384,768]{1,0:T(8,128)}, f32[768,1536]{1,0:T(8,128)}, /*index=5*/f32[1536,768]{1,0:T(8,128)}), ...) | async-done | bytes 14155792 | tf_op jit(solution)/shard_map/psum | solution.py:321
  (296 shorter events, 268.8 us)
Async XLA Ops:
  7.2 534.9 %copy-start = (bf16[768,1536]{1,0:T(8,128)(2,1)S(1)}, bf16[768,1536]{1,0:T(8,128)(2,1)}, u32[]{:S(2)}) copy-start(bf16[768,1536]{1,0:T(8,128)(2,1)} %param.41) | copy-start | bytes 7077892
  7.2 39.3 %all-gather.8.cloned.1.call-start = ((), (), s32[]{:S(2)}) async-start(), calls=%async_computation | async-start | bytes 3280896 | tf_op jit(solution)/shard_map/all_gather | solution.py:175
  7.9 530.7 %all-gather.10.cloned.1.call-start = ((), (), s32[]{:S(2)}) async-start(), calls=%async_computation.1 | async-start | bytes 3280896 | tf_op jit(solution)/shard_map/all_gather | solution.py:214
  22.4 27.5 %copy-start.33 = (bf16[768,384]{1,0:T(8,128)(2,1)S(1)}, bf16[768,384]{1,0:T(8,128)(2,1)}, u32[]{:S(2)}) copy-start(bf16[768,384]{1,0:T(8,128)(2,1)} %param.32) | copy-start | bytes 1769476
  57.4 2.6 copy-start.24
  67.0 2.6 copy-start.25
  76.6 3.6 copy-start.38
  76.6 3.6 copy-start.52
  76.6 3.6 copy-start.54
  76.6 3.6 copy-start.56
  243.1 8.5 copy-start.4
  403.6 8.5 copy-start.4
  417.2 6.9 copy-start.35
  428.5 60.7 %copy-start.49 = (bf16[768]{0:T(1024)(128)(2,1)S(1)}, bf16[768]{0:T(1024)(128)(2,1)}, u32[]{:S(2)}) copy-start(bf16[768]{0:T(1024)(128)(2,1)} %param.39) | copy-start | bytes 4612
  428.5 60.7 %copy-start.50 = (bf16[768]{0:T(1024)(128)(2,1)S(1)}, bf16[768]{0:T(1024)(128)(2,1)}, u32[]{:S(2)}) copy-start(bf16[768]{0:T(1024)(128)(2,1)} %param.40) | copy-start | bytes 4612
  484.6 5.4 collective-permute-start
  502.8 187.3 %all-gather.12.cloned.1.call-start = ((), (), s32[]{:S(2)}) async-start(), calls=%async_computation.2 | async-start | bytes 3280896 | tf_op jit(solution)/shard_map/all_gather | solution.py:235
  542.1 26.7 %copy-start.51 = (bf16[1536,768]{1,0:T(8,128)(2,1)S(1)}, bf16[1536,768]{1,0:T(8,128)(2,1)}, u32[]{:S(2)}) copy-start(bf16[1536,768]{1,0:T(8,128)(2,1)} %param.43) | copy-start | bytes 7077892
  629.2 7.9 collective-permute-start.1
  648.5 2.4 copy-start.45
  655.8 168.1 %all-gather.14.cloned.1.call-start = ((), (), s32[]{:S(2)}) async-start(), calls=%async_computation.3 | async-start | bytes 3280896 | tf_op jit(solution)/shard_map/all_gather | solution.py:257
  768.1 11.9 copy-start.7
  768.1 5.0 collective-permute-start.2
  787.9 851.6 %all-reduce.14.cloned.1.call-start = ((), (), s32[]{:S(2)}) async-start(), calls=%async_computation.4 | async-start | bytes 28311552 | tf_op jit(solution)/shard_map/psum | solution.py:321
  788.2 9.2 copy-start.27
  826.0 2.2 copy-start.31
  833.2 3.5 copy-start.10
  833.2 3.5 copy-start.36
  833.2 3.5 copy-start.37
  833.2 3.5 copy-start.39
  833.2 3.5 copy-start.48
  833.2 3.5 copy-start.53
  833.2 3.5 copy-start.55
  833.3 3.5 copy-start.57
  839.3 15.4 copy-start.11
  854.7 6.7 copy-start.9
  994.6 12.4 copy-start.3
  994.6 12.6 copy-start.12
  994.6 13.0 copy-start.16
  1007.6 6.3 copy-start.2
  1009.6 4.3 copy-start.17
  1029.4 24.2 %copy-start.5 = (bf16[6,709,709]{2,0,1:T(8,128)(2,1)S(1)}, bf16[6,709,709]{2,0,1:T(8,128)(2,1)}, u32[]{:S(2)}) copy-start(bf16[6,709,709]{2,0,1:T(8,128)(2,1)} %copy.179) | copy-start | bytes 18096520 | tf_op jit(solution)/shard_map/while
  1029.4 24.2 %copy-start.8 = (s32[709,709]{1,0:T(8,128)S(1)}, s32[709,709]{1,0:T(8,128)}, u32[]{:S(2)}) copy-start(s32[709,709]{1,0:T(8,128)} %get-tuple-element.673) | copy-start | bytes 6032176 | tf_op jit(solution)/shard_map/while
  1090.8 15.4 copy-start.11
  1106.2 6.7 copy-start.9
  1246.1 12.4 copy-start.3
  1246.1 12.6 copy-start.12
  1246.2 13.0 copy-start.16
  1259.1 6.3 copy-start.2
  1261.1 4.3 copy-start.17
  1280.9 24.2 %copy-start.5 = (bf16[6,709,709]{2,0,1:T(8,128)(2,1)S(1)}, bf16[6,709,709]{2,0,1:T(8,128)(2,1)}, u32[]{:S(2)}) copy-start(bf16[6,709,709]{2,0,1:T(8,128)(2,1)} %copy.179) | copy-start | bytes 18096520 | tf_op jit(solution)/shard_map/while
  1280.9 24.2 %copy-start.8 = (s32[709,709]{1,0:T(8,128)S(1)}, s32[709,709]{1,0:T(8,128)}, u32[]{:S(2)}) copy-start(s32[709,709]{1,0:T(8,128)} %get-tuple-element.673) | copy-start | bytes 6032176 | tf_op jit(solution)/shard_map/while
  1347.6 6.9 copy-start.18
  1360.7 4.3 copy-start.26
  1420.9 2.8 copy-start.32
  1426.6 35.8 %copy-start.47 = (f32[1536]{0:T(1024)S(1)}, f32[1536]{0:T(1024)}, u32[]{:S(2)}) copy-start(f32[1536]{0:T(1024)} %get-tuple-element.459) | copy-start | bytes 18436
  1457.7 69.6 %copy-start.14 = (f32[709,768]{1,0:T(8,128)S(1)}, f32[709,768]{1,0:T(8,128)}, u32[]{:S(2)}) copy-start(f32[709,768]{1,0:T(8,128)} %copy-done.13) | copy-start | bytes 6534148
  1457.7 64.6 %collective-permute-start.3 = (bf16[3,768]{1,0:T(4,128)(2,1)S(1)}, bf16[3,768]{1,0:T(4,128)(2,1)S(1)}, u32[]{:S(2)}, u32[]{:S(2)}) collective-permute-start(bf16[3,768]{1,0:T(4,128)(2,1)S(1)} %slice.19), channel_id=1, source_target_pairs={{0,1},{2,3},{4,5},{6,7},{8,9},{10,11},{12,13},{14,15},{16,17},{18,... | collective-permute-start | bytes 13832
  1639.5 2.8 copy-start.30
  1639.5 4.2 copy-start.29
  1642.4 2.8 copy-start.28
  1645.1 6.5 slice-start
  1646.1 5.5 slice-start.1
  1651.7 3.4 copy-start.1
  (17 other events, 25.5 us)
Sparse Core Ops, SparseCore 0:
  9.6 36.8 all-gather.7
  502.9 35.6 all-gather.9
  655.9 34.1 all-gather.11
  788.0 35.8 all-gather.13
  1377.6 261.9 all-reduce.13
where the time goes:
time: 1680 us; the launch traced here: 1660 us
  matrix products  585 us (35%)
  local copies, waits for them, and re-layouts  361 us (21%)
  blocking collectives  306 us (18%)
  waiting for transfers between devices  222 us (13%)
  other arithmetic  134 us (8%)
  loops' own time  24.2 us (1%)
    dot_general x12, matrix products, item_scores(): jnp.einsum('ngo,sn->sgo', one_hot_of(bucket, bias_table.shape[1]), bias_t...  240 us
    unnamed x5, blocking collectives  199 us
    dot_general x12, local copies, waits for them, and re-layouts, item_scores(): jnp.einsum('ngo,sn->sgo', one_hot_of(bucket, bias_table.shape[1]), bias_t...  197 us
    dot_general x6, matrix products, attend_backward(): jnp.einsum('fkm,pkm->pf', one_hot_of(bucket, bias_table.shape[1]), grad_s...  118 us
    psum x1, waiting for transfers between devices, per_device(): lax.psum((grad_w_query, grad_b_query, grad_w_key, grad_w_value, grad_b_va...  108 us
    dot_general x4, matrix products, item_scores(): jnp.einsum('qhd,khd->hqk', query_item, key_item, preferred_element_type=j...  86.9 us
    unnamed x125, local copies, waits for them, and re-layouts  71.5 us
    add x8, other arithmetic, bucket_index(): counted = counted + (distance >= border).astype(jnp.int32)  67.7 us
  transfers between devices with their start and end apart: 9, of which 6 were waited for; matrix products, arithmetic and copies ran while one was open for 4% of the time, Pallas kernels for 0%

commit v1 on v0

v1 whole, which is shorter than its diff:
```python
from functools import partial
import math

import jax
import jax.numpy as jnp
from jax import lax
from jax.experimental import pallas as pl
from jax.experimental.pallas import tpu as pltpu
from jax.sharding import PartitionSpec as P

HEAD_DIM = 64
BUCKETS = 32
MAX_DIST = 128
BUCKETS_2D = 64
MAX_DIST_2D = 256
TEXT = 512
layer_eps = 1e-05

f32 = jnp.float32
bf = jnp.bfloat16
i16 = jnp.int16
PT = 256
NT = (((1,), (1,)), ((), ()))
VM = 56 << 20

def bucket_edges(buckets, farthest):
    exact=buckets//4
    r=list(range(1,exact+1))
    for k in range(1,exact):
        r.append(int(math.ceil(exact*(farthest/exact)**(k/exact)-1e-09)))
    return r
def lane_gather(table, index):
    dn=lax.GatherDimensionNumbers(offset_dims=(),collapsed_slice_dims=(1,),start_index_map=(1,),operand_batching_dims=(0,),start_indices_batching_dims=(0,))
    return lax.gather(table,index[...,None],dn,(1,1),mode=lax.GatherScatterMode.PROMISE_IN_BOUNDS)

def prep_kernel(len_ref, box_ref, boxt_ref, tseq_ref, idx_ref, toep_ref, *, buckets2, dist2, buckets1, dist1, seq):
    rows, lanes = idx_ref.shape[1:]
    edges=bucket_edges(buckets2,dist2)
    near=[e for e in edges if e<128]; far=[e for e in edges if e>=128]
    half=buckets2//2
    n=len_ref[0]
    rb=16
    lane=lax.broadcasted_iota(jnp.int32,(rb,128),1)
    tab=jnp.zeros((rb,128),jnp.int32)
    for e in near: tab=tab+jnp.where(lane>=e,1,0)
    def body(i,_):
        r0=pl.multiple_of(i*rb,rb)
        r=pl.ds(r0,rb)
        place=lax.broadcasted_iota(jnp.int32,(rb,128),0)+r0
        ok=((place<n)|(place>=TEXT))&(place<seq)
        for ax in range(2):
            col=jnp.broadcast_to(boxt_ref[ax,r,:],(rb,128))
            for c in range(lanes//128):
                cs=slice(c*128,(c+1)*128)
                d=col-box_ref[ax:ax+1,cs]
                a=jnp.abs(d)
                b=lane_gather(tab,jnp.minimum(a,127))
                for e in far: b=b+jnp.where(a>=e,1,0)
                b=b+jnp.where(d>0,half,0)
                if ax==1: b=jnp.where(ok,b,buckets2)
                idx_ref[ax,r,cs]=b.astype(i16)
        return 0
    lax.fori_loop(0,rows//rb,body,0)
    edges1=bucket_edges(buckets1,dist1)
    for j in range(5):
        d=lax.broadcasted_iota(jnp.int32,(128,128),0)-lax.broadcasted_iota(jnp.int32,(128,128),1)+128*(j-2)
        a=jnp.abs(d)
        b=jnp.zeros_like(d)
        for e in edges1: b=b+jnp.where(a>=e,1,0)
        b=(b+jnp.where(d>0,buckets1//2,0)).astype(i16)
        for h in range(tseq_ref.shape[0]):
            toep_ref[h,j*128:(j+1)*128,:]=lane_gather(jnp.broadcast_to(tseq_ref[h:h+1,:],(128,128)),b)

def prep(length, box, tseq, *, rows, lanes, seq, buckets2=BUCKETS_2D, dist2=MAX_DIST_2D, buckets1=BUCKETS, dist1=MAX_DIST):
    H=tseq.shape[0]
    boxp=jnp.pad(box,((0,0),(0,lanes-seq)))
    boxt=boxp[:,:rows,None]
    ts=jnp.pad(tseq,((0,0),(0,128-tseq.shape[1])))
    return pl.pallas_call(partial(prep_kernel,buckets2=buckets2,dist2=dist2,buckets1=buckets1,dist1=dist1,seq=seq),
        out_shape=(jax.ShapeDtypeStruct((2,rows,lanes),i16),jax.ShapeDtypeStruct((H,640,128),bf)),
        in_specs=[pl.BlockSpec(memory_space=pltpu.SMEM)]+[pl.BlockSpec(memory_space=pltpu.VMEM)]*3,
        out_specs=(pl.BlockSpec(memory_space=pltpu.VMEM),)*2,
        compiler_params=pltpu.CompilerParams(vmem_limit_bytes=VM),name="buckets",
    )(length,boxp,boxt,ts)

def keep_rows(x,first_row,limit):
    rr=lax.broadcasted_iota(jnp.int32,(x.shape[0],1),0)+first_row
    return jnp.where(rr<limit,x,jnp.zeros_like(x))

def fwd_kernel(q_ref,k_ref,v_ref,idx_ref,toep_ref,tx_ref,ty_ref,ctx_ref,p_ref,s_ref):
    H,rows,PT=p_ref.shape
    nch=PT//128
    tile=pl.program_id(0)
    lane=lax.broadcasted_iota(jnp.int32,(1,128),1)
    first=lane<HEAD_DIM
    for hp in range(H//2):
        hs=slice(hp*128,(hp+1)*128)
        q=keep_rows(q_ref[:,hs],tile*PT,rows)*jnp.asarray(HEAD_DIM**-0.5,bf)
        for h in range(2):
            qm=jnp.where(first if h==0 else ~first,q,jnp.zeros_like(q))
            s_ref[2*hp+h]=lax.dot_general(k_ref[:,hs],qm,NT,preferred_element_type=f32)
    tabs=[(jnp.broadcast_to(tx_ref[h:h+1,:],(16,128)),jnp.broadcast_to(ty_ref[h:h+1,:],(16,128))) for h in range(H)]
    cuts=[(h,c) for c in range(nch) for h in range(H)]
    def pass1(g,ms):
        r0=pl.multiple_of(g*16,16); r=pl.ds(r0,16)
        sb=r0//128; off=r0%128
        out=[]
        for c in range(nch):
            cs=slice(c*128,(c+1)*128)
            ix=idx_ref[0,r,cs]; iy=idx_ref[1,r,cs]
            tr=pl.ds(pl.multiple_of((jnp.clip(sb-(tile*nch+c),-2,2)+2)*128+off,16),16)
            for h in range(H):
                s=s_ref[h,r,cs]+lane_gather(tabs[h][0],ix).astype(f32)+lane_gather(tabs[h][1],iy).astype(f32)+toep_ref[h,tr,:].astype(f32)
                s_ref[h,r,cs]=s
                out.append(jnp.maximum(ms[c*H+h],jnp.maximum(s[:8],s[8:])))
        return tuple(out)
    ms=lax.fori_loop(0,rows//16,pass1,tuple(jnp.full((8,128),-jnp.inf,f32) for _ in cuts))
    ms=[jnp.max(m,axis=0,keepdims=True) for m in ms]
    def pass2(g,ls):
        r=pl.ds(pl.multiple_of(g*16,16),16)
        out=[]
        for i,(h,c) in enumerate(cuts):
            cs=slice(c*128,(c+1)*128)
            e=jnp.exp(s_ref[h,r,cs]-ms[i])
            s_ref[h,r,cs]=e
            out.append(ls[i]+(e[:8]+e[8:]))
        return tuple(out)
    ls=lax.fori_loop(0,rows//16,pass2,tuple(jnp.zeros((8,128),f32) for _ in cuts))
    inv=[1.0/jnp.sum(l,axis=0,keepdims=True) for l in ls]
    def pass3(g,_):
        r=pl.ds(pl.multiple_of(g*16,16),16)
        for i,(h,c) in enumerate(cuts):
            cs=slice(c*128,(c+1)*128)
            p_ref[h,r,cs]=(s_ref[h,r,cs]*inv[i]).astype(bf)
        return 0
    lax.fori_loop(0,rows//16,pass3,0)
    for hp in range(H//2):
        hs=slice(hp*128,(hp+1)*128)
        vt=v_ref[:,hs].T
        o=[jnp.dot(vt[h*64:(h+1)*64],p_ref[2*hp+h],preferred_element_type=f32) for h in range(2)]
        ctx_ref[:,hs]=jnp.concatenate(o,0).T.astype(bf)

def attn_fwd(qkv,idx,toep,tx,ty):
    rows=qkv.shape[0]; W=qkv.shape[1]//3; H=W//HEAD_DIM; lanes=idx.shape[2]
    tx=jnp.pad(tx,((0,0),(0,128-tx.shape[1])))
    ty=jnp.concatenate([ty,jnp.full((H,128-ty.shape[1]),-1e9,bf)],1)
    whole=lambda shape: pl.BlockSpec(shape,lambda i:(0,)*len(shape))
    return pl.pallas_call(fwd_kernel,
        grid=(lanes//PT,),
        in_specs=[pl.BlockSpec((PT,W),lambda i:(i,0)),pl.BlockSpec((rows,W),lambda i:(0,1)),pl.BlockSpec((rows,W),lambda i:(0,2)),
                  pl.BlockSpec((2,rows,PT),lambda i:(0,0,i)),whole(toep.shape),whole(tx.shape),whole(ty.shape)],
        out_specs=(pl.BlockSpec((PT,W),lambda i:(i,0)),pl.BlockSpec((H,rows,PT),lambda i:(0,0,i))),
        out_shape=(jax.ShapeDtypeStruct((rows,W),bf),jax.ShapeDtypeStruct((H,rows,lanes),bf)),
        scratch_shapes=[pltpu.VMEM((H,rows,PT),f32)],
        compiler_params=pltpu.CompilerParams(vmem_limit_bytes=VM),name="attn_fwd",
        cost_estimate=pl.CostEstimate(flops=H*rows*lanes*256,bytes_accessed=H*rows*lanes*2,transcendentals=H*rows*lanes),
    )(qkv,qkv,qkv,idx,toep,tx,ty)

def bwd_kernel(q_ref,k_ref,v_ref,do_ref,p_ref,dq_ref,dk_ref,dv_ref,gs_ref,dp_ref,dka,dva):
    H,rows,PT=p_ref.shape
    nch=PT//128
    tile=pl.program_id(0); last=pl.num_programs(0)-1
    lane=lax.broadcasted_iota(jnp.int32,(1,128),1)
    first=lane<HEAD_DIM
    scale=HEAD_DIM**-0.5
    cuts=[(h,c) for c in range(nch) for h in range(H)]
    split=lambda x: (jnp.where(first,x,jnp.zeros_like(x)),jnp.where(first,jnp.zeros_like(x),x))
    for hp in range(H//2):
        hs=slice(hp*128,(hp+1)*128)
        dm=split(keep_rows(do_ref[:,hs],tile*PT,rows))
        for h in range(2):
            dp_ref[2*hp+h]=lax.dot_general(v_ref[:,hs],dm[h],NT,preferred_element_type=f32)
    def pass1(g,ds):
        r=pl.ds(pl.multiple_of(g*16,16),16)
        out=[]
        for i,(h,c) in enumerate(cuts):
            cs=slice(c*128,(c+1)*128)
            t=p_ref[h,r,cs].astype(f32)*dp_ref[h,r,cs]
            out.append(ds[i]+(t[:8]+t[8:]))
        return tuple(out)
    ds=lax.fori_loop(0,rows//16,pass1,tuple(jnp.zeros((8,128),f32) for _ in cuts))
    ds=[jnp.sum(d,axis=0,keepdims=True) for d in ds]
    def pass2(g,_):
        r=pl.ds(pl.multiple_of(g*16,16),16)
        for i,(h,c) in enumerate(cuts):
            cs=slice(c*128,(c+1)*128)
            gs_ref[h,r,cs]=(p_ref[h,r,cs].astype(f32)*(dp_ref[h,r,cs]-ds[i])).astype(bf)
        return 0
    lax.fori_loop(0,rows//16,pass2,0)
    @pl.when(tile==0)
    def _():
        dka[...]=jnp.zeros_like(dka); dva[...]=jnp.zeros_like(dva)
    for hp in range(H//2):
        hs=slice(hp*128,(hp+1)*128)
        kt=k_ref[:,hs].T
        o=[jnp.dot(kt[h*64:(h+1)*64],gs_ref[2*hp+h],preferred_element_type=f32) for h in range(2)]
        dq_ref[:,hs]=(jnp.concatenate(o,0)*scale).T.astype(bf)
        qm=split(keep_rows(q_ref[:,hs],tile*PT,rows))
        dm=split(keep_rows(do_ref[:,hs],tile*PT,rows))
        dka[:,hs]+=jnp.dot(gs_ref[2*hp],qm[0],preferred_element_type=f32)+jnp.dot(gs_ref[2*hp+1],qm[1],preferred_element_type=f32)
        dva[:,hs]+=jnp.dot(p_ref[2*hp],dm[0],preferred_element_type=f32)+jnp.dot(p_ref[2*hp+1],dm[1],preferred_element_type=f32)
    @pl.when(tile==last)
    def _():
        dk_ref[...]=(dka[...]*scale).astype(bf)
        dv_ref[...]=dva[...].astype(bf)

def attn_bwd(qkv,do,p):
    rows=qkv.shape[0]; W=qkv.shape[1]//3; H=W//HEAD_DIM; lanes=p.shape[2]
    tilew=pl.BlockSpec((PT,W),lambda i:(i,0))
    whole=lambda k: pl.BlockSpec((rows,W),lambda i,k=k:(0,k))
    big=pl.BlockSpec((H,rows,PT),lambda i:(0,0,i))
    o=jax.ShapeDtypeStruct((rows,W),bf)
    return pl.pallas_call(bwd_kernel,
        grid=(lanes//PT,),
        in_specs=[tilew,whole(1),whole(2),tilew,big],
        out_specs=(tilew,whole(0),whole(0),big),
        out_shape=(o,o,o,jax.ShapeDtypeStruct((H,rows,lanes),bf)),
        scratch_shapes=[pltpu.VMEM((H,rows,PT),f32),pltpu.VMEM((rows,W),f32),pltpu.VMEM((rows,W),f32)],
        compiler_params=pltpu.CompilerParams(vmem_limit_bytes=VM),name="attn_bwd",
        cost_estimate=pl.CostEstimate(flops=H*rows*lanes*640,bytes_accessed=H*rows*lanes*4,transcendentals=0),
    )(qkv,qkv,qkv,do,p)

def hist_kernel(gs_ref, go_ref, idx_ref, out_ref, toep_ref, acc, accT, *, buckets2):
    H, rows, lanes = gs_ref.shape
    step = pl.program_id(0)
    SB = 16
    heads = 2 * H

    @pl.when(step == 0)
    def _():
        acc[...] = jnp.zeros_like(acc)
        accT[...] = jnp.zeros_like(accT)

    iota = lax.broadcasted_iota(jnp.int32, (buckets2, lanes), 0).astype(i16)
    one = jnp.ones((buckets2, lanes), bf)
    zero = jnp.zeros((buckets2, lanes), bf)

    def body(i, _):
        r = pl.ds(pl.multiple_of(i * SB, SB), SB)
        s0 = step * rows + i * SB
        sb = s0 // 128
        off = pl.multiple_of(s0 % 128, SB)
        both = [gs_ref[:, r, :], go_ref[:, r, :]]
        for k in range(2):
            for h in range(H):
                for c in range(lanes // 128):
                    at = pl.ds(pl.multiple_of((jnp.clip(sb - c, -2, 2) + 2) * 128 + off, SB), SB)
                    accT[k * H + h, at, :] += both[k][h, :, c * 128:(c + 1) * 128].astype(f32)
        G = jnp.concatenate(both, 0).reshape(heads * SB, lanes)
        O = []
        for ax in range(2):
            ix = idx_ref[ax, r, :]
            for p in range(SB):
                O.append(jnp.where(iota == ix[p:p + 1, :], one, zero))
        acc[...] += lax.dot_general(jnp.concatenate(O, 0), G, NT, preferred_element_type=f32)
        return 0

    lax.fori_loop(0, rows // SB, body, 0)

    @pl.when(step == pl.num_programs(0) - 1)
    def _():
        lane = lax.broadcasted_iota(jnp.int32, (buckets2, heads * SB), 1) % SB
        for ax in range(2):
            t = jnp.zeros((buckets2, heads * SB), f32)
            for p in range(SB):
                at = (ax * SB + p) * buckets2
                t = t + jnp.where(lane == p, acc[at:at + buckets2, :], 0.0)
            out_ref[ax] = t
        m = lax.broadcasted_iota(jnp.int32, (128, 128), 1)
        turned = m + lax.broadcasted_iota(jnp.int32, (128, 128), 0)
        wraps = turned >= 128
        turned = jnp.where(wraps, turned - 128, turned)
        for h in range(heads):
            for j in (-1, 0, 1):
                x = lane_gather(accT[h, (j + 2) * 128:(j + 3) * 128, :], turned)
                at = 2 * (j + 1)
                toep_ref[h, at:at + 1, :] = jnp.sum(jnp.where(wraps, 0.0, x), axis=0, keepdims=True)
                toep_ref[h, at + 1:at + 2, :] = jnp.sum(jnp.where(wraps, x, 0.0), axis=0, keepdims=True)
            toep_ref[h, 6:7, :] = jnp.sum(accT[h, 0:128, :], axis=0, keepdims=True)
            toep_ref[h, 7:8, :] = jnp.sum(accT[h, 512:640, :], axis=0, keepdims=True)


def hist(gs, go, idx, SB=240):
    H, rows, lanes = gs.shape
    big = pl.BlockSpec((H, SB, lanes), lambda i: (0, i, 0))
    out, toep = pl.pallas_call(
        partial(hist_kernel, buckets2=BUCKETS_2D),
        grid=(rows // SB,),
        in_specs=[big, big, pl.BlockSpec((2, SB, lanes), lambda i: (0, i, 0))],
        out_specs=(pl.BlockSpec((2, BUCKETS_2D, 2 * H * 16), lambda i: (0, 0, 0)), pl.BlockSpec((2 * H, 8, 128), lambda i: (0, 0, 0))),
        out_shape=(jax.ShapeDtypeStruct((2, BUCKETS_2D, 2 * H * 16), f32), jax.ShapeDtypeStruct((2 * H, 8, 128), f32)),
        scratch_shapes=[pltpu.VMEM((32 * BUCKETS_2D, 2 * H * 16), f32), pltpu.VMEM((2 * H, 640, 128), f32)],
        compiler_params=pltpu.CompilerParams(vmem_limit_bytes=VM),
        name="table_sums",
        cost_estimate=pl.CostEstimate(flops=rows * 128 * lanes * 2 * H * 32, bytes_accessed=4 * H * rows * lanes, transcendentals=0),
    )(gs, go, idx)
    xy = out.reshape(2, BUCKETS_2D, 2 * H, 16).sum(3).transpose(0, 2, 1)
    line = toep.reshape(2 * H, 1024)
    base = jnp.array([-128, 0, 0, 128, 128, 256, -MAX_DIST - 128, MAX_DIST + 256])
    d = (base[:, None] - jnp.arange(128)).reshape(1024)
    b = jnp.zeros_like(d)
    for e in bucket_edges(BUCKETS, MAX_DIST):
        b = b + (jnp.abs(d) >= e)
    b = b + (d > 0) * (BUCKETS // 2)
    seq = jnp.dot(line, (b[:, None] == jnp.arange(BUCKETS)).astype(f32), precision=lax.Precision.HIGHEST)
    return seq, xy[0], xy[1]


def swap(value, axis, bit):
    count = lax.axis_size(axis)
    return lax.ppermute(value, axis, [(i, i ^ bit) for i in range(count)])


def side(axis, bit):
    return (lax.axis_index(axis) // bit) % 2


def half_of(value, axis, which):
    size = value.shape[axis] // 2
    return lax.dynamic_slice_in_dim(value, which * size, size, axis)


def join(mine, theirs, which, axis):
    low = jnp.where(which == 0, mine, theirs)
    high = jnp.where(which == 0, theirs, mine)
    return jnp.concatenate([low, high], axis)


def fetch(own):
    core = side("dp", 1)
    got = swap(half_of(own, 0, core), "tensor", 1)
    return join(got, swap(got, "dp", 1), core, 0)


def dp_bits():
    count = lax.axis_size("dp")
    bits = []
    bit = 1
    while bit < count:
        bits.append(bit)
        bit *= 2
    return bits


def add_low(a, b):
    return (a.astype(f32) + b.astype(f32)).astype(bf)


def reduce_weight(own, other):
    bits = dp_bits()
    core = side("dp", 1)
    both = jnp.stack([own, other])
    got = swap(half_of(both, 1, 1 - core), "dp", 1)
    both = add_low(half_of(both, 1, core), got)
    total = add_low(both[0], swap(both[1], "tensor", 1))
    for bit in bits[1:]:
        at = side("dp", bit)
        got = swap(half_of(total, 0, 1 - at), "dp", bit)
        total = add_low(half_of(total, 0, at), got)
    for bit in bits[::-1]:
        total = join(total, swap(total, "dp", bit), side("dp", bit), 0)
    return total.astype(f32)


def reduce_small(own, other):
    total = own + swap(other, "tensor", 1)
    for bit in dp_bits():
        total = total + swap(total, "dp", bit)
    return total


def norm_parts(values):
    center = values - jnp.mean(values, axis=1, keepdims=True)
    inverse = lax.rsqrt(jnp.mean(center * center, axis=1, keepdims=True) + layer_eps)
    return center * inverse, inverse


def norm_back(grad_scaled, scaled, inverse):
    return inverse * (
        grad_scaled
        - jnp.mean(grad_scaled, axis=1, keepdims=True)
        - scaled * jnp.mean(grad_scaled * scaled, axis=1, keepdims=True)
    )


def gelu_parts(v):
    cdf = 0.5 * (1.0 + lax.erf(v * (0.5 ** 0.5)))
    pdf = jnp.exp(-0.5 * v * v) * (1.0 / math.sqrt(2.0 * math.pi))
    return v * cdf, cdf + v * pdf


def mm(a, b):
    return jnp.dot(a, b, preferred_element_type=f32)


def mm_nt(a, b):
    return lax.dot_general(a, b, (((1,), (1,)), ((), ())), preferred_element_type=f32)


def mm_tn(a, b):
    return lax.dot_general(a, b, (((0,), (0,)), ((), ())), preferred_element_type=f32)


def per_device(
    tokens, text_len, box_coords, w_query, b_query, w_key, w_value, b_value, w_out, b_out,
    table_seq, table_x, table_y, gain_attn, shift_attn, w_up, b_up, w_down, b_down,
    gain_ffn, shift_ffn, cotangent,
):
    seq, width = tokens.shape[1:]
    rows = -(-seq // 240) * 240
    lanes = -(-rows // PT) * PT
    local = w_query.shape[1]
    heads = local // HEAD_DIM
    hidden = w_up.shape[1]

    smalls = [b_query, b_value, b_up, table_seq.reshape(-1), table_x.reshape(-1), table_y.reshape(-1)]
    small_other = swap(jnp.concatenate(smalls), "tensor", 1)
    others = []
    at = 0
    for piece in smalls:
        others.append(small_other[at:at + piece.shape[0]])
        at += piece.shape[0]
    bq_o, bv_o, bu_o = others[:3]
    ts_o, tx_o, ty_o = others[3].reshape(heads, -1), others[4].reshape(heads, -1), others[5].reshape(heads, -1)

    w_qkv = jnp.concatenate([w_query, w_key, w_value], 1)
    w_qkv_o = fetch(w_qkv)
    w_out_o = fetch(w_out)
    w_up_o = fetch(w_up)
    w_down_o = fetch(w_down)

    x = jnp.pad(tokens[0], ((0, rows - seq), (0, 0)))
    g = jnp.pad(cotangent[0], ((0, rows - seq), (0, 0)))

    def bias_of(bq, bv):
        return jnp.concatenate([bq, jnp.zeros((local,), bf), bv]).astype(f32)

    idx, toep = prep(text_len, box_coords[0], jnp.concatenate([table_seq, ts_o], 0), rows=rows, lanes=lanes, seq=seq)
    qkv = (mm(x, w_qkv) + bias_of(b_query, b_value)).astype(bf)
    ctx, prob = attn_fwd(qkv, idx, toep[:heads], table_x, table_y)
    qkv_o = (mm(x, w_qkv_o) + bias_of(bq_o, bv_o)).astype(bf)
    ctx_o, prob_o = attn_fwd(qkv_o, idx, toep[heads:], tx_o, ty_o)

    attn = mm(ctx, w_out) + mm(ctx_o, w_out_o) + b_out.astype(f32)
    n1, inv1 = norm_parts(x.astype(f32) + attn)
    normed = n1 * gain_attn.astype(f32) + shift_attn.astype(f32)
    low = normed.astype(bf)
    act, slope = gelu_parts(mm(low, w_up) + b_up.astype(f32))
    act_o, slope_o = gelu_parts(mm(low, w_up_o) + bu_o.astype(f32))
    act, act_o = act.astype(bf), act_o.astype(bf)
    slope, slope_o = slope.astype(bf), slope_o.astype(bf)
    branch = mm(act, w_down) + mm(act_o, w_down_o) + b_down.astype(f32)
    n2, inv2 = norm_parts(normed + branch)
    output = (n2 * gain_ffn.astype(f32) + shift_ffn.astype(f32)).astype(bf)[:seq][None]

    gf = g.astype(f32)
    grad_gain_ffn = jnp.sum(gf * n2, axis=0)
    grad_shift_ffn = jnp.sum(gf, axis=0)
    grad_mid = norm_back(gf * gain_ffn.astype(f32), n2, inv2)
    gb = grad_mid.astype(bf)
    grad_b_down = jnp.sum(gb.astype(f32), axis=0)
    grad_w_down = reduce_weight(mm_tn(act, gb).astype(bf), mm_tn(act_o, gb).astype(bf))
    gh = (mm_nt(gb, w_down) * slope.astype(f32)).astype(bf)
    gh_o = (mm_nt(gb, w_down_o) * slope_o.astype(f32)).astype(bf)
    grad_b_up = jnp.sum(gh.astype(f32), axis=0)
    grad_b_up_o = jnp.sum(gh_o.astype(f32), axis=0)
    grad_w_up = reduce_weight(mm_tn(low, gh).astype(bf), mm_tn(low, gh_o).astype(bf))
    grad_normed = mm_nt(gh, w_up) + mm_nt(gh_o, w_up_o) + grad_mid
    grad_gain_attn = jnp.sum(grad_normed * n1, axis=0)
    grad_shift_attn = jnp.sum(grad_normed, axis=0)
    grad_first = norm_back(grad_normed * gain_attn.astype(f32), n1, inv1)
    ga = grad_first.astype(bf)
    grad_b_out = jnp.sum(ga.astype(f32), axis=0)
    grad_w_out = reduce_weight(mm_tn(ctx, ga).astype(bf), mm_tn(ctx_o, ga).astype(bf))
    gc = mm_nt(ga, w_out).astype(bf)
    gc_o = mm_nt(ga, w_out_o).astype(bf)
    dq, dk, dv, gs = attn_bwd(qkv, gc, prob)
    dq_o, dk_o, dv_o, gs_o = attn_bwd(qkv_o, gc_o, prob_o)
    dqkv = jnp.concatenate([dq, dk, dv], 1)
    dqkv_o = jnp.concatenate([dq_o, dk_o, dv_o], 1)
    grad_w_qkv = reduce_weight(mm_tn(x, dqkv).astype(bf), mm_tn(x, dqkv_o).astype(bf))
    grad_tokens = (grad_first + mm_nt(dqkv, w_qkv) + mm_nt(dqkv_o, w_qkv_o))[:seq][None]
    t_seq, t_x, t_y = hist(gs, gs_o, idx)

    sums = jnp.sum(dqkv.astype(f32), axis=0)
    sums_o = jnp.sum(dqkv_o.astype(f32), axis=0)
    shared = [grad_b_out, grad_gain_attn, grad_shift_attn, grad_b_down, grad_gain_ffn, grad_shift_ffn]

    def packed(bias_sums, up, at):
        tables = [t[at:at + heads].reshape(-1) for t in (t_seq, t_x, t_y)]
        return jnp.concatenate([bias_sums[:local], bias_sums[2 * local:], up] + tables + shared)

    small = reduce_small(packed(sums, grad_b_up, 0), packed(sums_o, grad_b_up_o, heads))
    shapes = [(local,), (local,), (hidden,), table_seq.shape, table_x.shape, table_y.shape] + [(width,)] * 6
    pieces = []
    at = 0
    for shape in shapes:
        size = math.prod(shape)
        pieces.append(small[at:at + size].reshape(shape))
        at += size
    g_bq, g_bv, g_bu, g_ts, g_tx, g_ty, g_bo, g_ga, g_sa, g_bd, g_gf, g_sf = pieces
    return (
        output, grad_tokens,
        grad_w_qkv[:, :local], g_bq, grad_w_qkv[:, local:2 * local], grad_w_qkv[:, 2 * local:], g_bv,
        grad_w_out, g_bo, g_ts, g_tx, g_ty, g_ga, g_sa, grad_w_up, g_bu, grad_w_down, g_bd, g_gf, g_sf,
    )


def solution(mesh):
    item = P(("dp", "tensor"), None, None)
    column, row, split, copied = P(None, "tensor"), P("tensor", None), P("tensor"), P()
    return jax.shard_map(
        per_device,
        mesh=mesh,
        in_specs=(
            item, P(("dp", "tensor")), item, column, split, column, column, split, row, copied,
            row, row, row, copied, copied, column, split, row, copied, copied, copied, item,
        ),
        out_specs=(
            item, item, column, split, column, column, split, row, copied, row, row, row,
            copied, copied, column, split, row, copied, copied, copied,
        ),
        check_vma=False,
    )
```

time: 1680 us -> 530 us (0.32)
  matrix products: 585 us -> 65.7 us
  blocking collectives: 306 us -> 0 us
  local copies, waits for them, and re-layouts: 361 us -> 62.6 us
  Pallas kernels: 0 us -> 157 us
  waiting for transfers between devices: 222 us -> 134 us
  other arithmetic: 134 us -> 56.6 us
  starting transfers between devices: 14.7 us -> 45.8 us
  loops' own time: 24.2 us -> 0 us
    dot_general x50 -> x25, matrix products: 585 us -> 65.7 us  [the longest x8 24.9 us: mm_nt(): lax.dot_general(a, b, (((1,), (1,)), ((), ())), preferred_element_type=f32)]
    unnamed x5 -> x0, blocking collectives: 199 us -> none
    dot_general x12 -> x0, local copies, waits for them, and re-layouts: 197 us -> none  [item_scores(): jnp.einsum('ngo,sn->sgo', one_hot_of(bucket, bias_table.shape[1]), bias_t...]
    pallas_call x0 -> x6, Pallas kernels: none -> 157 us  [the longest x2 57.4 us: attn_fwd(): pl.pallas_call(fwd_kernel, grid=(lanes // PT,), in_specs=[pl.BlockSpec((P...]
    ppermute x0 -> x50, waiting for transfers between devices: none -> 134 us  [swap(): return lax.ppermute(value, axis, [(i, i ^ bit) for i in range(count)])]
    all_gather x4 -> x0, waiting for transfers between devices: 111 us -> none  [the longest x1 34.5 us: per_device(): lax.all_gather(normed.astype(jnp.bfloat16), 'tensor', axis=0, tiled=True)]
    psum x1 -> x0, waiting for transfers between devices: 108 us -> none  [per_device(): lax.psum((grad_w_query, grad_b_query, grad_w_key, grad_w_value, grad_b_va...]
    psum x2 -> x0, blocking collectives: 102 us -> none  [the longest x1 59.9 us: per_device(): lax.psum((grad_w_query, grad_b_query, grad_w_key, grad_w_value, grad_b_va...]
  transfers between devices with their start and end apart: 9 -> 50, of which waited for: 6 -> 25; matrix products, arithmetic and copies ran while one was open for 4% -> 23% of each run, Pallas kernels for 0% -> 23%
where the time goes in v1:
time: 530 us; the launch traced here: 525 us
  Pallas kernels  157 us (30%)
  waiting for transfers between devices  134 us (25%)
  matrix products  65.7 us (12%)
  local copies, waits for them, and re-layouts  62.6 us (12%)
  other arithmetic  56.6 us (11%)
  starting transfers between devices  45.8 us (9%)
    ppermute x50, waiting for transfers between devices, swap(): return lax.ppermute(value, axis, [(i, i ^ bit) for i in range(count)])  134 us
    pallas_call x2, Pallas kernels, attn_fwd(): pl.pallas_call(fwd_kernel, grid=(lanes // PT,), in_specs=[pl.BlockSpec((P...  57.4 us
    pallas_call x1, Pallas kernels, hist(): pl.pallas_call(partial(hist_kernel, buckets2=BUCKETS_2D), grid=(rows // S...  52.2 us
    ppermute x50, starting transfers between devices, swap(): return lax.ppermute(value, axis, [(i, i ^ bit) for i in range(count)])  45.8 us
    pallas_call x2, Pallas kernels, attn_bwd(): pl.pallas_call(bwd_kernel, grid=(lanes // PT,), in_specs=[tilew, whole(1)...  34.2 us
    dot_general x8, matrix products, mm_nt(): lax.dot_general(a, b, (((1,), (1,)), ((), ())), preferred_element_type=f32)  24.9 us
    dot_general x8, matrix products, mm(): return jnp.dot(a, b, preferred_element_type=f32)  21.2 us
    dot_general x8, matrix products, mm_tn(): lax.dot_general(a, b, (((0,), (0,)), ((), ())), preferred_element_type=f32)  19.2 us
  transfers between devices with their start and end apart: 50, of which 25 were waited for; matrix products, arithmetic and copies ran while one was open for 23% of the time, Pallas kernels for 23%

profile of v1, /device:TPU:0, one launch (start us, length us, event | category | flops | bytes accessed | tf_op | source)
XLA Modules:
  0.0 525.1 jit_solution(13553882895832935631)
XLA Ops:
  3.1 2.8 concatenate.106
  5.9 2.9 collective-permute-start
  8.8 2.0 constant_dynamic-update-slice_fusion.2
  10.9 2.0 constant_dynamic-update-slice_fusion.1
  13.8 2.1 constant_dynamic-slice_fusion.15
  16.0 2.1 collective-permute-start.3
  19.2 2.4 constant_dynamic-slice_fusion.12
  21.6 2.0 collective-permute-start.7
  41.0 4.6 fusion.10.q_ref.k_ref.v_ref
  46.3 13.5 %buckets.1 = (s16[2,720,768]{2,1,0:T(8,128)(2,1)}, bf16[12,640,128]{2,1,0:T(8,128)(2,1)}) custom-call(s32[1]{0:T(128)S(6)} %copy.54.len_ref, s32[2,768]{1,0:T(2,128)} %pad.25.box_ref, s32[2,720,1]{2,1,0:T(8,128)} %copy.44.boxt_ref, bf16[12,128]{1,0:T(8,128)(2,1)} %fusion.58.tseq_ref), custom_call_target="tpu_custom_call" | custom-call | tf_op jit(solution)/shard_map/buckets/pallas_call | solution.py:79
  59.8 2.9 fusion.91
  67.9 28.7 %attn_fwd.2 = (bf16[720,384]{1,0:T(8,128)(2,1)}, bf16[6,720,768]{2,1,0:T(8,128)(2,1)}) custom-call(bf16[720,1152]{1,0:T(8,128)(2,1)} %fusion.10.q_ref.k_ref.v_ref, bf16[720,1152]{1,0:T(8,128)(2,1)} %fusion.10.q_ref.k_ref.v_ref, bf16[720,1152]{1,0:T(8,128)(2,1)} %fusion.10.q_ref.k_ref.v_ref, s16[2,720,768]{2,1,0:T(8,128)(2,1)} %get-tuple-element.36.idx_ref, ...), custom_call_target="tpu_custom_call" | custom-call | flops 849346560 | bytes 6635520 | tf_op jit(solution)/shard_map/attn_fwd/pallas_call | solution.py:148
  102.9 2.8 fusion.11.q_ref.k_ref.v_ref
  105.7 28.7 %attn_fwd.3 = (bf16[720,384]{1,0:T(8,128)(2,1)}, bf16[6,720,768]{2,1,0:T(8,128)(2,1)}) custom-call(bf16[720,1152]{1,0:T(8,128)(2,1)} %fusion.11.q_ref.k_ref.v_ref, bf16[720,1152]{1,0:T(8,128)(2,1)} %fusion.11.q_ref.k_ref.v_ref, bf16[720,1152]{1,0:T(8,128)(2,1)} %fusion.11.q_ref.k_ref.v_ref, s16[2,720,768]{2,1,0:T(8,128)(2,1)} %get-tuple-element.36.idx_ref, ...), custom_call_target="tpu_custom_call" | custom-call | flops 849346560 | bytes 6635520 | tf_op jit(solution)/shard_map/attn_fwd/pallas_call | solution.py:148
  134.5 2.3 fusion.99
  137.9 2.3 multiply_convert_fusion.3
  143.6 3.1 multiply_convert_fusion.2
  146.8 2.2 broadcast_select_fusion.3
  149.0 2.4 fusion.100
  155.6 4.3 convert_reduce_fusion.1
  159.8 1.9 fusion.103
  161.8 6.0 %convert_reduce_fusion = (f32[1536]{0:T(1024)}, bf16[720,1536]{1,0:T(8,128)(2,1)S(1)}) fusion(f32[720,1536]{1,0:T(8,128)S(1)} %get-tuple-element.182, f32[1536]{0:T(1024)S(1)} %slice_convert_fusion, bf16[720,768]{1,0:T(8,128)(2,1)S(1)} %get-tuple-element.101, bf16[768,768]{1,0:T(8,128)(2,1)S(1)} %get-tuple-element.114, ...), kind=kOutput, calls=%fused_computation.22 | convolution fusion | flops 1719998976 | bytes 10113024 | tf_op jit(solution)/shard_map/dot_general | solution.py:397
  167.8 3.5 multiply_reduce_fusion
  171.3 2.5 convert_reduce_fusion.6
  176.9 16.9 %attn_bwd.2 = (bf16[720,384]{1,0:T(8,128)(2,1)}, bf16[720,384]{1,0:T(8,128)(2,1)}, bf16[720,384]{1,0:T(8,128)(2,1)}, bf16[6,720,768]{2,1,0:T(8,128)(2,1)}) custom-call(bf16[720,1152]{1,0:T(8,128)(2,1)} %fusion.10.q_ref.k_ref.v_ref, bf16[720,1152]{1,0:T(8,128)(2,1)} %fusion.10.q_ref.k_ref.v_ref, bf16[720,1152]{1,0:T(8,128)(2,1)} %fusion.10.q_ref.k_ref.v_ref, ...), custom_call_target="tpu_custom_call" | custom-call | flops 2123366400 | bytes 13271040 | tf_op jit(solution)/shard_map/attn_bwd/pallas_call | solution.py:213
  197.4 3.0 fusion.104
  202.1 17.3 %attn_bwd.3 = (bf16[720,384]{1,0:T(8,128)(2,1)}, bf16[720,384]{1,0:T(8,128)(2,1)}, bf16[720,384]{1,0:T(8,128)(2,1)}, bf16[6,720,768]{2,1,0:T(8,128)(2,1)}) custom-call(bf16[720,1152]{1,0:T(8,128)(2,1)} %fusion.11.q_ref.k_ref.v_ref, bf16[720,1152]{1,0:T(8,128)(2,1)} %fusion.11.q_ref.k_ref.v_ref, bf16[720,1152]{1,0:T(8,128)(2,1)} %fusion.11.q_ref.k_ref.v_ref, ...), custom_call_target="tpu_custom_call" | custom-call | flops 2123366400 | bytes 13271040 | tf_op jit(solution)/shard_map/attn_bwd/pallas_call | solution.py:213
  226.5 3.4 fusion.17
  230.0 3.4 fusion.18
  233.4 2.1 fusion.19
  237.1 52.2 %table_sums.1 = (f32[2,64,192]{2,1,0:T(8,128)}, f32[12,8,128]{2,1,0:T(8,128)}) custom-call(bf16[6,720,768]{2,1,0:T(8,128)(2,1)} %get-tuple-element.48.gs_ref, bf16[6,720,768]{2,1,0:T(8,128)(2,1)} %get-tuple-element.49.go_ref, s16[2,720,768]{2,1,0:T(8,128)(2,1)} %get-tuple-element.36.idx_ref), custom_call_target="tpu_custom_call" | custom-call | flops 27179089920 | bytes 13271040 | tf_op jit(solution)/shard_map/table_sums/pallas_call | solution.py:286
  300.7 5.5 %fusion.20 = bf16[1,1536,768]{2,1,0:T(8,128)(2,1)} fusion(bf16[720,1536]{1,0:T(8,128)(2,1)} %copy-done.68, bf16[720,768]{1,0:T(8,128)(2,1)} %copy-done.25), kind=kOutput, calls=%fused_computation.58 | convolution fusion | flops 1699872768 | bytes 5677056 | tf_op jit(solution)/shard_map/dot_general | solution.py:401
  307.6 2.1 collective-permute-start.24
  309.7 3.0 fusion.41
  312.8 3.9 collective-permute-done.24
  318.9 3.1 collective-permute-done.25
  326.5 2.9 collective-permute-start.27
  329.4 3.5 fusion.31
  342.7 3.6 copy.46
  353.3 1.9 add_convert_fusion.2
  365.8 11.9 %collective-permute-done.10 = bf16[384,1152]{1,0:T(8,128)(2,1)} collective-permute-done((bf16[384,1152]{1,0:T(8,128)(2,1)S(1)}, bf16[384,1152]{1,0:T(8,128)(2,1)}, u32[]{:S(2)}, u32[]{:S(2)}) %collective-permute-start.10) | collective-permute-done | bytes 884768 | tf_op jit(solution)/shard_map/ppermute | solution.py:311
  380.2 2.3 add_convert_fusion.1
  382.5 7.3 %collective-permute-done.11 = bf16[192,1152]{1,0:T(8,128)(2,1)S(1)} collective-permute-done((bf16[192,1152]{1,0:T(8,128)(2,1)S(1)}, bf16[192,1152]{1,0:T(8,128)(2,1)S(1)}, u32[]{:S(2)}, u32[]{:S(2)}) %collective-permute-start.11) | collective-permute-done | bytes 442400 | tf_op jit(solution)/shard_map/ppermute | solution.py:311
  392.3 3.7 collective-permute-done.12
  396.0 3.4 collective-permute-start.13
  399.5 2.5 add_convert_fusion
  402.0 3.3 collective-permute-done.13
  407.1 4.4 collective-permute-done.14
  411.7 8.0 %collective-permute-done.33 = bf16[384,1536]{1,0:T(8,128)(2,1)S(1)} collective-permute-done((bf16[384,1536]{1,0:T(8,128)(2,1)S(1)}, bf16[384,1536]{1,0:T(8,128)(2,1)S(1)}, u32[]{:S(2)}, u32[]{:S(2)}) %collective-permute-start.33) | collective-permute-done | bytes 1179680 | tf_op jit(solution)/shard_map/ppermute | solution.py:311
  420.6 20.6 %collective-permute-done.42 = bf16[768,768]{1,0:T(8,128)(2,1)S(1)} collective-permute-done((bf16[768,768]{1,0:T(8,128)(2,1)S(1)}, bf16[768,768]{1,0:T(8,128)(2,1)S(1)}, u32[]{:S(2)}, u32[]{:S(2)}) %collective-permute-start.42) | collective-permute-done | bytes 1179680 | tf_op jit(solution)/shard_map/ppermute | solution.py:311
  445.5 12.4 %collective-permute-done.43 = bf16[384,768]{1,0:T(8,128)(2,1)S(1)} collective-permute-done((bf16[384,768]{1,0:T(8,128)(2,1)S(1)}, bf16[384,768]{1,0:T(8,128)(2,1)S(1)}, u32[]{:S(2)}, u32[]{:S(2)}) %collective-permute-start.43) | collective-permute-done | bytes 589856 | tf_op jit(solution)/shard_map/ppermute | solution.py:311
  459.5 3.2 collective-permute-done.16
  463.0 2.1 collective-permute-start.36
  465.1 3.2 collective-permute-done.44
  469.9 7.8 %collective-permute-done.36 = bf16[48,1536]{1,0:T(8,128)(2,1)S(1)} collective-permute-done((bf16[48,1536]{1,0:T(8,128)(2,1)S(1)}, bf16[48,1536]{1,0:T(8,128)(2,1)S(1)}, u32[]{:S(2)}, u32[]{:S(2)}) %collective-permute-start.36) | collective-permute-done | bytes 147488 | tf_op jit(solution)/shard_map/ppermute | solution.py:311
  477.8 3.0 collective-permute-done.45
  480.9 4.4 collective-permute-done.37
  485.8 2.4 collective-permute-done.46
  489.6 4.0 collective-permute-done.38
  494.0 2.8 collective-permute-done.47
  497.0 12.8 %collective-permute-done.39 = bf16[192,1536]{1,0:T(8,128)(2,1)S(1)} collective-permute-done((bf16[192,1536]{1,0:T(8,128)(2,1)S(1)}, bf16[192,1536]{1,0:T(8,128)(2,1)S(1)}, u32[]{:S(2)}, u32[]{:S(2)}) %collective-permute-start.39) | collective-permute-done | bytes 589856 | tf_op jit(solution)/shard_map/ppermute | solution.py:311
  510.8 5.6 %collective-permute-done.48 = bf16[384,768]{1,0:T(8,128)(2,1)S(1)} collective-permute-done((bf16[384,768]{1,0:T(8,128)(2,1)S(1)}, bf16[384,768]{1,0:T(8,128)(2,1)S(1)}, u32[]{:S(2)}, u32[]{:S(2)}) %collective-permute-start.48) | collective-permute-done | bytes 589856 | tf_op jit(solution)/shard_map/ppermute | solution.py:311
  519.0 2.8 maximum_convert_fusion
  522.3 2.5 maximum_convert_fusion.1
  (374 shorter events, 127.9 us)
Async XLA Ops:
  0.7 17.5 %copy-start = (bf16[768,1536]{1,0:T(8,128)(2,1)S(1)}, bf16[768,1536]{1,0:T(8,128)(2,1)}, u32[]{:S(2)}) copy-start(bf16[768,1536]{1,0:T(8,128)(2,1)} %param.38) | copy-start | bytes 7077892
  0.7 12.2 %copy-start.36 = (bf16[768,384]{1,0:T(8,128)(2,1)S(1)}, bf16[768,384]{1,0:T(8,128)(2,1)}, u32[]{:S(2)}) copy-start(bf16[768,384]{1,0:T(8,128)(2,1)} %param.29) | copy-start | bytes 1769476
  5.9 29.9 %collective-permute-start = (bf16[3264]{0:T(1024)(128)(2,1)}, bf16[3264]{0:T(1024)(128)(2,1)}, u32[]{:S(2)}, u32[]{:S(2)}) collective-permute-start(bf16[3264]{0:T(1024)(128)(2,1)} %concatenate.106), channel_id=1, source_target_pairs={{0,1},{1,0},{2,3},{3,2},{4,5},{5,4},{6,7},{7,6},{8,9},{9,8},{10,11... | collective-permute-start | bytes 19592 | tf_op jit(solution)/shard_map/ppermute | solution.py:311
  16.0 43.8 %collective-permute-start.1 = (bf16[384,1152]{1,0:T(8,128)(2,1)}, bf16[384,1152]{1,0:T(8,128)(2,1)}, u32[]{:S(2)}, u32[]{:S(2)}) collective-permute-start(bf16[384,1152]{1,0:T(8,128)(2,1)} %constant_dynamic-slice_fusion.15), channel_id=1, source_target_pairs={{0,1},{1,0},{2,3},{3,2},{4,5},{5,4},{6,7},{7,6},{8,9},{9,8},{10,11... | collective-permute-start | bytes 2654216 | tf_op jit(solution)/shard_map/ppermute | solution.py:311
  16.0 81.2 %collective-permute-start.3 = (bf16[192,768]{1,0:T(8,128)(2,1)S(1)}, bf16[192,768]{1,0:T(8,128)(2,1)S(1)}, u32[]{:S(2)}, u32[]{:S(2)}) collective-permute-start(bf16[192,768]{1,0:T(8,128)(2,1)S(1)} %constant_dynamic-slice_fusion.14), channel_id=1, source_target_pairs={{0,1},{1,0},{2,3},{3,2},{4,5},{5,4},{6,7},{7,6},{8,9},{9,8},{10,11... | collective-permute-start | bytes 884744 | tf_op jit(solution)/shard_map/ppermute | solution.py:311
  19.2 81.5 %collective-permute-start.5 = (bf16[384,1536]{1,0:T(8,128)(2,1)}, bf16[384,1536]{1,0:T(8,128)(2,1)}, u32[]{:S(2)}, u32[]{:S(2)}) collective-permute-start(bf16[384,1536]{1,0:T(8,128)(2,1)} %constant_dynamic-slice_fusion.13), channel_id=1, source_target_pairs={{0,1},{1,0},{2,3},{3,2},{4,5},{5,4},{6,7},{7,6},{8,9},{9,8},{10,11... | collective-permute-start | bytes 3538952 | tf_op jit(solution)/shard_map/ppermute | solution.py:311
  21.6 79.3 %collective-permute-start.7 = (bf16[768,768]{1,0:T(8,128)(2,1)}, bf16[768,768]{1,0:T(8,128)(2,1)}, u32[]{:S(2)}, u32[]{:S(2)}) collective-permute-start(bf16[768,768]{1,0:T(8,128)(2,1)} %constant_dynamic-slice_fusion.12), channel_id=1, source_target_pairs={{0,1},{1,0},{2,3},{3,2},{4,5},{5,4},{6,7},{7,6},{8,9},{9,8},{10,11... | collective-permute-start | bytes 3538952 | tf_op jit(solution)/shard_map/ppermute | solution.py:311
  26.9 140.9 %copy-start.42 = (f32[768]{0:T(1024)}, f32[768]{0:T(1024)S(1)}, u32[]{:S(2)}) copy-start(f32[768]{0:T(1024)S(1)} %convert_element_type.514) | copy-start | bytes 9220
  59.8 41.5 %collective-permute-start.2 = (bf16[384,1152]{1,0:T(8,128)(2,1)}, bf16[384,1152]{1,0:T(8,128)(2,1)}, u32[]{:S(2)}, u32[]{:S(2)}) collective-permute-start(bf16[384,1152]{1,0:T(8,128)(2,1)} %collective-permute-done.1), channel_id=1, source_target_pairs={{0,2},{2,0},{4,6},{6,4},{8,10},{10,8},{12,14},{14,12},{16,18},{18,... | collective-permute-start | bytes 2654216 | tf_op jit(solution)/shard_map/ppermute | solution.py:311
  97.3 2.3 collective-permute-start.4
  100.7 41.5 %collective-permute-start.6 = (bf16[384,1536]{1,0:T(8,128)(2,1)}, bf16[384,1536]{1,0:T(8,128)(2,1)S(1)}, u32[]{:S(2)}, u32[]{:S(2)}) collective-permute-start(bf16[384,1536]{1,0:T(8,128)(2,1)} %collective-permute-done.5), channel_id=1, source_target_pairs={{0,2},{2,0},{4,6},{6,4},{8,10},{10,8},{12,14},{14,12},{16,18},{18,... | collective-permute-start | bytes 3538952 | tf_op jit(solution)/shard_map/ppermute | solution.py:311
  100.9 45.9 %collective-permute-start.8 = (bf16[768,768]{1,0:T(8,128)(2,1)}, bf16[768,768]{1,0:T(8,128)(2,1)S(1)}, u32[]{:S(2)}, u32[]{:S(2)}) collective-permute-start(bf16[768,768]{1,0:T(8,128)(2,1)} %collective-permute-done.7), channel_id=1, source_target_pairs={{0,2},{2,0},{4,6},{6,4},{8,10},{10,8},{12,14},{14,12},{16,18},{18,... | collective-permute-start | bytes 3538952 | tf_op jit(solution)/shard_map/ppermute | solution.py:311
  154.2 13.6 %copy-start.2 = (f32[720,768]{1,0:T(8,128)}, f32[720,768]{1,0:T(8,128)S(1)}, u32[]{:S(2)}) copy-start(f32[720,768]{1,0:T(8,128)S(1)} %get-tuple-element.105) | copy-start | bytes 6635524
  202.1 33.4 %copy-start.10 = (bf16[1,768,1152]{2,1,0:T(8,128)(2,1)}, bf16[1,768,1152]{2,1,0:T(8,128)(2,1)S(1)}, u32[]{:S(2)}) copy-start(bf16[1,768,1152]{2,1,0:T(8,128)(2,1)S(1)} %fusion.15) | copy-start | bytes 5308420
  223.6 11.9 %copy-start.12 = (bf16[1,768,1152]{2,1,0:T(8,128)(2,1)}, bf16[1,768,1152]{2,1,0:T(8,128)(2,1)S(1)}, u32[]{:S(2)}) copy-start(bf16[1,768,1152]{2,1,0:T(8,128)(2,1)S(1)} %fusion.16) | copy-start | bytes 5308420
  237.0 116.3 %collective-permute-start.9 = (bf16[2,384,1152]{2,1,0:T(8,128)(2,1)}, bf16[2,384,1152]{2,1,0:T(8,128)(2,1)}, u32[]{:S(2)}, u32[]{:S(2)}) collective-permute-start(bf16[2,384,1152]{2,1,0:T(8,128)(2,1)} %fusion.35), channel_id=1, source_target_pairs={{0,2},{2,0},{4,6},{6,4},{8,10},{10,8},{12,14},{14,12},{16,18},{18,... | collective-permute-start | bytes 5308424 | tf_op jit(solution)/shard_map/ppermute | solution.py:311
  237.1 53.0 %copy-start.60 = (s32[1024]{0:T(1024)S(1)}, s32[1024]{0:T(1024)}, u32[]{:S(2)}) copy-start(s32[1024]{0:T(1024)} %bitcast_add_fusion) | copy-start | bytes 12292
  295.2 11.0 %collective-permute-start.23 = (bf16[2,192,768]{2,1,0:T(8,128)(2,1)}, bf16[2,192,768]{2,1,0:T(8,128)(2,1)}, u32[]{:S(2)}, u32[]{:S(2)}) collective-permute-start(bf16[2,192,768]{2,1,0:T(8,128)(2,1)} %fusion.47), channel_id=1, source_target_pairs={{0,2},{2,0},{4,6},{6,4},{8,10},{10,8},{12,14},{14,12},{16,18},{18,... | collective-permute-start | bytes 1769480 | tf_op jit(solution)/shard_map/ppermute | solution.py:311
  300.7 23.6 %collective-permute-start.18 = (f32[7872]{0:T(1024)}, f32[7872]{0:T(1024)}, u32[]{:S(2)}, u32[]{:S(2)}) collective-permute-start(f32[7872]{0:T(1024)} %concatenate.122), channel_id=1, source_target_pairs={{0,1},{1,0},{2,3},{3,2},{4,5},{5,4},{6,7},{7,6},{8,9},{9,8},{10,11... | collective-permute-start | bytes 94472 | tf_op jit(solution)/shard_map/ppermute | solution.py:311
  307.6 9.1 %collective-permute-start.24 = (bf16[192,768]{1,0:T(8,128)(2,1)S(1)}, bf16[192,768]{1,0:T(8,128)(2,1)S(1)}, u32[]{:S(2)}, u32[]{:S(2)}) collective-permute-start(bf16[192,768]{1,0:T(8,128)(2,1)S(1)} %slice_bitcast_fusion.6), channel_id=1, source_target_pairs={{0,1},{1,0},{2,3},{3,2},{4,5},{5,4},{6,7},{7,6},{8,9},{9,8},{10,11... | collective-permute-start | bytes 884744 | tf_op jit(solution)/shard_map/ppermute | solution.py:311
  312.7 11.5 %copy-start.44 = (f32[768]{0:T(1024)S(1)}, f32[768]{0:T(1024)}, u32[]{:S(2)}) copy-start(f32[768]{0:T(1024)} %get-tuple-element.102) | copy-start | bytes 9220
  312.8 11.5 %copy-start.45 = (f32[768]{0:T(1024)S(1)}, f32[768]{0:T(1024)}, u32[]{:S(2)}) copy-start(f32[768]{0:T(1024)} %get-tuple-element.94) | copy-start | bytes 9220
  316.8 5.2 collective-permute-start.25
  322.1 4.4 collective-permute-start.26
  325.1 7.8 %collective-permute-start.19 = (f32[7872]{0:T(1024)S(1)}, f32[7872]{0:T(1024)S(1)}, u32[]{:S(2)}, u32[]{:S(2)}) collective-permute-start(f32[7872]{0:T(1024)S(1)} %add.509), channel_id=1, source_target_pairs={{0,2},{2,0},{4,6},{6,4},{8,10},{10,8},{12,14},{14,12},{16,18},{18,... | collective-permute-start | bytes 94472 | tf_op jit(solution)/shard_map/ppermute | solution.py:311
  326.5 8.0 %collective-permute-start.27 = (bf16[24,768]{1,0:T(8,128)(2,1)S(1)}, bf16[24,768]{1,0:T(8,128)(2,1)S(1)}, u32[]{:S(2)}, u32[]{:S(2)}) collective-permute-start(bf16[24,768]{1,0:T(8,128)(2,1)S(1)} %constant_dynamic-slice_fusion.6), channel_id=1, source_target_pairs={{0,16},{2,18},{4,20},{6,22},{8,24},{10,26},{12,28},{14,30},{16,0},... | collective-permute-start | bytes 110600 | tf_op jit(solution)/shard_map/ppermute | solution.py:311
  329.4 11.7 %copy-start.6 = (bf16[1,768,1536]{2,1,0:T(8,128)(2,1)S(1)}, bf16[1,768,1536]{2,1,0:T(8,128)(2,1)}, u32[]{:S(2)}) copy-start(bf16[1,768,1536]{2,1,0:T(8,128)(2,1)} %fusion.18) | copy-start | bytes 7077892
  333.0 4.0 collective-permute-start.20
  334.6 4.9 collective-permute-start.28
  337.0 9.3 %collective-permute-start.21 = (f32[7872]{0:T(1024)S(1)}, f32[7872]{0:T(1024)S(1)}, u32[]{:S(2)}, u32[]{:S(2)}) collective-permute-start(f32[7872]{0:T(1024)S(1)} %add.511), channel_id=1, source_target_pairs={{0,8},{2,10},{4,12},{6,14},{8,0},{10,2},{12,4},{14,6},{16,24},{18,... | collective-permute-start | bytes 94472 | tf_op jit(solution)/shard_map/ppermute | solution.py:311
  339.5 7.6 %collective-permute-start.29 = (bf16[48,768]{1,0:T(8,128)(2,1)S(1)}, bf16[48,768]{1,0:T(8,128)(2,1)S(1)}, u32[]{:S(2)}, u32[]{:S(2)}) collective-permute-start(bf16[48,768]{1,0:T(8,128)(2,1)S(1)} %pad_maximum_fusion.23), channel_id=1, source_target_pairs={{0,8},{2,10},{4,12},{6,14},{8,0},{10,2},{12,4},{14,6},{16,24},{18,... | collective-permute-start | bytes 221192 | tf_op jit(solution)/shard_map/ppermute | solution.py:311
  346.3 33.9 %collective-permute-start.32 = (bf16[2,384,1536]{2,1,0:T(8,128)(2,1)}, bf16[2,384,1536]{2,1,0:T(8,128)(2,1)}, u32[]{:S(2)}, u32[]{:S(2)}) collective-permute-start(bf16[2,384,1536]{2,1,0:T(8,128)(2,1)} %fusion.23), channel_id=1, source_target_pairs={{0,2},{2,0},{4,6},{6,4},{8,10},{10,8},{12,14},{14,12},{16,18},{18,... | collective-permute-start | bytes 7077896 | tf_op jit(solution)/shard_map/ppermute | solution.py:311
  346.3 5.4 %collective-permute-start.22 = (f32[7872]{0:T(1024)S(1)}, f32[7872]{0:T(1024)S(1)}, u32[]{:S(2)}, u32[]{:S(2)}) collective-permute-start(f32[7872]{0:T(1024)S(1)} %add.512), channel_id=1, source_target_pairs={{0,16},{2,18},{4,20},{6,22},{8,24},{10,26},{12,28},{14,30},{16,0},... | collective-permute-start | bytes 94472 | tf_op jit(solution)/shard_map/ppermute | solution.py:311
  347.2 6.0 %collective-permute-start.30 = (bf16[96,768]{1,0:T(8,128)(2,1)S(1)}, bf16[96,768]{1,0:T(8,128)(2,1)S(1)}, u32[]{:S(2)}, u32[]{:S(2)}) collective-permute-start(bf16[96,768]{1,0:T(8,128)(2,1)S(1)} %pad_maximum_fusion.22), channel_id=1, source_target_pairs={{0,4},{2,6},{4,0},{6,2},{8,12},{10,14},{12,8},{14,10},{16,20},{18,... | collective-permute-start | bytes 442376 | tf_op jit(solution)/shard_map/ppermute | solution.py:311
  350.0 49.5 %collective-permute-start.41 = (bf16[2,768,768]{2,1,0:T(8,128)(2,1)}, bf16[2,768,768]{2,1,0:T(8,128)(2,1)}, u32[]{:S(2)}, u32[]{:S(2)}) collective-permute-start(bf16[2,768,768]{2,1,0:T(8,128)(2,1)} %fusion.21), channel_id=1, source_target_pairs={{0,2},{2,0},{4,6},{6,4},{8,10},{10,8},{12,14},{14,12},{16,18},{18,... | collective-permute-start | bytes 7077896 | tf_op jit(solution)/shard_map/ppermute | solution.py:311
  356.6 21.1 %collective-permute-start.10 = (bf16[384,1152]{1,0:T(8,128)(2,1)S(1)}, bf16[384,1152]{1,0:T(8,128)(2,1)}, u32[]{:S(2)}, u32[]{:S(2)}) collective-permute-start(bf16[384,1152]{1,0:T(8,128)(2,1)S(1)} %slice_bitcast_fusion.4), channel_id=1, source_target_pairs={{0,1},{1,0},{2,3},{3,2},{4,5},{5,4},{6,7},{7,6},{8,9},{9,8},{10,11... | collective-permute-start | bytes 2654216 | tf_op jit(solution)/shard_map/ppermute | solution.py:311
  358.8 4.8 collective-permute-start.31
  362.0 15.6 %copy-start.15 = (bf16[2,384,1152]{2,1,0:T(8,128)(2,1)S(1)}, bf16[2,384,1152]{2,1,0:T(8,128)(2,1)}, u32[]{:S(2)}) copy-start(bf16[2,384,1152]{2,1,0:T(8,128)(2,1)} %copy-done.14) | copy-start | bytes 5308420
  364.7 15.5 %copy-start.7 = (bf16[1,768,1536]{2,1,0:T(8,128)(2,1)S(1)}, bf16[1,768,1536]{2,1,0:T(8,128)(2,1)}, u32[]{:S(2)}) copy-start(bf16[1,768,1536]{2,1,0:T(8,128)(2,1)} %fusion.18) | copy-start | bytes 7077892
  365.8 14.4 %copy-start.5 = (bf16[1,768,1536]{2,1,0:T(8,128)(2,1)S(1)}, bf16[1,768,1536]{2,1,0:T(8,128)(2,1)}, u32[]{:S(2)}) copy-start(bf16[1,768,1536]{2,1,0:T(8,128)(2,1)} %fusion.17) | copy-start | bytes 7077892
  379.2 10.6 %collective-permute-start.11 = (bf16[192,1152]{1,0:T(8,128)(2,1)S(1)}, bf16[192,1152]{1,0:T(8,128)(2,1)S(1)}, u32[]{:S(2)}, u32[]{:S(2)}) collective-permute-start(bf16[192,1152]{1,0:T(8,128)(2,1)S(1)} %constant_dynamic-slice_fusion.11), channel_id=1, source_target_pairs={{0,4},{2,6},{4,0},{6,2},{8,12},{10,14},{12,8},{14,10},{16,20},{18,... | collective-permute-start | bytes 1327112 | tf_op jit(solution)/shard_map/ppermute | solution.py:311
  382.5 17.0 %copy-start.9 = (bf16[1,1536,768]{2,1,0:T(8,128)(2,1)S(1)}, bf16[1,1536,768]{2,1,0:T(8,128)(2,1)}, u32[]{:S(2)}) copy-start(bf16[1,1536,768]{2,1,0:T(8,128)(2,1)} %fusion.20) | copy-start | bytes 7077892
  389.9 6.0 %collective-permute-start.12 = (bf16[96,1152]{1,0:T(8,128)(2,1)S(1)}, bf16[96,1152]{1,0:T(8,128)(2,1)S(1)}, u32[]{:S(2)}, u32[]{:S(2)}) collective-permute-start(bf16[96,1152]{1,0:T(8,128)(2,1)S(1)} %constant_dynamic-slice_fusion.10), channel_id=1, source_target_pairs={{0,8},{2,10},{4,12},{6,14},{8,0},{10,2},{12,4},{14,6},{16,24},{18,... | collective-permute-start | bytes 663560 | tf_op jit(solution)/shard_map/ppermute | solution.py:311
  390.7 29.0 %collective-permute-start.33 = (bf16[384,1536]{1,0:T(8,128)(2,1)S(1)}, bf16[384,1536]{1,0:T(8,128)(2,1)S(1)}, u32[]{:S(2)}, u32[]{:S(2)}) collective-permute-start(bf16[384,1536]{1,0:T(8,128)(2,1)S(1)} %slice_bitcast_fusion.2), channel_id=1, source_target_pairs={{0,1},{1,0},{2,3},{3,2},{4,5},{5,4},{6,7},{7,6},{8,9},{9,8},{10,11... | collective-permute-start | bytes 3538952 | tf_op jit(solution)/shard_map/ppermute | solution.py:311
  396.0 9.3 %collective-permute-start.13 = (bf16[48,1152]{1,0:T(8,128)(2,1)S(1)}, bf16[48,1152]{1,0:T(8,128)(2,1)S(1)}, u32[]{:S(2)}, u32[]{:S(2)}) collective-permute-start(bf16[48,1152]{1,0:T(8,128)(2,1)S(1)} %constant_dynamic-slice_fusion.9), channel_id=1, source_target_pairs={{0,16},{2,18},{4,20},{6,22},{8,24},{10,26},{12,28},{14,30},{16,0},... | collective-permute-start | bytes 331784 | tf_op jit(solution)/shard_map/ppermute | solution.py:311
  405.3 6.2 %collective-permute-start.14 = (bf16[48,1152]{1,0:T(8,128)(2,1)S(1)}, bf16[48,1152]{1,0:T(8,128)(2,1)S(1)}, u32[]{:S(2)}, u32[]{:S(2)}) collective-permute-start(bf16[48,1152]{1,0:T(8,128)(2,1)S(1)} %add_convert_fusion.13), channel_id=1, source_target_pairs={{0,16},{2,18},{4,20},{6,22},{8,24},{10,26},{12,28},{14,30},{16,0},... | collective-permute-start | bytes 331784 | tf_op jit(solution)/shard_map/ppermute | solution.py:311
  405.5 35.7 %collective-permute-start.42 = (bf16[768,768]{1,0:T(8,128)(2,1)S(1)}, bf16[768,768]{1,0:T(8,128)(2,1)S(1)}, u32[]{:S(2)}, u32[]{:S(2)}) collective-permute-start(bf16[768,768]{1,0:T(8,128)(2,1)S(1)} %slice_bitcast_fusion), channel_id=1, source_target_pairs={{0,1},{1,0},{2,3},{3,2},{4,5},{5,4},{6,7},{7,6},{8,9},{9,8},{10,11... | collective-permute-start | bytes 3538952 | tf_op jit(solution)/shard_map/ppermute | solution.py:311
  411.6 30.6 %collective-permute-start.15 = (bf16[96,1152]{1,0:T(8,128)(2,1)S(1)}, bf16[96,1152]{1,0:T(8,128)(2,1)S(1)}, u32[]{:S(2)}, u32[]{:S(2)}) collective-permute-start(bf16[96,1152]{1,0:T(8,128)(2,1)S(1)} %pad_maximum_fusion.21), channel_id=1, source_target_pairs={{0,8},{2,10},{4,12},{6,14},{8,0},{10,2},{12,4},{14,6},{16,24},{18,... | collective-permute-start | bytes 663560 | tf_op jit(solution)/shard_map/ppermute | solution.py:311
  420.0 23.8 %collective-permute-start.34 = (bf16[192,1536]{1,0:T(8,128)(2,1)S(1)}, bf16[192,1536]{1,0:T(8,128)(2,1)S(1)}, u32[]{:S(2)}, u32[]{:S(2)}) collective-permute-start(bf16[192,1536]{1,0:T(8,128)(2,1)S(1)} %constant_dynamic-slice_fusion.5), channel_id=1, source_target_pairs={{0,4},{2,6},{4,0},{6,2},{8,12},{10,14},{12,8},{14,10},{16,20},{18,... | collective-permute-start | bytes 1769480 | tf_op jit(solution)/shard_map/ppermute | solution.py:311
  441.6 16.3 %collective-permute-start.43 = (bf16[384,768]{1,0:T(8,128)(2,1)S(1)}, bf16[384,768]{1,0:T(8,128)(2,1)S(1)}, u32[]{:S(2)}, u32[]{:S(2)}) collective-permute-start(bf16[384,768]{1,0:T(8,128)(2,1)S(1)} %constant_dynamic-slice_fusion.2), channel_id=1, source_target_pairs={{0,4},{2,6},{4,0},{6,2},{8,12},{10,14},{12,8},{14,10},{16,20},{18,... | collective-permute-start | bytes 1769480 | tf_op jit(solution)/shard_map/ppermute | solution.py:311
  442.4 20.3 %collective-permute-start.16 = (bf16[192,1152]{1,0:T(8,128)(2,1)S(1)}, bf16[192,1152]{1,0:T(8,128)(2,1)S(1)}, u32[]{:S(2)}, u32[]{:S(2)}) collective-permute-start(bf16[192,1152]{1,0:T(8,128)(2,1)S(1)} %pad_maximum_fusion.15), channel_id=1, source_target_pairs={{0,4},{2,6},{4,0},{6,2},{8,12},{10,14},{12,8},{14,10},{16,20},{18,... | collective-permute-start | bytes 1327112 | tf_op jit(solution)/shard_map/ppermute | solution.py:311
  444.0 18.8 %collective-permute-start.35 = (bf16[96,1536]{1,0:T(8,128)(2,1)S(1)}, bf16[96,1536]{1,0:T(8,128)(2,1)S(1)}, u32[]{:S(2)}, u32[]{:S(2)}) collective-permute-start(bf16[96,1536]{1,0:T(8,128)(2,1)S(1)} %constant_dynamic-slice_fusion.4), channel_id=1, source_target_pairs={{0,8},{2,10},{4,12},{6,14},{8,0},{10,2},{12,4},{14,6},{16,24},{18,... | collective-permute-start | bytes 884744 | tf_op jit(solution)/shard_map/ppermute | solution.py:311
  458.1 10.2 %collective-permute-start.44 = (bf16[192,768]{1,0:T(8,128)(2,1)S(1)}, bf16[192,768]{1,0:T(8,128)(2,1)S(1)}, u32[]{:S(2)}, u32[]{:S(2)}) collective-permute-start(bf16[192,768]{1,0:T(8,128)(2,1)S(1)} %constant_dynamic-slice_fusion.1), channel_id=1, source_target_pairs={{0,8},{2,10},{4,12},{6,14},{8,0},{10,2},{12,4},{14,6},{16,24},{18,... | collective-permute-start | bytes 884744 | tf_op jit(solution)/shard_map/ppermute | solution.py:311
  463.0 14.7 %collective-permute-start.36 = (bf16[48,1536]{1,0:T(8,128)(2,1)S(1)}, bf16[48,1536]{1,0:T(8,128)(2,1)S(1)}, u32[]{:S(2)}, u32[]{:S(2)}) collective-permute-start(bf16[48,1536]{1,0:T(8,128)(2,1)S(1)} %constant_dynamic-slice_fusion.3), channel_id=1, source_target_pairs={{0,16},{2,18},{4,20},{6,22},{8,24},{10,26},{12,28},{14,30},{16,0},... | collective-permute-start | bytes 442376 | tf_op jit(solution)/shard_map/ppermute | solution.py:311
  468.4 12.4 %collective-permute-start.45 = (bf16[96,768]{1,0:T(8,128)(2,1)S(1)}, bf16[96,768]{1,0:T(8,128)(2,1)S(1)}, u32[]{:S(2)}, u32[]{:S(2)}) collective-permute-start(bf16[96,768]{1,0:T(8,128)(2,1)S(1)} %constant_dynamic-slice_fusion), channel_id=1, source_target_pairs={{0,16},{2,18},{4,20},{6,22},{8,24},{10,26},{12,28},{14,30},{16,0},... | collective-permute-start | bytes 442376 | tf_op jit(solution)/shard_map/ppermute | solution.py:311
  477.7 7.7 %collective-permute-start.37 = (bf16[48,1536]{1,0:T(8,128)(2,1)S(1)}, bf16[48,1536]{1,0:T(8,128)(2,1)S(1)}, u32[]{:S(2)}, u32[]{:S(2)}) collective-permute-start(bf16[48,1536]{1,0:T(8,128)(2,1)S(1)} %add_convert_fusion.11), channel_id=1, source_target_pairs={{0,16},{2,18},{4,20},{6,22},{8,24},{10,26},{12,28},{14,30},{16,0},... | collective-permute-start | bytes 442376 | tf_op jit(solution)/shard_map/ppermute | solution.py:311
  480.9 7.3 %collective-permute-start.46 = (bf16[96,768]{1,0:T(8,128)(2,1)S(1)}, bf16[96,768]{1,0:T(8,128)(2,1)S(1)}, u32[]{:S(2)}, u32[]{:S(2)}) collective-permute-start(bf16[96,768]{1,0:T(8,128)(2,1)S(1)} %add_convert_fusion.10), channel_id=1, source_target_pairs={{0,16},{2,18},{4,20},{6,22},{8,24},{10,26},{12,28},{14,30},{16,0},... | collective-permute-start | bytes 442376 | tf_op jit(solution)/shard_map/ppermute | solution.py:311
  485.4 8.2 %collective-permute-start.38 = (bf16[96,1536]{1,0:T(8,128)(2,1)S(1)}, bf16[96,1536]{1,0:T(8,128)(2,1)S(1)}, u32[]{:S(2)}, u32[]{:S(2)}) collective-permute-start(bf16[96,1536]{1,0:T(8,128)(2,1)S(1)} %pad_maximum_fusion.19), channel_id=1, source_target_pairs={{0,8},{2,10},{4,12},{6,14},{8,0},{10,2},{12,4},{14,6},{16,24},{18,... | collective-permute-start | bytes 884744 | tf_op jit(solution)/shard_map/ppermute | solution.py:311
  488.3 8.5 %collective-permute-start.47 = (bf16[192,768]{1,0:T(8,128)(2,1)S(1)}, bf16[192,768]{1,0:T(8,128)(2,1)S(1)}, u32[]{:S(2)}, u32[]{:S(2)}) collective-permute-start(bf16[192,768]{1,0:T(8,128)(2,1)S(1)} %pad_maximum_fusion.20), channel_id=1, source_target_pairs={{0,8},{2,10},{4,12},{6,14},{8,0},{10,2},{12,4},{14,6},{16,24},{18,... | collective-permute-start | bytes 884744 | tf_op jit(solution)/shard_map/ppermute | solution.py:311
  493.7 16.1 %collective-permute-start.39 = (bf16[192,1536]{1,0:T(8,128)(2,1)S(1)}, bf16[192,1536]{1,0:T(8,128)(2,1)S(1)}, u32[]{:S(2)}, u32[]{:S(2)}) collective-permute-start(bf16[192,1536]{1,0:T(8,128)(2,1)S(1)} %pad_maximum_fusion.13), channel_id=1, source_target_pairs={{0,4},{2,6},{4,0},{6,2},{8,12},{10,14},{12,8},{14,10},{16,20},{18,... | collective-permute-start | bytes 1769480 | tf_op jit(solution)/shard_map/ppermute | solution.py:311
  493.9 16.3 %collective-permute-start.17 = (bf16[384,1152]{1,0:T(8,128)(2,1)S(1)}, bf16[384,1152]{1,0:T(8,128)(2,1)S(1)}, u32[]{:S(2)}, u32[]{:S(2)}) collective-permute-start(bf16[384,1152]{1,0:T(8,128)(2,1)S(1)} %pad_maximum_fusion.11), channel_id=1, source_target_pairs={{0,2},{2,0},{4,6},{6,4},{8,10},{10,8},{12,14},{14,12},{16,18},{18,... | collective-permute-start | bytes 2654216 | tf_op jit(solution)/shard_map/ppermute | solution.py:311
  496.9 19.4 %collective-permute-start.48 = (bf16[384,768]{1,0:T(8,128)(2,1)S(1)}, bf16[384,768]{1,0:T(8,128)(2,1)S(1)}, u32[]{:S(2)}, u32[]{:S(2)}) collective-permute-start(bf16[384,768]{1,0:T(8,128)(2,1)S(1)} %pad_maximum_fusion.14), channel_id=1, source_target_pairs={{0,4},{2,6},{4,0},{6,2},{8,12},{10,14},{12,8},{14,10},{16,20},{18,... | collective-permute-start | bytes 1769480 | tf_op jit(solution)/shard_map/ppermute | solution.py:311
  510.1 8.5 %collective-permute-start.40 = (bf16[384,1536]{1,0:T(8,128)(2,1)S(1)}, bf16[384,1536]{1,0:T(8,128)(2,1)S(1)}, u32[]{:S(2)}, u32[]{:S(2)}) collective-permute-start(bf16[384,1536]{1,0:T(8,128)(2,1)S(1)} %pad_maximum_fusion.7), channel_id=1, source_target_pairs={{0,2},{2,0},{4,6},{6,4},{8,10},{10,8},{12,14},{14,12},{16,18},{18,... | collective-permute-start | bytes 3538952 | tf_op jit(solution)/shard_map/ppermute | solution.py:311
  516.6 5.2 collective-permute-start.49
  (57 other events, 292.2 us)

commit v2 on v1

v2 whole, which is shorter than its diff:
```python
from functools import partial
import math

import jax
import jax.numpy as jnp
from jax import lax
from jax.experimental import pallas as pl
from jax.experimental.pallas import tpu as pltpu
from jax.sharding import PartitionSpec as P

HEAD_DIM = 64
BUCKETS = 32
MAX_DIST = 128
BUCKETS_2D = 64
MAX_DIST_2D = 256
TEXT = 512
layer_eps = 1e-05

f32 = jnp.float32
bf = jnp.bfloat16
i16 = jnp.int16
PT = 256
NT = (((1,), (1,)), ((), ()))
VM = 56 << 20

def bucket_edges(buckets, farthest):
    exact=buckets//4
    r=list(range(1,exact+1))
    for k in range(1,exact):
        r.append(int(math.ceil(exact*(farthest/exact)**(k/exact)-1e-09)))
    return r
def lane_gather(table, index):
    dn=lax.GatherDimensionNumbers(offset_dims=(),collapsed_slice_dims=(1,),start_index_map=(1,),operand_batching_dims=(0,),start_indices_batching_dims=(0,))
    return lax.gather(table,index[...,None],dn,(1,1),mode=lax.GatherScatterMode.PROMISE_IN_BOUNDS)

def prep_kernel(len_ref, box_ref, own_ref, oth_ref, idx_ref, toep_ref, toep_o_ref, line_ref, col_ref, *, seq):
    rows, lanes = idx_ref.shape[1:]
    heads = toep_ref.shape[0]
    edges = bucket_edges(BUCKETS_2D, MAX_DIST_2D)
    near = [e for e in edges if e < 128]
    far = [e for e in edges if e >= 128]
    n = len_ref[0]
    rb = 16
    line_ref[...] = jnp.zeros_like(line_ref)
    line_ref[0:2, 0:seq] = box_ref[...].astype(f32)
    col_ref[...] = line_ref[...].T
    lane = lax.broadcasted_iota(jnp.int32, (rb, 128), 1)
    tab = jnp.zeros((rb, 128), jnp.int32)
    for e in near:
        tab = tab + jnp.where(lane >= e, 1, 0)
    tab = tab.astype(i16)

    def body(i, _):
        r = pl.ds(pl.multiple_of(i * rb, rb), rb)
        place = lax.broadcasted_iota(jnp.int32, (rb, 128), 0) + i * rb
        ok = ((place < n) | (place >= TEXT)) & (place < seq)
        for ax in range(2):
            col = jnp.broadcast_to(col_ref[r, ax:ax + 1], (rb, 128))
            for c in range(lanes // 128):
                cs = slice(c * 128, (c + 1) * 128)
                d = col - line_ref[ax:ax + 1, cs]
                a = jnp.abs(d)
                b = jnp.where(d > 0, float(BUCKETS_2D // 2), 0.0)
                for e in far:
                    b = b + jnp.where(a >= e, 1.0, 0.0)
                b = b.astype(jnp.int32).astype(i16) + lane_gather(tab, jnp.minimum(a, 127.0).astype(jnp.int32).astype(i16))
                if ax == 1:
                    b = jnp.where(ok, b.astype(jnp.int32), BUCKETS_2D).astype(i16)
                idx_ref[ax, r, cs] = b
        return 0

    lax.fori_loop(0, rows // rb, body, 0, unroll=5)
    for j in range(5):
        d = lax.broadcasted_iota(jnp.int32, (128, 128), 0) - lax.broadcasted_iota(jnp.int32, (128, 128), 1) + 128 * (j - 2)
        a = jnp.abs(d)
        b = jnp.zeros_like(d)
        for e in bucket_edges(BUCKETS, MAX_DIST):
            b = b + jnp.where(a >= e, 1, 0)
        b = (b + jnp.where(d > 0, BUCKETS // 2, 0)).astype(i16)
        for src, dst in ((own_ref, toep_ref), (oth_ref, toep_o_ref)):
            for h in range(heads):
                dst[h, j * 128:(j + 1) * 128, :] = lane_gather(jnp.broadcast_to(src[2 + h:3 + h, 0:128], (128, 128)), b)


VMEM = pl.BlockSpec(memory_space=pltpu.VMEM)
SMEM = pl.BlockSpec(memory_space=pltpu.SMEM)
ANY = pl.BlockSpec(memory_space=pl.ANY)


def prep(length, box, own, oth, heads, rows, lanes):
    seq = box.shape[1]
    toep = jax.ShapeDtypeStruct((heads, 640, 128), bf)
    return pl.pallas_call(
        partial(prep_kernel, seq=seq),
        out_shape=(jax.ShapeDtypeStruct((2, rows, lanes), i16), toep, toep),
        in_specs=[SMEM, VMEM, VMEM, VMEM],
        out_specs=(VMEM,) * 3,
        scratch_shapes=[pltpu.VMEM((8, lanes), f32), pltpu.VMEM((lanes, 8), f32)],
        compiler_params=pltpu.CompilerParams(vmem_limit_bytes=VM),
        name="buckets",
    )(length, box, own, oth)


def pack_kernel(bq, bv, bu, ts, tx, ty, bo, ga, sa, bd, gf, sf, small_ref, wide_ref):
    local = bq.shape[0]
    heads = ts.shape[0]
    hidden = bu.shape[0]
    small_ref[...] = jnp.zeros_like(small_ref)
    small_ref[0:1, 0:hidden] = bu[...][None]
    small_ref[1:2, 0:local] = bq[...][None]
    small_ref[1:2, 2 * local:3 * local] = bv[...][None]
    small_ref[2:2 + heads, 0:ts.shape[1]] = ts[...]
    small_ref[2:2 + heads, 128:128 + tx.shape[1]] = tx[...]
    small_ref[2:2 + heads, 256:384] = jnp.full((heads, 128), -1e9, bf)
    small_ref[2:2 + heads, 256:256 + ty.shape[1]] = ty[...]
    wide_ref[...] = jnp.zeros_like(wide_ref)
    for i, v in enumerate((bo, ga, sa, bd, gf, sf)):
        wide_ref[i:i + 1, :] = v[...].astype(f32)[None]


def pack(split, copied, width, hidden):
    return pl.pallas_call(
        pack_kernel,
        out_shape=(jax.ShapeDtypeStruct((16, hidden), bf), jax.ShapeDtypeStruct((8, width), f32)),
        in_specs=[VMEM] * 12,
        out_specs=(VMEM,) * 2,
        name="pack",
    )(*split, *copied)


def keep_rows(x,first_row,limit):
    rr=lax.broadcasted_iota(jnp.int32,(x.shape[0],1),0)+first_row
    return jnp.where(rr<limit,x,jnp.zeros_like(x))

def fwd_kernel(q_ref, k_ref, v_ref, idx_ref, toep_ref, small_ref, ctx_ref, p_ref, s_ref):
    H,rows,PT=p_ref.shape
    nch=PT//128
    tile=pl.program_id(0)
    lane=lax.broadcasted_iota(jnp.int32,(1,128),1)
    first=lane<HEAD_DIM
    for hp in range(H//2):
        hs=slice(hp*128,(hp+1)*128)
        q=keep_rows(q_ref[:,hs],tile*PT,rows)*jnp.asarray(HEAD_DIM**-0.5,bf)
        for h in range(2):
            qm=jnp.where(first if h==0 else ~first,q,jnp.zeros_like(q))
            s_ref[2*hp+h]=lax.dot_general(k_ref[:,hs],qm,NT,preferred_element_type=f32)
    tabs=[(jnp.broadcast_to(small_ref[2+h:3+h,128:256],(16,128)),jnp.broadcast_to(small_ref[2+h:3+h,256:384],(16,128))) for h in range(H)]
    cuts=[(h,c) for c in range(nch) for h in range(H)]
    def pass1(g,ms):
        r0=pl.multiple_of(g*16,16); r=pl.ds(r0,16)
        sb=r0//128; off=r0%128
        out=[]
        for c in range(nch):
            cs=slice(c*128,(c+1)*128)
            ix=idx_ref[0,r,cs]; iy=idx_ref[1,r,cs]
            tr=pl.ds(pl.multiple_of((jnp.clip(sb-(tile*nch+c),-2,2)+2)*128+off,16),16)
            gx=[lane_gather(tabs[h][0],ix) for h in range(H)]
            gy=[lane_gather(tabs[h][1],iy) for h in range(H)]
            for h in range(H):
                s=s_ref[h,r,cs]+gx[h].astype(f32)+gy[h].astype(f32)+toep_ref[h,tr,:].astype(f32)
                s_ref[h,r,cs]=s
                out.append(jnp.maximum(ms[c*H+h],jnp.maximum(s[:8],s[8:])))
        return tuple(out)
    ms=lax.fori_loop(0,rows//16,pass1,tuple(jnp.full((8,128),-jnp.inf,f32) for _ in cuts),unroll=9)
    ms=[jnp.max(m,axis=0,keepdims=True) for m in ms]
    def pass2(g,ls):
        r=pl.ds(pl.multiple_of(g*16,16),16)
        out=[]
        for i,(h,c) in enumerate(cuts):
            cs=slice(c*128,(c+1)*128)
            e=jnp.exp(s_ref[h,r,cs]-ms[i])
            s_ref[h,r,cs]=e
            out.append(ls[i]+(e[:8]+e[8:]))
        return tuple(out)
    ls=lax.fori_loop(0,rows//16,pass2,tuple(jnp.zeros((8,128),f32) for _ in cuts),unroll=5)
    inv=[1.0/jnp.sum(l,axis=0,keepdims=True) for l in ls]
    def pass3(g,_):
        r=pl.ds(pl.multiple_of(g*16,16),16)
        for i,(h,c) in enumerate(cuts):
            cs=slice(c*128,(c+1)*128)
            p_ref[h,r,cs]=(s_ref[h,r,cs]*inv[i]).astype(bf)
        return 0
    lax.fori_loop(0,rows//16,pass3,0,unroll=5)
    for hp in range(H//2):
        hs=slice(hp*128,(hp+1)*128)
        vt=v_ref[:,hs].T
        o=[jnp.dot(vt[h*64:(h+1)*64],p_ref[2*hp+h],preferred_element_type=f32) for h in range(2)]
        ctx_ref[:,hs]=jnp.concatenate(o,0).T.astype(bf)

def attn_fwd(q, k, v, idx, toep, small):
    rows, W = q.shape
    H = W // HEAD_DIM
    lanes = idx.shape[2]
    whole = lambda shape: pl.BlockSpec(shape, lambda i: (0,) * len(shape))
    return pl.pallas_call(
        fwd_kernel,
        grid=(lanes // PT,),
        in_specs=[pl.BlockSpec((PT, W), lambda i: (i, 0)), whole((rows, W)), whole((rows, W)), pl.BlockSpec((2, rows, PT), lambda i: (0, 0, i)), whole(toep.shape), whole(small.shape)],
        out_specs=(pl.BlockSpec((PT, W), lambda i: (i, 0)), pl.BlockSpec((H, rows, PT), lambda i: (0, 0, i))),
        out_shape=(jax.ShapeDtypeStruct((rows, W), bf), jax.ShapeDtypeStruct((H, rows, lanes), bf)),
        scratch_shapes=[pltpu.VMEM((H, rows, PT), f32)],
        compiler_params=pltpu.CompilerParams(vmem_limit_bytes=VM),
        name="attn_fwd",
        cost_estimate=pl.CostEstimate(flops=H * rows * lanes * 4096, bytes_accessed=H * rows * lanes * 2, transcendentals=H * rows * lanes),
    )(q, k, v, idx, toep, small)


def skip_refs(kernel, first, count, *refs):
    kernel(*refs[:first], *refs[first + count:])


def bwd_kernel(q_ref,k_ref,v_ref,do_ref,p_ref,dq_ref,dk_ref,dv_ref,gs_ref,dp_ref,dka,dva):
    H,rows,PT=p_ref.shape
    nch=PT//128
    tile=pl.program_id(0); last=pl.num_programs(0)-1
    lane=lax.broadcasted_iota(jnp.int32,(1,128),1)
    first=lane<HEAD_DIM
    scale=HEAD_DIM**-0.5
    cuts=[(h,c) for c in range(nch) for h in range(H)]
    split=lambda x: (jnp.where(first,x,jnp.zeros_like(x)),jnp.where(first,jnp.zeros_like(x),x))
    for hp in range(H//2):
        hs=slice(hp*128,(hp+1)*128)
        dm=split(keep_rows(do_ref[:,hs],tile*PT,rows))
        for h in range(2):
            dp_ref[2*hp+h]=lax.dot_general(v_ref[:,hs],dm[h],NT,preferred_element_type=f32)
    def pass1(g,ds):
        r=pl.ds(pl.multiple_of(g*16,16),16)
        out=[]
        for i,(h,c) in enumerate(cuts):
            cs=slice(c*128,(c+1)*128)
            t=p_ref[h,r,cs].astype(f32)*dp_ref[h,r,cs]
            out.append(ds[i]+(t[:8]+t[8:]))
        return tuple(out)
    ds=lax.fori_loop(0,rows//16,pass1,tuple(jnp.zeros((8,128),f32) for _ in cuts),unroll=9)
    ds=[jnp.sum(d,axis=0,keepdims=True) for d in ds]
    def pass2(g,_):
        r=pl.ds(pl.multiple_of(g*16,16),16)
        for i,(h,c) in enumerate(cuts):
            cs=slice(c*128,(c+1)*128)
            gs_ref[h,r,cs]=(p_ref[h,r,cs].astype(f32)*(dp_ref[h,r,cs]-ds[i])).astype(bf)
        return 0
    lax.fori_loop(0,rows//16,pass2,0,unroll=9)
    @pl.when(tile==0)
    def _():
        dka[...]=jnp.zeros_like(dka); dva[...]=jnp.zeros_like(dva)
    for hp in range(H//2):
        hs=slice(hp*128,(hp+1)*128)
        kt=k_ref[:,hs].T
        o=[jnp.dot(kt[h*64:(h+1)*64],gs_ref[2*hp+h],preferred_element_type=f32) for h in range(2)]
        dq_ref[:,hs]=(jnp.concatenate(o,0)*scale).T.astype(bf)
        qm=split(keep_rows(q_ref[:,hs],tile*PT,rows))
        dm=split(keep_rows(do_ref[:,hs],tile*PT,rows))
        dka[:,hs]+=jnp.dot(gs_ref[2*hp],qm[0],preferred_element_type=f32)+jnp.dot(gs_ref[2*hp+1],qm[1],preferred_element_type=f32)
        dva[:,hs]+=jnp.dot(p_ref[2*hp],dm[0],preferred_element_type=f32)+jnp.dot(p_ref[2*hp+1],dm[1],preferred_element_type=f32)
    @pl.when(tile==last)
    def _():
        dk_ref[...]=(dka[...]*scale).astype(bf)
        dv_ref[...]=dva[...].astype(bf)

def attn_bwd(q, k, v, do, p, after=()):
    rows, W = q.shape
    H = W // HEAD_DIM
    lanes = p.shape[2]
    tilew = pl.BlockSpec((PT, W), lambda i: (i, 0))
    whole = pl.BlockSpec((rows, W), lambda i: (0, 0))
    big = pl.BlockSpec((H, rows, PT), lambda i: (0, 0, i))
    o = jax.ShapeDtypeStruct((rows, W), bf)
    return pl.pallas_call(
        partial(skip_refs, bwd_kernel, 5, len(after)),
        grid=(lanes // PT,),
        in_specs=[tilew, whole, whole, tilew, big] + [ANY] * len(after),
        out_specs=(tilew, whole, whole, big),
        out_shape=(o, o, o, jax.ShapeDtypeStruct((H, rows, lanes), bf)),
        scratch_shapes=[pltpu.VMEM((H, rows, PT), f32), pltpu.VMEM((rows, W), f32), pltpu.VMEM((rows, W), f32)],
        compiler_params=pltpu.CompilerParams(vmem_limit_bytes=VM),
        name="attn_bwd",
        cost_estimate=pl.CostEstimate(flops=H * rows * lanes * 4096, bytes_accessed=H * rows * lanes * 4, transcendentals=0),
    )(q, k, v, do, p, *after)


def hist_kernel(gs_ref, go_ref, idx_ref, out_ref, toep_ref, acc, accT, *, part):
    H, rows, lanes = gs_ref.shape
    SB = 16
    heads = 2 * H
    near = BUCKETS_2D // 2
    step = pl.program_id(0)

    @pl.when(step == 0)
    def _():
        acc[...] = jnp.zeros_like(acc)
        accT[...] = jnp.zeros_like(accT)

    iota = lax.broadcasted_iota(jnp.int32, (near, lanes), 0).astype(i16)
    one = jnp.ones((near, lanes), bf)
    zero = jnp.zeros((near, lanes), bf)

    def body(i, _):
        r = pl.ds(pl.multiple_of(i * SB, SB), SB)
        s0 = (part + step) * rows + i * SB
        sb = s0 // 128
        off = pl.multiple_of(s0 % 128, SB)
        idx = [idx_ref[ax, r, :] for ax in range(2)]
        positive = [(x >= near).astype(i16).astype(jnp.int32) > 0 for x in idx]
        cols = [[], []]
        for ref in (gs_ref, go_ref):
            for h in range(H):
                full = ref[h, r, :].astype(f32)
                k = len(cols[0])
                for c in range(lanes // 128):
                    at = pl.ds(pl.multiple_of((jnp.clip(sb - c, -2, 2) + 2) * 128 + off, SB), SB)
                    accT[k, at, :] += full[:, c * 128:(c + 1) * 128]
                for ax in range(2):
                    some = jnp.where(positive[ax], full, 0.0)
                    cols[ax].append([jnp.concatenate([full[t:t + 8], some[t:t + 8]], 0).astype(bf) for t in (0, 8)])
        for ax in range(2):
            ix = jnp.bitwise_and(idx[ax], jnp.asarray(near - 1, i16))
            left = []
            right = []
            for t in range(2):
                left.append(jnp.concatenate([jnp.where(iota == ix[t * 8 + p:t * 8 + p + 1, :], one, zero) for p in range(8)], 0))
                right.append(jnp.concatenate([x[t] for x in cols[ax]], 0))
            acc[ax] += lax.dot_general(jnp.concatenate(left, 1), jnp.concatenate(right, 1), NT, preferred_element_type=f32)
        return 0

    lax.fori_loop(0, rows // SB, body, 0, unroll=3)

    @pl.when(step == pl.num_programs(0) - 1)
    def _():
        lane = lax.broadcasted_iota(jnp.int32, (near, heads * SB), 1) % 8
        for ax in range(2):
            t = jnp.zeros((near, heads * SB), f32)
            for p in range(8):
                t = t + jnp.where(lane == p, acc[ax, p * near:(p + 1) * near, :], 0.0)
            out_ref[ax] = t
        m = lax.broadcasted_iota(jnp.int32, (128, 128), 1)
        turned = m + lax.broadcasted_iota(jnp.int32, (128, 128), 0)
        wraps = turned >= 128
        turned = jnp.where(wraps, turned - 128, turned)
        for h in range(heads):
            for j in (-1, 0, 1):
                x = lane_gather(accT[h, (j + 2) * 128:(j + 3) * 128, :], turned)
                at = 2 * (j + 1)
                toep_ref[h, at:at + 1, :] = jnp.sum(jnp.where(wraps, 0.0, x), axis=0, keepdims=True)
                toep_ref[h, at + 1:at + 2, :] = jnp.sum(jnp.where(wraps, x, 0.0), axis=0, keepdims=True)
            toep_ref[h, 6:7, :] = jnp.sum(accT[h, 0:128, :], axis=0, keepdims=True)
            toep_ref[h, 7:8, :] = jnp.sum(accT[h, 512:640, :], axis=0, keepdims=True)


def hist(gs, go, idx, part, parts, after=()):
    H, rows, lanes = gs.shape
    SB = 48
    steps = rows // SB // parts
    part = part * steps
    near = BUCKETS_2D // 2
    big = pl.BlockSpec((H, SB, lanes), lambda i: (0, part + i, 0))
    return pl.pallas_call(
        partial(skip_refs, partial(hist_kernel, part=part), 3, len(after)),
        grid=(steps,),
        in_specs=[big, big, pl.BlockSpec((2, SB, lanes), lambda i: (0, part + i, 0))] + [ANY] * len(after),
        out_specs=(pl.BlockSpec((2, near, 2 * H * 16), lambda i: (0, 0, 0)), pl.BlockSpec((2 * H, 8, 128), lambda i: (0, 0, 0))),
        out_shape=(jax.ShapeDtypeStruct((2, near, 2 * H * 16), f32), jax.ShapeDtypeStruct((2 * H, 8, 128), f32)),
        scratch_shapes=[pltpu.VMEM((2, 8 * near, 2 * H * 16), f32), pltpu.VMEM((2 * H, 640, 128), f32)],
        compiler_params=pltpu.CompilerParams(vmem_limit_bytes=VM),
        name="table_sums",
        cost_estimate=pl.CostEstimate(flops=steps * SB * 128 * lanes * 2 * H * 32, bytes_accessed=4 * H * steps * SB * lanes, transcendentals=0),
    )(gs, go, idx, *after)


def tables_of(sums):
    out = sum(s[0] for s in sums)
    toep = sum(s[1] for s in sums)
    heads = toep.shape[0]
    xy = out.reshape(2, BUCKETS_2D // 2, heads, 2, 8).sum(4).transpose(0, 2, 3, 1)
    xy = jnp.concatenate([xy[:, :, 0] - xy[:, :, 1], xy[:, :, 1]], 2)
    line = toep.reshape(heads, 1024)
    base = jnp.array([-128, 0, 0, 128, 128, 256, -MAX_DIST - 128, MAX_DIST + 256])
    d = (base[:, None] - jnp.arange(128)).reshape(1024)
    b = jnp.zeros_like(d)
    for e in bucket_edges(BUCKETS, MAX_DIST):
        b = b + (jnp.abs(d) >= e)
    b = b + (d > 0) * (BUCKETS // 2)
    seq = jnp.dot(line, (b[:, None] == jnp.arange(BUCKETS)).astype(f32), precision=lax.Precision.HIGHEST)
    return seq, xy[0], xy[1]


def swap(value, axis, bit=1):
    count = lax.axis_size(axis)
    return lax.ppermute(value, axis, [(i, i ^ bit) for i in range(count)])


def half_of(value, axis, which):
    size = value.shape[axis] // 2
    return lax.dynamic_slice_in_dim(value, which * size, size, axis)


def join(mine, theirs, which, axis):
    low = jnp.where(which == 0, mine, theirs)
    high = jnp.where(which == 0, theirs, mine)
    return jnp.concatenate([low, high], axis)


def far_bits():
    count = lax.axis_size("far")
    bits = []
    bit = 1
    while bit < count:
        bits.append(bit)
        bit *= 2
    return bits


def add_low(a, b):
    return (a.astype(f32) + b.astype(f32)).astype(bf)


def core_sum(own, other):
    core = lax.axis_index("core")
    both = jnp.stack([own, other])
    return add_low(half_of(both, 1, core), swap(half_of(both, 1, 1 - core), "core"))


def tensor_sum(both):
    return add_low(both[0], swap(both[1], "tensor"))


def far_halve(total, bit):
    at = (lax.axis_index("far") // bit) % 2
    return add_low(half_of(total, 0, at), swap(half_of(total, 0, 1 - at), "far", bit))


def far_double(total, bit):
    return join(total, swap(total, "far", bit), (lax.axis_index("far") // bit) % 2, 0)


def core_join(total):
    return join(total, swap(total, "core"), lax.axis_index("core"), 0).astype(f32)


def reduce_small(own, other):
    total = own + swap(other, "tensor")
    total = total + swap(total, "core")
    for bit in far_bits():
        total = total + swap(total, "far", bit)
    return total


def norm_parts(values):
    center = values - jnp.mean(values, axis=1, keepdims=True)
    inverse = lax.rsqrt(jnp.mean(center * center, axis=1, keepdims=True) + layer_eps)
    return center * inverse, inverse


def norm_back(grad_scaled, scaled, inverse):
    return inverse * (
        grad_scaled
        - jnp.mean(grad_scaled, axis=1, keepdims=True)
        - scaled * jnp.mean(grad_scaled * scaled, axis=1, keepdims=True)
    )


def gelu_parts(v):
    cdf = 0.5 * (1.0 + lax.erf(v * (0.5 ** 0.5)))
    pdf = jnp.exp(-0.5 * v * v) * (1.0 / math.sqrt(2.0 * math.pi))
    return v * cdf, cdf + v * pdf


def mm(a, b):
    return jnp.dot(a, b, preferred_element_type=f32)


def mm_nt(a, b):
    return lax.dot_general(a, b, (((1,), (1,)), ((), ())), preferred_element_type=f32)


def mm_tn(a, b):
    return lax.dot_general(a, b, (((0,), (0,)), ((), ())), preferred_element_type=f32)


def per_device(
    tokens, text_len, box_coords, w_query, b_query, w_key, w_value, b_value, w_out, b_out,
    table_seq, table_x, table_y, gain_attn, shift_attn, w_up, b_up, w_down, b_down,
    gain_ffn, shift_ffn, cotangent,
):
    seq, width = tokens.shape[1:]
    rows = -(-seq // 240) * 240
    lanes = -(-rows // PT) * PT
    local = w_query.shape[1]
    heads = local // HEAD_DIM
    hidden = w_up.shape[1]
    core = lax.axis_index("core")

    small, wide = pack(
        [b_query, b_value, b_up, table_seq, table_x, table_y],
        [b_out, gain_attn, shift_attn, b_down, gain_ffn, shift_ffn], width, hidden,
    )
    small_o = swap(small, "tensor")
    b_out, gain_attn, shift_attn, b_down, gain_ffn, shift_ffn = [wide[i:i + 1] for i in range(6)]

    def fetch(mine):
        got = swap(mine, "tensor")
        return join(got, swap(got, "core"), core, mine.ndim - 2)

    wqkv_o = fetch(jnp.stack([half_of(w, 0, core) for w in (w_query, w_key, w_value)]))
    wq_o, wk_o, wv_o = wqkv_o[0], wqkv_o[1], wqkv_o[2]
    wo_o, wu_o, wd_o = [fetch(half_of(w, 0, core)) for w in (w_out, w_up, w_down)]

    x = jnp.pad(tokens[0], ((0, rows - seq), (0, 0)))
    g = jnp.pad(cotangent[0], ((0, rows - seq), (0, 0)))

    def project(wq, wk, wv, vectors):
        bias = vectors[1:2].astype(f32)
        return (
            (mm(x, wq) + bias[:, :local]).astype(bf),
            mm(x, wk).astype(bf),
            (mm(x, wv) + bias[:, 2 * local:3 * local]).astype(bf),
        )

    idx, toep, toep_o = prep(text_len, box_coords[0], small, small_o, heads, rows, lanes)
    q, k, v = project(w_query, w_key, w_value, small)
    ctx, prob = attn_fwd(q, k, v, idx, toep, small)
    q_o, k_o, v_o = project(wq_o, wk_o, wv_o, small_o)
    ctx_o, prob_o = attn_fwd(q_o, k_o, v_o, idx, toep_o, small_o)

    attn = mm(ctx, w_out) + mm(ctx_o, wo_o) + b_out
    n1, inv1 = norm_parts(x.astype(f32) + attn)
    normed = n1 * gain_attn + shift_attn
    low = normed.astype(bf)
    act, slope = gelu_parts(mm(low, w_up) + small[0:1].astype(f32))
    act_o, slope_o = gelu_parts(mm(low, wu_o) + small_o[0:1].astype(f32))
    act, act_o = act.astype(bf), act_o.astype(bf)
    slope, slope_o = slope.astype(bf), slope_o.astype(bf)
    branch = mm(act, w_down) + mm(act_o, wd_o) + b_down
    n2, inv2 = norm_parts(normed + branch)
    output = (n2 * gain_ffn + shift_ffn).astype(bf)[:seq][None]

    gf = g.astype(f32)
    grad_gain_ffn = jnp.sum(gf * n2, axis=0)
    grad_shift_ffn = jnp.sum(gf, axis=0)
    grad_mid = norm_back(gf * gain_ffn, n2, inv2)
    gb = grad_mid.astype(bf)
    grad_b_down = jnp.sum(gb.astype(f32), axis=0)
    down = core_sum(mm_tn(act, gb).astype(bf), mm_tn(act_o, gb).astype(bf))
    gh = (mm_nt(gb, w_down) * slope.astype(f32)).astype(bf)
    gh_o = (mm_nt(gb, wd_o) * slope_o.astype(f32)).astype(bf)
    grad_b_up = jnp.sum(gh.astype(f32), axis=0)
    grad_b_up_o = jnp.sum(gh_o.astype(f32), axis=0)
    grad_normed = mm_nt(gh, w_up) + mm_nt(gh_o, wu_o) + grad_mid
    grad_gain_attn = jnp.sum(grad_normed * n1, axis=0)
    grad_shift_attn = jnp.sum(grad_normed, axis=0)
    grad_first = norm_back(grad_normed * gain_attn, n1, inv1)
    ga = grad_first.astype(bf)
    grad_b_out = jnp.sum(ga.astype(f32), axis=0)
    gc = mm_nt(ga, w_out).astype(bf)
    gc_o = mm_nt(ga, wo_o).astype(bf)
    bits = far_bits()

    def wide_rows(first, second):
        second = second.reshape(-1, first.shape[1])
        extra = -(first.shape[0] + second.shape[0]) % (2 * lax.axis_size("far"))
        return jnp.concatenate([first, second, jnp.zeros((extra, first.shape[1]), bf)], 0)

    up = core_sum(
        wide_rows(mm_tn(low, gh).astype(bf), mm_tn(ctx, ga).astype(bf)),
        wide_rows(mm_tn(low, gh_o).astype(bf), mm_tn(ctx_o, ga).astype(bf)),
    )
    dq, dk, dv, gs = attn_bwd(q, k, v, gc, prob, (up,))
    down = tensor_sum(down)
    dq_o, dk_o, dv_o, gs_o = attn_bwd(q_o, k_o, v_o, gc_o, prob_o, (down,))
    grads = [mm_tn(x, d).astype(bf) for d in (dq, dk, dv, dq_o, dk_o, dv_o)]
    qkv = core_sum(jnp.concatenate(grads[:3], 1), jnp.concatenate(grads[3:], 1))
    up = tensor_sum(up)
    sums = [hist(gs, gs_o, idx, 0, 3, (qkv, up))]
    up = far_halve(up, bits[0])
    sums.append(hist(gs, gs_o, idx, 1, 3, (up,)))
    up = far_halve(up, bits[1])
    qkv = tensor_sum(qkv)
    sums.append(hist(gs, gs_o, idx, 2, 3, (up, qkv)))
    for bit in bits[2:]:
        up = far_halve(up, bit)
    for bit in bits[::-1]:
        up = far_double(up, bit)
    for bit in bits:
        qkv = far_halve(qkv, bit)
    for bit in bits[::-1]:
        qkv = far_double(qkv, bit)
    down = lax.psum(down, "far")
    late = lax.optimization_barrier((sums[-1][0], down, dq, dk, dv, dq_o, dk_o, dv_o))
    grad_w_down = core_join(late[1])
    up = core_join(up)
    grad_w_up = up[:width]
    grad_w_out = up[width:width + w_out.size // hidden].reshape(w_out.shape)
    qkv = core_join(qkv)
    t_seq, t_x, t_y = tables_of(sums)
    grad_tokens = grad_first
    for d, w in zip(late[2:], (w_query, w_key, w_value, wq_o, wk_o, wv_o)):
        grad_tokens = grad_tokens + mm_nt(d, w)
    grad_tokens = grad_tokens[:seq][None]

    bias_sums = [jnp.sum(d.astype(f32), axis=0) for d in (dq, dv, dq_o, dv_o)]
    shared = [grad_b_out, grad_gain_attn, grad_shift_attn, grad_b_down, grad_gain_ffn, grad_shift_ffn]

    def packed(query_sum, value_sum, up_sum, at):
        tables = [t[at:at + heads].reshape(-1) for t in (t_seq, t_x, t_y)]
        return jnp.concatenate([query_sum, value_sum, up_sum] + tables + shared)

    totals = reduce_small(packed(*bias_sums[:2], grad_b_up, 0), packed(*bias_sums[2:], grad_b_up_o, heads))
    shapes = [(local,), (local,), (hidden,), table_seq.shape, table_x.shape, table_y.shape] + [(width,)] * 6
    pieces = []
    at = 0
    for shape in shapes:
        size = math.prod(shape)
        pieces.append(totals[at:at + size].reshape(shape))
        at += size
    g_bq, g_bv, g_bu, g_ts, g_tx, g_ty, g_bo, g_ga, g_sa, g_bd, g_gf, g_sf = pieces
    return (
        output, grad_tokens,
        qkv[:, :local], g_bq, qkv[:, local:2 * local], qkv[:, 2 * local:], g_bv,
        grad_w_out, g_bo, g_ts, g_tx, g_ty, g_ga, g_sa, grad_w_up, g_bu, grad_w_down, g_bd, g_gf, g_sf,
    )


def solution(mesh):
    grid = mesh.devices.shape
    mesh = jax.sharding.Mesh(mesh.devices.reshape(grid[0] // 2, 2, grid[1]), ("far", "core", "tensor"))
    every = ("far", "core", "tensor")
    item = P(every, None, None)
    column, row, split, copied = P(None, "tensor"), P("tensor", None), P("tensor"), P()
    return jax.shard_map(
        per_device,
        mesh=mesh,
        in_specs=(
            item, P(every), item, column, split, column, column, split, row, copied,
            row, row, row, copied, copied, column, split, row, copied, copied, copied, item,
        ),
        out_specs=(
            item, item, column, split, column, column, split, row, copied, row, row, row,
            copied, copied, column, split, row, copied, copied, copied,
        ),
        check_vma=False,
    )
```

time: 530 us -> 433 us (0.82)
  waiting for transfers between devices: 134 us -> 88 us
  Pallas kernels: 157 us -> 114 us
  local copies, waits for them, and re-layouts: 62.6 us -> 32.3 us
  between operations: 2.87 us -> 16.3 us
  matrix products: 65.7 us -> 76.9 us
  starting transfers between devices: 45.8 us -> 40.3 us
    ppermute x50 -> x35, waiting for transfers between devices: 134 us -> 85.4 us  [swap(): return lax.ppermute(value, axis, [(i, i ^ bit) for i in range(count)])]
    pallas_call x4 -> x7, Pallas kernels: 99.9 us -> 76.7 us  [the longest x3 35.2 us: hist(): pl.pallas_call(partial(skip_refs, partial(hist_kernel, part=part), 3, len...]
    pallas_call x2, Pallas kernels: 57.4 us -> 37.2 us  [attn_fwd(): pl.pallas_call(fwd_kernel, grid=(lanes // PT,), in_specs=[pl.BlockSpec((P...]
    concatenate x9 -> x2, local copies, waits for them, and re-layouts: 9 us -> 0.18 us  [packed(): return jnp.concatenate([query_sum, value_sum, up_sum] + tables + shared)]
    dot_general x8 -> x12, matrix products: 24.9 us -> 33.1 us  [mm_nt(): lax.dot_general(a, b, (((1,), (1,)), ((), ())), preferred_element_type=f32)]
    convert_element_type x13 -> x5, other arithmetic: 13.9 us -> 7.1 us  [the longest x3 5.61 us: core_join(): join(total, swap(total, 'core'), lax.axis_index('core'), 0).astype(f32)]
    unnamed x151 -> x149, local copies, waits for them, and re-layouts: 16.4 us -> 10.3 us
    ppermute x50 -> x35, starting transfers between devices: 45.8 us -> 40.2 us  [swap(): return lax.ppermute(value, axis, [(i, i ^ bit) for i in range(count)])]
  transfers between devices with their start and end apart: 50 -> 36, of which waited for: 25 -> 17; matrix products, arithmetic and copies ran while one was open for 23% -> 27% of each run, Pallas kernels for 23% -> 26%
where the time goes in v2:
time: 433 us; the launch traced here: 429 us
  Pallas kernels  114 us (26%)
  waiting for transfers between devices  88 us (20%)
  matrix products  76.9 us (18%)
  other arithmetic  60.9 us (14%)
  starting transfers between devices  40.3 us (9%)
  local copies, waits for them, and re-layouts  32.3 us (7%)
  between operations  16.3 us (4%)
    ppermute x35, waiting for transfers between devices, swap(): return lax.ppermute(value, axis, [(i, i ^ bit) for i in range(count)])  85.4 us
    ppermute x35, starting transfers between devices, swap(): return lax.ppermute(value, axis, [(i, i ^ bit) for i in range(count)])  40.2 us
    pallas_call x2, Pallas kernels, attn_fwd(): pl.pallas_call(fwd_kernel, grid=(lanes // PT,), in_specs=[pl.BlockSpec((P...  37.2 us
    pallas_call x3, Pallas kernels, hist(): pl.pallas_call(partial(skip_refs, partial(hist_kernel, part=part), 3, len...  35.2 us
    dot_general x12, matrix products, mm_nt(): lax.dot_general(a, b, (((1,), (1,)), ((), ())), preferred_element_type=f32)  33.1 us
    pallas_call x2, Pallas kernels, attn_bwd(): pl.pallas_call(partial(skip_refs, bwd_kernel, 5, len(after)), grid=(lanes...  31.8 us
    dot_general x12, matrix products, mm(): return jnp.dot(a, b, preferred_element_type=f32)  21.9 us
    dot_general x12, matrix products, mm_tn(): lax.dot_general(a, b, (((0,), (0,)), ((), ())), preferred_element_type=f32)  21.5 us
  transfers between devices with their start and end apart: 36, of which 17 were waited for; matrix products, arithmetic and copies ran while one was open for 27% of the time, Pallas kernels for 26%

profile of v2, /device:TPU:0, one launch (start us, length us, event | category | flops | bytes accessed | tf_op | source)
XLA Modules:
  0.0 428.7 jit_solution(7724944944779966096)
XLA Ops:
  8.8 2.9 collective-permute-start
  15.7 2.0 collective-permute-start.3
  18.8 2.5 constant_dynamic-slice_fusion.6
  21.3 2.0 collective-permute-start.7
  32.4 8.1 %buckets.1 = (s16[2,720,768]{2,1,0:T(8,128)(2,1)}, bf16[6,640,128]{2,1,0:T(8,128)(2,1)}, bf16[6,640,128]{2,1,0:T(8,128)(2,1)}) custom-call(s32[1]{0:T(128)S(6)} %copy.93.len_ref, s32[2,709]{1,0:T(2,128)} %bitcast.158, bf16[16,1536]{1,0:T(8,128)(2,1)} %get-tuple-element.50.own_ref.small_ref, bf16[16,1536]{1,0:T(8,128)(2,1)} %copy-done.59), custom_call_target="tpu_custom_call" | custom-call | tf_op jit(solution)/shard_map/buckets/pallas_call | solution.py:93
  40.5 18.7 %attn_fwd.2 = (bf16[720,384]{1,0:T(8,128)(2,1)}, bf16[6,720,768]{2,1,0:T(8,128)(2,1)}) custom-call(bf16[720,384]{1,0:T(8,128)(2,1)} %fusion.34.q_ref.refs_0_, bf16[720,384]{1,0:T(8,128)(2,1)} %convolution_convert_fusion.15.k_ref.refs_1_, bf16[720,384]{1,0:T(8,128)(2,1)} %fusion.35.v_ref.refs_2_, s16[2,720,768]{2,1,0:T(8,128)(2,1)} %get-tuple-element.51.idx_ref.refs_2_, ...), custom_call_target="tpu_custom_call" | custom-call | flops 13589544960 | bytes 6635520 | tf_op jit(solution)/shard_map/attn_fwd/pallas_call | solution.py:195
  62.4 7.1 %collective-permute-done.5 = bf16[384,1536]{1,0:T(8,128)(2,1)} collective-permute-done((bf16[384,1536]{1,0:T(8,128)(2,1)}, bf16[384,1536]{1,0:T(8,128)(2,1)}, u32[]{:S(2)}, u32[]{:S(2)}) %collective-permute-start.5) | collective-permute-done | bytes 1179680 | tf_op jit(solution)/shard_map/ppermute | solution.py:388
  69.4 23.8 %collective-permute-done.7 = bf16[768,768]{1,0:T(8,128)(2,1)} collective-permute-done((bf16[768,768]{1,0:T(8,128)(2,1)}, bf16[768,768]{1,0:T(8,128)(2,1)}, u32[]{:S(2)}, u32[]{:S(2)}) %collective-permute-start.7) | collective-permute-done | bytes 1179680 | tf_op jit(solution)/shard_map/ppermute | solution.py:388
  99.3 18.6 %attn_fwd.3 = (bf16[720,384]{1,0:T(8,128)(2,1)}, bf16[6,720,768]{2,1,0:T(8,128)(2,1)}) custom-call(bf16[720,384]{1,0:T(8,128)(2,1)} %add_convert_fusion.4.q_ref.refs_0_, bf16[720,384]{1,0:T(8,128)(2,1)} %convolution_convert_fusion.14.k_ref.refs_1_, bf16[720,384]{1,0:T(8,128)(2,1)} %fusion.36.v_ref.refs_2_, ...), custom_call_target="tpu_custom_call" | custom-call | flops 13589544960 | bytes 6635520 | tf_op jit(solution)/shard_map/attn_fwd/pallas_call | solution.py:195
  117.9 1.9 fusion.44
  121.6 2.4 multiply_convert_fusion.3
  124.0 1.9 fusion.122
  127.3 3.1 multiply_convert_fusion.2
  131.9 2.3 fusion.109
  137.9 4.3 convert_reduce_fusion.1
  142.2 1.9 fusion.123
  144.1 3.5 convolution_convert_fusion.3
  147.5 6.1 %convert_reduce_fusion = (f32[1536]{0:T(1024)}, bf16[720,1536]{1,0:T(8,128)(2,1)S(1)}) fusion(f32[720,1536]{1,0:T(8,128)S(1)} %get-tuple-element.236, f32[1536]{0:T(1024)S(1)} %fusion.46, bf16[720,768]{1,0:T(8,128)(2,1)S(1)} %get-tuple-element.183, bf16[768,768]{1,0:T(8,128)(2,1)S(1)} %get-tuple-element.196, bf16[768,768]{1,0:T(8,128)(2,1)S(1)} %get-tuple-element.195), kind=kOutput, calls=%fused_computation.22 | convolution fusion | flops 1719998976 | bytes 10113024 | tf_op jit(solution)/shard_map/dot_general | solution.py:472
  153.6 3.4 multiply_reduce_fusion
  157.0 2.2 convert_reduce_fusion.4
  162.2 3.4 convolution_convert_fusion.2
  165.6 2.1 fusion.13
  167.7 3.5 fusion.14
  173.5 3.0 fusion.18
  178.4 1.9 fusion.15
  182.9 3.1 convolution_convert_fusion.12.refs_3_
  189.6 2.4 add_convert_fusion.1
  193.5 2.6 add_convert_fusion.refs_5_
  199.2 16.0 %attn_bwd.2 = (bf16[720,384]{1,0:T(8,128)(2,1)}, bf16[720,384]{1,0:T(8,128)(2,1)}, bf16[720,384]{1,0:T(8,128)(2,1)}, bf16[6,720,768]{2,1,0:T(8,128)(2,1)}) custom-call(bf16[720,384]{1,0:T(8,128)(2,1)} %fusion.34.q_ref.refs_0_, bf16[720,384]{1,0:T(8,128)(2,1)} %convolution_convert_fusion.15.k_ref.refs_1_, bf16[720,384]{1,0:T(8,128)(2,1)} %fusion.35.v_ref.refs_2_, ...), custom_call_target="tpu_custom_call" | custom-call | flops 13589544960 | bytes 13271040 | tf_op jit(solution)/shard_map/attn_bwd/pallas_call | solution.py:268
  224.4 15.7 %attn_bwd.3 = (bf16[720,384]{1,0:T(8,128)(2,1)}, bf16[720,384]{1,0:T(8,128)(2,1)}, bf16[720,384]{1,0:T(8,128)(2,1)}, bf16[6,720,768]{2,1,0:T(8,128)(2,1)}) custom-call(bf16[720,384]{1,0:T(8,128)(2,1)} %add_convert_fusion.4.q_ref.refs_0_, bf16[720,384]{1,0:T(8,128)(2,1)} %convolution_convert_fusion.14.k_ref.refs_1_, bf16[720,384]{1,0:T(8,128)(2,1)} %fusion.36.v_ref.refs_2_, ...), custom_call_target="tpu_custom_call" | custom-call | flops 13589544960 | bytes 13271040 | tf_op jit(solution)/shard_map/attn_bwd/pallas_call | solution.py:268
  244.6 8.5 %collective-permute-done.12 = bf16[480,1536]{1,0:T(8,128)(2,1)} collective-permute-done((bf16[480,1536]{1,0:T(8,128)(2,1)}, bf16[480,1536]{1,0:T(8,128)(2,1)}, u32[]{:S(2)}, u32[]{:S(2)}) %collective-permute-start.12) | collective-permute-done | bytes 1474592 | tf_op jit(solution)/shard_map/ppermute | solution.py:388
  258.2 14.8 %collective-permute-done.13 = bf16[240,1536]{1,0:T(8,128)(2,1)S(1)} collective-permute-done((bf16[240,1536]{1,0:T(8,128)(2,1)S(1)}, bf16[240,1536]{1,0:T(8,128)(2,1)S(1)}, u32[]{:S(2)}, u32[]{:S(2)}) %collective-permute-start.13) | collective-permute-done | bytes 737312 | tf_op jit(solution)/shard_map/ppermute | solution.py:388
  274.9 11.5 %table_sums.5 = (f32[2,32,192]{2,1,0:T(8,128)}, f32[12,8,128]{2,1,0:T(8,128)}) custom-call(bf16[6,720,768]{2,1,0:T(8,128)(2,1)} %get-tuple-element.58.refs_0_, bf16[6,720,768]{2,1,0:T(8,128)(2,1)} %get-tuple-element.60.refs_1_, s16[2,720,768]{2,1,0:T(8,128)(2,1)} %get-tuple-element.51.idx_ref.refs_2_, bf16[240,1536]{1,0:T(8,128)(2,1)} %copy-done.25), custom_call_target="tpu_custom_call" | custom-call | flops 9059696640 | bytes 4423680 | tf_op jit(solution)/shard_map/table_sums/pallas_call | solution.py:356
  286.4 2.0 add_convert_fusion.2.refs_3_
  288.6 2.5 collective-permute-start.29
  292.6 8.4 %collective-permute-done.29 = bf16[60,1536]{1,0:T(8,128)(2,1)S(1)} collective-permute-done((bf16[60,1536]{1,0:T(8,128)(2,1)S(1)}, bf16[60,1536]{1,0:T(8,128)(2,1)S(1)}, u32[]{:S(2)}, u32[]{:S(2)}) %collective-permute-start.29) | collective-permute-done | bytes 184352 | tf_op jit(solution)/shard_map/ppermute | solution.py:388
  301.2 11.7 %table_sums.4 = (f32[2,32,192]{2,1,0:T(8,128)}, f32[12,8,128]{2,1,0:T(8,128)}) custom-call(bf16[6,720,768]{2,1,0:T(8,128)(2,1)} %get-tuple-element.58.refs_0_, bf16[6,720,768]{2,1,0:T(8,128)(2,1)} %get-tuple-element.60.refs_1_, s16[2,720,768]{2,1,0:T(8,128)(2,1)} %get-tuple-element.51.idx_ref.refs_2_, bf16[2,384,1152]{2,1,0:T(8,128)(2,1)} %copy-done.17, ...), custom_call_target="tpu_custom_call" | custom-call | flops 9059696640 | bytes 4423680 | tf_op jit(solution)/shard_map/table_sums/pallas_call | solution.py:356
  313.8 3.8 collective-permute-start.31
  317.6 2.3 fusion.32.refs_4_
  319.9 12.0 %table_sums.3 = (f32[2,32,192]{2,1,0:T(8,128)}, f32[12,8,128]{2,1,0:T(8,128)}) custom-call(bf16[6,720,768]{2,1,0:T(8,128)(2,1)} %get-tuple-element.58.refs_0_, bf16[6,720,768]{2,1,0:T(8,128)(2,1)} %get-tuple-element.60.refs_1_, s16[2,720,768]{2,1,0:T(8,128)(2,1)} %get-tuple-element.51.idx_ref.refs_2_, bf16[120,1536]{1,0:T(8,128)(2,1)} %copy-done.37, ...), custom_call_target="tpu_custom_call" | custom-call | flops 9059696640 | bytes 4423680 | tf_op jit(solution)/shard_map/table_sums/pallas_call | solution.py:356
  331.9 2.0 all-reduce.4.cloned.1.call-done
  333.8 2.1 fusion.77
  336.0 2.1 fusion.86
  338.1 2.1 fusion.126
  340.3 2.2 fusion.125
  342.6 2.2 fusion.124
  346.7 2.2 fusion.80
  350.0 6.5 %fusion.26 = f32[1,709,768]{2,1,0:T(8,128)S(1)} fusion(f32[720,768]{1,0:T(8,128)} %fusion.77, f32[720,768]{1,0:T(8,128)} %fusion.86, f32[720,768]{1,0:T(8,128)} %fusion.80, f32[720,768]{1,0:T(8,128)} %fusion.126, f32[720,768]{1,0:T(8,128)} %fusion.125, f32[720,768]{1,0:T(8,128)} %fusion.124, f32[720,768]{1,0:T(8,128)} %get-tuple-element.186), kind=kLoop, calls=%fused_computation.78 | loop fusion | flops 3267072 | bytes 17424384 | tf_op jit(solution)/shard_map/broadcast_in_dim | solution.py:597
  356.5 3.0 collective-permute-start.26
  359.5 3.6 copy.79
  363.3 2.4 collective-permute-start.27
  365.8 1.9 collective-permute-done.27
  367.7 2.1 collective-permute-start.28
  372.9 3.2 collective-permute-done.17
  376.3 2.0 collective-permute-start.18
  379.0 3.6 collective-permute-done.18
  382.6 2.1 collective-permute-start.19
  388.4 2.1 collective-permute-start.20
  391.4 2.7 collective-permute-done.20
  396.2 4.0 collective-permute-done.21
  402.3 2.5 maximum_convert_fusion
  404.9 4.3 collective-permute-done.22
  412.1 2.4 reshape.292
  414.5 2.8 fusion.20
  (322 shorter events, 96.8 us)
Async XLA Ops:
  7.2 10.5 %copy-start = (bf16[768,1536]{1,0:T(8,128)(2,1)S(1)}, bf16[768,1536]{1,0:T(8,128)(2,1)}, u32[]{:S(2)}) copy-start(bf16[768,1536]{1,0:T(8,128)(2,1)} %param.38) | copy-start | bytes 7077892
  7.2 7.7 %copy-start.38 = (bf16[384,768]{1,0:T(8,128)(2,1)S(1)}, bf16[384,768]{1,0:T(8,128)(2,1)}, u32[]{:S(2)}) copy-start(bf16[384,768]{1,0:T(8,128)(2,1)} %param.31) | copy-start | bytes 1769476
  8.8 23.0 %collective-permute-start = (bf16[16,1536]{1,0:T(8,128)(2,1)}, bf16[16,1536]{1,0:T(8,128)(2,1)S(1)}, u32[]{:S(2)}, u32[]{:S(2)}) collective-permute-start(bf16[16,1536]{1,0:T(8,128)(2,1)} %get-tuple-element.50.own_ref.small_ref), channel_id=1, source_target_pairs={{0,1},{1,0},{2,3},{3,2},{4,5},{5,4},{6,7},{7,6},{8,9},{9,8},{10,11... | collective-permute-start | bytes 147464 | tf_op jit(solution)/shard_map/ppermute | solution.py:388
  14.9 44.4 %collective-permute-start.1 = (bf16[3,384,384]{2,1,0:T(8,128)(2,1)}, bf16[3,384,384]{2,1,0:T(8,128)(2,1)}, u32[]{:S(2)}, u32[]{:S(2)}) collective-permute-start(bf16[3,384,384]{2,1,0:T(8,128)(2,1)} %pad_maximum_fusion.8), channel_id=1, source_target_pairs={{0,1},{1,0},{2,3},{3,2},{4,5},{5,4},{6,7},{7,6},{8,9},{9,8},{10,11... | collective-permute-start | bytes 2654216 | tf_op jit(solution)/shard_map/ppermute | solution.py:388
  15.7 10.0 %copy-start.19 = (bf16[1,709,768]{2,1,0:T(8,128)(2,1)S(1)}, bf16[1,709,768]{2,1,0:T(8,128)(2,1)}, u32[]{:S(2)}) copy-start(bf16[1,709,768]{2,1,0:T(8,128)(2,1)} %param.23) | copy-start | bytes 3267076
  15.7 43.5 %collective-permute-start.3 = (bf16[192,768]{1,0:T(8,128)(2,1)}, bf16[192,768]{1,0:T(8,128)(2,1)}, u32[]{:S(2)}, u32[]{:S(2)}) collective-permute-start(bf16[192,768]{1,0:T(8,128)(2,1)} %constant_dynamic-slice_fusion.8), channel_id=1, source_target_pairs={{0,1},{1,0},{2,3},{3,2},{4,5},{5,4},{6,7},{7,6},{8,9},{9,8},{10,11... | collective-permute-start | bytes 884744 | tf_op jit(solution)/shard_map/ppermute | solution.py:388
  18.8 50.6 %collective-permute-start.5 = (bf16[384,1536]{1,0:T(8,128)(2,1)}, bf16[384,1536]{1,0:T(8,128)(2,1)}, u32[]{:S(2)}, u32[]{:S(2)}) collective-permute-start(bf16[384,1536]{1,0:T(8,128)(2,1)} %constant_dynamic-slice_fusion.7), channel_id=1, source_target_pairs={{0,1},{1,0},{2,3},{3,2},{4,5},{5,4},{6,7},{7,6},{8,9},{9,8},{10,11... | collective-permute-start | bytes 3538952 | tf_op jit(solution)/shard_map/ppermute | solution.py:388
  18.8 6.9 %copy-start.43 = (bf16[768,384]{1,0:T(8,128)(2,1)S(1)}, bf16[768,384]{1,0:T(8,128)(2,1)}, u32[]{:S(2)}) copy-start(bf16[768,384]{1,0:T(8,128)(2,1)} %param.28) | copy-start | bytes 1769476
  18.8 8.4 %copy-start.45 = (bf16[768,384]{1,0:T(8,128)(2,1)S(1)}, bf16[768,384]{1,0:T(8,128)(2,1)}, u32[]{:S(2)}) copy-start(bf16[768,384]{1,0:T(8,128)(2,1)} %param.26) | copy-start | bytes 1769476
  21.3 72.0 %collective-permute-start.7 = (bf16[768,768]{1,0:T(8,128)(2,1)}, bf16[768,768]{1,0:T(8,128)(2,1)}, u32[]{:S(2)}, u32[]{:S(2)}) collective-permute-start(bf16[768,768]{1,0:T(8,128)(2,1)} %constant_dynamic-slice_fusion.6), channel_id=1, source_target_pairs={{0,1},{1,0},{2,3},{3,2},{4,5},{5,4},{6,7},{7,6},{8,9},{9,8},{10,11... | collective-permute-start | bytes 3538952 | tf_op jit(solution)/shard_map/ppermute | solution.py:388
  59.2 2.1 collective-permute-start.4
  59.3 33.9 %collective-permute-start.2 = (bf16[3,384,384]{2,1,0:T(8,128)(2,1)}, bf16[3,384,384]{2,1,0:T(8,128)(2,1)S(1)}, u32[]{:S(2)}, u32[]{:S(2)}) collective-permute-start(bf16[3,384,384]{2,1,0:T(8,128)(2,1)} %collective-permute-done.1), channel_id=1, source_target_pairs={{0,2},{2,0},{1,3},{3,1},{4,6},{6,4},{5,7},{7,5},{8,10},{10,8},{9,1... | collective-permute-start | bytes 2654216 | tf_op jit(solution)/shard_map/ppermute | solution.py:388
  62.3 55.6 %copy-start.48 = (bf16[192,768]{1,0:T(8,128)(2,1)}, bf16[192,768]{1,0:T(8,128)(2,1)S(1)}, u32[]{:S(2)}) copy-start(bf16[192,768]{1,0:T(8,128)(2,1)S(1)} %get-tuple-element.209) | copy-start | bytes 884740
  62.3 55.6 %copy-start.49 = (bf16[192,768]{1,0:T(8,128)(2,1)}, bf16[192,768]{1,0:T(8,128)(2,1)S(1)}, u32[]{:S(2)}) copy-start(bf16[192,768]{1,0:T(8,128)(2,1)S(1)} %get-tuple-element.210) | copy-start | bytes 884740
  69.4 56.5 %collective-permute-start.6 = (bf16[384,1536]{1,0:T(8,128)(2,1)}, bf16[384,1536]{1,0:T(8,128)(2,1)S(1)}, u32[]{:S(2)}, u32[]{:S(2)}) collective-permute-start(bf16[384,1536]{1,0:T(8,128)(2,1)} %collective-permute-done.5), channel_id=1, source_target_pairs={{0,2},{2,0},{1,3},{3,1},{4,6},{6,4},{5,7},{7,5},{8,10},{10,8},{9,1... | collective-permute-start | bytes 3538952 | tf_op jit(solution)/shard_map/ppermute | solution.py:388
  93.2 37.2 %collective-permute-start.8 = (bf16[768,768]{1,0:T(8,128)(2,1)}, bf16[768,768]{1,0:T(8,128)(2,1)S(1)}, u32[]{:S(2)}, u32[]{:S(2)}) collective-permute-start(bf16[768,768]{1,0:T(8,128)(2,1)} %collective-permute-done.7), channel_id=1, source_target_pairs={{0,2},{2,0},{1,3},{3,1},{4,6},{6,4},{5,7},{7,5},{8,10},{10,8},{9,1... | collective-permute-start | bytes 3538952 | tf_op jit(solution)/shard_map/ppermute | solution.py:388
  136.6 17.0 %copy-start.8 = (f32[720,768]{1,0:T(8,128)}, f32[720,768]{1,0:T(8,128)S(1)}, u32[]{:S(2)}) copy-start(f32[720,768]{1,0:T(8,128)S(1)} %get-tuple-element.187) | copy-start | bytes 6635524
  167.7 5.8 %copy-start.12 = (bf16[1,1536,768]{2,1,0:T(8,128)(2,1)}, bf16[1,1536,768]{2,1,0:T(8,128)(2,1)S(1)}, u32[]{:S(2)}) copy-start(bf16[1,1536,768]{2,1,0:T(8,128)(2,1)S(1)} %fusion.13) | copy-start | bytes 7077892
  173.5 3.6 copy-start.27
  176.5 12.2 %collective-permute-start.10 = (bf16[2,768,768]{2,1,0:T(8,128)(2,1)}, bf16[2,768,768]{2,1,0:T(8,128)(2,1)}, u32[]{:S(2)}, u32[]{:S(2)}) collective-permute-start(bf16[2,768,768]{2,1,0:T(8,128)(2,1)} %fusion.18), channel_id=1, source_target_pairs={{0,2},{2,0},{1,3},{3,1},{4,6},{6,4},{5,7},{7,5},{8,10},{10,8},{9,1... | collective-permute-start | bytes 7077896 | tf_op jit(solution)/shard_map/ppermute | solution.py:388
  181.0 5.0 %copy-start.40 = (bf16[384,768]{1,0:T(8,128)(2,1)S(1)}, bf16[384,768]{1,0:T(8,128)(2,1)}, u32[]{:S(2)}) copy-start(bf16[384,768]{1,0:T(8,128)(2,1)} %param.31) | copy-start | bytes 1769476
  181.0 12.6 %collective-permute-start.9 = (bf16[2,480,1536]{2,1,0:T(8,128)(2,1)}, bf16[2,480,1536]{2,1,0:T(8,128)(2,1)}, u32[]{:S(2)}, u32[]{:S(2)}) collective-permute-start(bf16[2,480,1536]{2,1,0:T(8,128)(2,1)} %fusion.15), channel_id=1, source_target_pairs={{0,2},{2,0},{1,3},{3,1},{4,6},{6,4},{5,7},{7,5},{8,10},{10,8},{9,1... | collective-permute-start | bytes 8847368 | tf_op jit(solution)/shard_map/ppermute | solution.py:388
  181.5 4.5 %copy-start.51 = (bf16[720,768]{1,0:T(8,128)(2,1)S(1)}, bf16[720,768]{1,0:T(8,128)(2,1)}, u32[]{:S(2)}) copy-start(bf16[720,768]{1,0:T(8,128)(2,1)} %copy-done.50) | copy-start | bytes 3317764
  182.9 4.7 %copy-start.9 = (f32[720,768]{1,0:T(8,128)S(1)}, f32[720,768]{1,0:T(8,128)}, u32[]{:S(2)}) copy-start(f32[720,768]{1,0:T(8,128)} %copy-done.8) | copy-start | bytes 6635524
  182.9 4.7 %copy-start.67 = (f32[768]{0:T(1024)S(1)}, f32[768]{0:T(1024)}, u32[]{:S(2)}) copy-start(f32[768]{0:T(1024)} %get-tuple-element.173) | copy-start | bytes 9220
  189.6 3.9 copy-start.3
  192.0 4.1 copy-start.15
  193.2 29.0 %collective-permute-start.11 = (bf16[768,768]{1,0:T(8,128)(2,1)}, bf16[768,768]{1,0:T(8,128)(2,1)S(1)}, u32[]{:S(2)}, u32[]{:S(2)}) collective-permute-start(bf16[768,768]{1,0:T(8,128)(2,1)} %slice_bitcast_fusion.2), channel_id=1, source_target_pairs={{0,1},{1,0},{2,3},{3,2},{4,5},{5,4},{6,7},{7,6},{8,9},{9,8},{10,11... | collective-permute-start | bytes 3538952 | tf_op jit(solution)/shard_map/ppermute | solution.py:388
  197.4 55.6 %collective-permute-start.12 = (bf16[480,1536]{1,0:T(8,128)(2,1)}, bf16[480,1536]{1,0:T(8,128)(2,1)}, u32[]{:S(2)}, u32[]{:S(2)}) collective-permute-start(bf16[480,1536]{1,0:T(8,128)(2,1)} %slice_bitcast_fusion), channel_id=1, source_target_pairs={{0,1},{1,0},{2,3},{3,2},{4,5},{5,4},{6,7},{7,6},{8,9},{9,8},{10,11... | collective-permute-start | bytes 4423688 | tf_op jit(solution)/shard_map/ppermute | solution.py:388
  199.2 18.5 %copy-start.20 = (bf16[1,709,768]{2,1,0:T(8,128)(2,1)S(1)}, bf16[1,709,768]{2,1,0:T(8,128)(2,1)}, u32[]{:S(2)}) copy-start(bf16[1,709,768]{2,1,0:T(8,128)(2,1)} %param.23) | copy-start | bytes 3267076
  215.2 4.3 %copy-start.32 = (bf16[720,384]{1,0:T(8,128)(2,1)S(1)}, bf16[720,384]{1,0:T(8,128)(2,1)}, u32[]{:S(2)}) copy-start(bf16[720,384]{1,0:T(8,128)(2,1)} %get-tuple-element.68) | copy-start | bytes 1658884
  240.2 93.7 %all-reduce.4.cloned.1.call-start = ((), (), s32[]{:S(2)}) async-start(), calls=%async_computation | async-start | bytes 2359296 | tf_op jit(solution)/shard_map/psum | solution.py:586
  243.6 9.5 %copy-start.11 = (bf16[2,480,1536]{2,1,0:T(8,128)(2,1)S(1)}, bf16[2,480,1536]{2,1,0:T(8,128)(2,1)}, u32[]{:S(2)}) copy-start(bf16[2,480,1536]{2,1,0:T(8,128)(2,1)} %copy-done.10) | copy-start | bytes 8847364
  254.8 18.3 %copy-start.18 = (bf16[480,1536]{1,0:T(8,128)(2,1)}, bf16[480,1536]{1,0:T(8,128)(2,1)S(1)}, u32[]{:S(2)}) copy-start(bf16[480,1536]{1,0:T(8,128)(2,1)S(1)} %fusion.17.refs_4_) | copy-start | bytes 4423684
  254.9 18.2 %collective-permute-start.13 = (bf16[240,1536]{1,0:T(8,128)(2,1)S(1)}, bf16[240,1536]{1,0:T(8,128)(2,1)S(1)}, u32[]{:S(2)}, u32[]{:S(2)}) collective-permute-start(bf16[240,1536]{1,0:T(8,128)(2,1)S(1)} %constant_dynamic-slice_fusion.5), channel_id=1, source_target_pairs={{0,4},{4,0},{8,12},{12,8},{16,20},{20,16},{24,28},{28,24},{1,5},{5... | collective-permute-start | bytes 2211848 | tf_op jit(solution)/shard_map/ppermute | solution.py:388
  258.0 28.4 %collective-permute-start.15 = (bf16[2,384,1152]{2,1,0:T(8,128)(2,1)}, bf16[2,384,1152]{2,1,0:T(8,128)(2,1)}, u32[]{:S(2)}, u32[]{:S(2)}) collective-permute-start(bf16[2,384,1152]{2,1,0:T(8,128)(2,1)} %fusion.30), channel_id=1, source_target_pairs={{0,2},{2,0},{1,3},{3,1},{4,6},{6,4},{5,7},{7,5},{8,10},{10,8},{9,1... | collective-permute-start | bytes 5308424 | tf_op jit(solution)/shard_map/ppermute | solution.py:388
  273.3 15.1 %collective-permute-start.14 = (bf16[120,1536]{1,0:T(8,128)(2,1)S(1)}, bf16[120,1536]{1,0:T(8,128)(2,1)S(1)}, u32[]{:S(2)}, u32[]{:S(2)}) collective-permute-start(bf16[120,1536]{1,0:T(8,128)(2,1)S(1)} %constant_dynamic-slice_fusion.4), channel_id=1, source_target_pairs={{0,8},{4,12},{8,0},{12,4},{16,24},{20,28},{24,16},{28,20},{1,9},{5... | collective-permute-start | bytes 1105928 | tf_op jit(solution)/shard_map/ppermute | solution.py:388
  288.3 12.8 %copy-start.17 = (bf16[2,384,1152]{2,1,0:T(8,128)(2,1)}, bf16[2,384,1152]{2,1,0:T(8,128)(2,1)S(1)}, u32[]{:S(2)}) copy-start(bf16[2,384,1152]{2,1,0:T(8,128)(2,1)S(1)} %add_convert_fusion.2.refs_3_) | copy-start | bytes 5308420
  288.5 24.4 %copy-start.37 = (bf16[120,1536]{1,0:T(8,128)(2,1)}, bf16[120,1536]{1,0:T(8,128)(2,1)S(1)}, u32[]{:S(2)}) copy-start(bf16[120,1536]{1,0:T(8,128)(2,1)S(1)} %add_convert_fusion.6.refs_3_) | copy-start | bytes 1105924
  288.6 12.5 %collective-permute-start.29 = (bf16[60,1536]{1,0:T(8,128)(2,1)S(1)}, bf16[60,1536]{1,0:T(8,128)(2,1)S(1)}, u32[]{:S(2)}, u32[]{:S(2)}) collective-permute-start(bf16[60,1536]{1,0:T(8,128)(2,1)S(1)} %constant_dynamic-slice_fusion), channel_id=1, source_target_pairs={{0,16},{4,20},{8,24},{12,28},{16,0},{20,4},{24,8},{28,12},{1,17},{... | collective-permute-start | bytes 552968 | tf_op jit(solution)/shard_map/ppermute | solution.py:388
  291.1 26.5 %collective-permute-start.16 = (bf16[384,1152]{1,0:T(8,128)(2,1)S(1)}, bf16[384,1152]{1,0:T(8,128)(2,1)S(1)}, u32[]{:S(2)}, u32[]{:S(2)}) collective-permute-start(bf16[384,1152]{1,0:T(8,128)(2,1)S(1)} %slice_bitcast_fusion.4), channel_id=1, source_target_pairs={{0,1},{1,0},{2,3},{3,2},{4,5},{5,4},{6,7},{7,6},{8,9},{9,8},{10,11... | collective-permute-start | bytes 2654216 | tf_op jit(solution)/shard_map/ppermute | solution.py:388
  301.1 11.8 %collective-permute-start.30 = (bf16[60,1536]{1,0:T(8,128)(2,1)S(1)}, bf16[60,1536]{1,0:T(8,128)(2,1)S(1)}, u32[]{:S(2)}, u32[]{:S(2)}) collective-permute-start(bf16[60,1536]{1,0:T(8,128)(2,1)S(1)} %add_convert_fusion.8), channel_id=1, source_target_pairs={{0,16},{4,20},{8,24},{12,28},{16,0},{20,4},{24,8},{28,12},{1,17},{... | collective-permute-start | bytes 552968 | tf_op jit(solution)/shard_map/ppermute | solution.py:388
  313.8 51.9 %collective-permute-start.31 = (bf16[120,1536]{1,0:T(8,128)(2,1)}, bf16[120,1536]{1,0:T(8,128)(2,1)S(1)}, u32[]{:S(2)}, u32[]{:S(2)}) collective-permute-start(bf16[120,1536]{1,0:T(8,128)(2,1)} %pad_maximum_fusion.16), channel_id=1, source_target_pairs={{0,8},{4,12},{8,0},{12,4},{16,24},{20,28},{24,16},{28,20},{1,9},{5... | collective-permute-start | bytes 1105928 | tf_op jit(solution)/shard_map/ppermute | solution.py:388
  319.9 14.0 %copy-start.5 = (bf16[3,384,384]{2,1,0:T(8,128)(2,1)S(1)}, bf16[3,384,384]{2,1,0:T(8,128)(2,1)}, u32[]{:S(2)}) copy-start(bf16[3,384,384]{2,1,0:T(8,128)(2,1)} %copy-done.4) | copy-start | bytes 2654212
  319.9 14.0 %copy-start.7 = (bf16[3,384,384]{2,1,0:T(8,128)(2,1)S(1)}, bf16[3,384,384]{2,1,0:T(8,128)(2,1)}, u32[]{:S(2)}) copy-start(bf16[3,384,384]{2,1,0:T(8,128)(2,1)} %copy-done.6) | copy-start | bytes 2654212
  319.9 14.0 %copy-start.36 = (bf16[720,384]{1,0:T(8,128)(2,1)S(1)}, bf16[720,384]{1,0:T(8,128)(2,1)}, u32[]{:S(2)}) copy-start(bf16[720,384]{1,0:T(8,128)(2,1)} %get-tuple-element.73) | copy-start | bytes 1658884
  342.5 4.2 copy-start.31
  345.9 4.0 collective-permute-start.24
  349.9 6.5 %collective-permute-start.25 = (f32[7872]{0:T(1024)S(1)}, f32[7872]{0:T(1024)S(1)}, u32[]{:S(2)}, u32[]{:S(2)}) collective-permute-start(f32[7872]{0:T(1024)S(1)} %add.528), channel_id=1, source_target_pairs={{0,2},{2,0},{1,3},{3,1},{4,6},{6,4},{5,7},{7,5},{8,10},{10,8},{9,1... | collective-permute-start | bytes 94472 | tf_op jit(solution)/shard_map/ppermute | solution.py:388
  349.9 9.5 %copy-start.24 = (bf16[384,1152]{1,0:T(8,128)(2,1)S(1)}, bf16[384,1152]{1,0:T(8,128)(2,1)}, u32[]{:S(2)}) copy-start(bf16[384,1152]{1,0:T(8,128)(2,1)} %fusion.32.refs_4_) | copy-start | bytes 2654212
  356.5 6.9 %collective-permute-start.26 = (f32[7872]{0:T(1024)S(1)}, f32[7872]{0:T(1024)S(1)}, u32[]{:S(2)}, u32[]{:S(2)}) collective-permute-start(f32[7872]{0:T(1024)S(1)} %add.529), channel_id=1, source_target_pairs={{0,4},{4,0},{8,12},{12,8},{16,20},{20,16},{24,28},{28,24},{1,5},{5... | collective-permute-start | bytes 94472 | tf_op jit(solution)/shard_map/ppermute | solution.py:388
  359.5 3.6 copy-start.47
  363.1 13.0 %collective-permute-start.17 = (bf16[192,1152]{1,0:T(8,128)(2,1)S(1)}, bf16[192,1152]{1,0:T(8,128)(2,1)S(1)}, u32[]{:S(2)}, u32[]{:S(2)}) collective-permute-start(bf16[192,1152]{1,0:T(8,128)(2,1)S(1)} %constant_dynamic-slice_fusion.3), channel_id=1, source_target_pairs={{0,4},{4,0},{8,12},{12,8},{16,20},{20,16},{24,28},{28,24},{1,5},{5... | collective-permute-start | bytes 1327112 | tf_op jit(solution)/shard_map/ppermute | solution.py:388
  363.1 37.8 %collective-permute-start.34 = (bf16[768,768]{1,0:T(8,128)(2,1)S(1)}, bf16[768,768]{1,0:T(8,128)(2,1)}, u32[]{:S(2)}, u32[]{:S(2)}) collective-permute-start(bf16[768,768]{1,0:T(8,128)(2,1)S(1)} %copy-done.47), channel_id=1, source_target_pairs={{0,2},{2,0},{1,3},{3,1},{4,6},{6,4},{5,7},{7,5},{8,10},{10,8},{9,1... | collective-permute-start | bytes 3538952 | tf_op jit(solution)/shard_map/ppermute | solution.py:388
  363.3 4.4 %collective-permute-start.27 = (f32[7872]{0:T(1024)S(1)}, f32[7872]{0:T(1024)S(1)}, u32[]{:S(2)}, u32[]{:S(2)}) collective-permute-start(f32[7872]{0:T(1024)S(1)} %add.530), channel_id=1, source_target_pairs={{0,8},{4,12},{8,0},{12,4},{16,24},{20,28},{24,16},{28,20},{1,9},{5... | collective-permute-start | bytes 94472 | tf_op jit(solution)/shard_map/ppermute | solution.py:388
  367.7 5.1 %collective-permute-start.28 = (f32[7872]{0:T(1024)S(1)}, f32[7872]{0:T(1024)S(1)}, u32[]{:S(2)}, u32[]{:S(2)}) collective-permute-start(f32[7872]{0:T(1024)S(1)} %add.531), channel_id=1, source_target_pairs={{0,16},{4,20},{8,24},{12,28},{16,0},{20,4},{24,8},{28,12},{1,17},{... | collective-permute-start | bytes 94472 | tf_op jit(solution)/shard_map/ppermute | solution.py:388
  370.8 20.4 %collective-permute-start.32 = (bf16[240,1536]{1,0:T(8,128)(2,1)}, bf16[240,1536]{1,0:T(8,128)(2,1)S(1)}, u32[]{:S(2)}, u32[]{:S(2)}) collective-permute-start(bf16[240,1536]{1,0:T(8,128)(2,1)} %pad_maximum_fusion.10), channel_id=1, source_target_pairs={{0,4},{4,0},{8,12},{12,8},{16,20},{20,16},{24,28},{28,24},{1,5},{5... | collective-permute-start | bytes 2211848 | tf_op jit(solution)/shard_map/ppermute | solution.py:388
  376.3 6.3 %collective-permute-start.18 = (bf16[96,1152]{1,0:T(8,128)(2,1)S(1)}, bf16[96,1152]{1,0:T(8,128)(2,1)S(1)}, u32[]{:S(2)}, u32[]{:S(2)}) collective-permute-start(bf16[96,1152]{1,0:T(8,128)(2,1)S(1)} %constant_dynamic-slice_fusion.2), channel_id=1, source_target_pairs={{0,8},{4,12},{8,0},{12,4},{16,24},{20,28},{24,16},{28,20},{1,9},{5... | collective-permute-start | bytes 663560 | tf_op jit(solution)/shard_map/ppermute | solution.py:388
  382.6 5.7 %collective-permute-start.19 = (bf16[48,1152]{1,0:T(8,128)(2,1)S(1)}, bf16[48,1152]{1,0:T(8,128)(2,1)S(1)}, u32[]{:S(2)}, u32[]{:S(2)}) collective-permute-start(bf16[48,1152]{1,0:T(8,128)(2,1)S(1)} %constant_dynamic-slice_fusion.1), channel_id=1, source_target_pairs={{0,16},{4,20},{8,24},{12,28},{16,0},{20,4},{24,8},{28,12},{1,17},{... | collective-permute-start | bytes 331784 | tf_op jit(solution)/shard_map/ppermute | solution.py:388
  388.4 5.7 %collective-permute-start.20 = (bf16[48,1152]{1,0:T(8,128)(2,1)S(1)}, bf16[48,1152]{1,0:T(8,128)(2,1)S(1)}, u32[]{:S(2)}, u32[]{:S(2)}) collective-permute-start(bf16[48,1152]{1,0:T(8,128)(2,1)S(1)} %add_convert_fusion.9), channel_id=1, source_target_pairs={{0,16},{4,20},{8,24},{12,28},{16,0},{20,4},{24,8},{28,12},{1,17},{... | collective-permute-start | bytes 331784 | tf_op jit(solution)/shard_map/ppermute | solution.py:388
  394.1 6.0 %collective-permute-start.21 = (bf16[96,1152]{1,0:T(8,128)(2,1)S(1)}, bf16[96,1152]{1,0:T(8,128)(2,1)S(1)}, u32[]{:S(2)}, u32[]{:S(2)}) collective-permute-start(bf16[96,1152]{1,0:T(8,128)(2,1)S(1)} %pad_maximum_fusion.17), channel_id=1, source_target_pairs={{0,8},{4,12},{8,0},{12,4},{16,24},{20,28},{24,16},{28,20},{1,9},{5... | collective-permute-start | bytes 663560 | tf_op jit(solution)/shard_map/ppermute | solution.py:388
  396.1 14.3 %collective-permute-start.33 = (bf16[480,1536]{1,0:T(8,128)(2,1)S(1)}, bf16[480,1536]{1,0:T(8,128)(2,1)S(1)}, u32[]{:S(2)}, u32[]{:S(2)}) collective-permute-start(bf16[480,1536]{1,0:T(8,128)(2,1)S(1)} %pad_maximum_fusion.7), channel_id=1, source_target_pairs={{0,2},{2,0},{1,3},{3,1},{4,6},{6,4},{5,7},{7,5},{8,10},{10,8},{9,1... | collective-permute-start | bytes 4423688 | tf_op jit(solution)/shard_map/ppermute | solution.py:388
  400.3 8.9 %collective-permute-start.22 = (bf16[192,1152]{1,0:T(8,128)(2,1)S(1)}, bf16[192,1152]{1,0:T(8,128)(2,1)S(1)}, u32[]{:S(2)}, u32[]{:S(2)}) collective-permute-start(bf16[192,1152]{1,0:T(8,128)(2,1)S(1)} %pad_maximum_fusion.13), channel_id=1, source_target_pairs={{0,4},{4,0},{8,12},{12,8},{16,20},{20,16},{24,28},{28,24},{1,5},{5... | collective-permute-start | bytes 1327112 | tf_op jit(solution)/shard_map/ppermute | solution.py:388
  410.4 7.0 %collective-permute-start.23 = (bf16[384,1152]{1,0:T(8,128)(2,1)}, bf16[384,1152]{1,0:T(8,128)(2,1)}, u32[]{:S(2)}, u32[]{:S(2)}) collective-permute-start(bf16[384,1152]{1,0:T(8,128)(2,1)} %pad_maximum_fusion.9), channel_id=1, source_target_pairs={{0,2},{2,0},{1,3},{3,1},{4,6},{6,4},{5,7},{7,5},{8,10},{10,8},{9,1... | collective-permute-start | bytes 2654216 | tf_op jit(solution)/shard_map/ppermute | solution.py:388
  (45 other events, 103.0 us)
Sparse Core Ops, SparseCore 0:
  245.1 88.7 all-reduce.3

commit v3 on v2

--- a/solution.py
+++ b/solution.py
@@ -22,6 +22,9 @@
 PT = 256
 NT = (((1,), (1,)), ((), ()))
 VM = 56 << 20
+
+BRIEF = pl.CostEstimate(flops=10_000_000_000, bytes_accessed=1, transcendentals=0)
+
 
 def bucket_edges(buckets, farthest):
     exact=buckets//4
@@ -98,6 +101,7 @@
         scratch_shapes=[pltpu.VMEM((8, lanes), f32), pltpu.VMEM((lanes, 8), f32)],
         compiler_params=pltpu.CompilerParams(vmem_limit_bytes=VM),
         name="buckets",
+        cost_estimate=BRIEF,
     )(length, box, own, oth)
 
 
@@ -125,6 +129,7 @@
         in_specs=[VMEM] * 12,
         out_specs=(VMEM,) * 2,
         name="pack",
+        cost_estimate=BRIEF,
     )(*split, *copied)
 
 
@@ -187,29 +192,30 @@
         o=[jnp.dot(vt[h*64:(h+1)*64],p_ref[2*hp+h],preferred_element_type=f32) for h in range(2)]
         ctx_ref[:,hs]=jnp.concatenate(o,0).T.astype(bf)
 
-def attn_fwd(q, k, v, idx, toep, small):
-    rows, W = q.shape
+def attn_fwd(q, k, v, W, idx, toep, small, after=()):
+    rows = q[0].shape[0]
     H = W // HEAD_DIM
     lanes = idx.shape[2]
     whole = lambda shape: pl.BlockSpec(shape, lambda i: (0,) * len(shape))
+    column = lambda at: pl.BlockSpec((rows, W), lambda i: (0, at))
     return pl.pallas_call(
-        fwd_kernel,
+        partial(skip_refs, fwd_kernel, 6, len(after)),
         grid=(lanes // PT,),
-        in_specs=[pl.BlockSpec((PT, W), lambda i: (i, 0)), whole((rows, W)), whole((rows, W)), pl.BlockSpec((2, rows, PT), lambda i: (0, 0, i)), whole(toep.shape), whole(small.shape)],
+        in_specs=[pl.BlockSpec((PT, W), lambda i: (i, q[1])), column(k[1]), column(v[1]), pl.BlockSpec((2, rows, PT), lambda i: (0, 0, i)), whole(toep.shape), whole(small.shape)] + [ANY] * len(after),
         out_specs=(pl.BlockSpec((PT, W), lambda i: (i, 0)), pl.BlockSpec((H, rows, PT), lambda i: (0, 0, i))),
         out_shape=(jax.ShapeDtypeStruct((rows, W), bf), jax.ShapeDtypeStruct((H, rows, lanes), bf)),
         scratch_shapes=[pltpu.VMEM((H, rows, PT), f32)],
         compiler_params=pltpu.CompilerParams(vmem_limit_bytes=VM),
         name="attn_fwd",
-        cost_estimate=pl.CostEstimate(flops=H * rows * lanes * 4096, bytes_accessed=H * rows * lanes * 2, transcendentals=H * rows * lanes),
-    )(q, k, v, idx, toep, small)
+        cost_estimate=BRIEF,
+    )(q[0], k[0], v[0], idx, toep, small, *after)
 
 
 def skip_refs(kernel, first, count, *refs):
     kernel(*refs[:first], *refs[first + count:])
 
 
-def bwd_kernel(q_ref,k_ref,v_ref,do_ref,p_ref,dq_ref,dk_ref,dv_ref,gs_ref,dp_ref,dka,dva):
+def bwd_kernel(q_ref, k_ref, v_ref, do_ref, p_ref, out_ref, gs_ref, dp_ref, dka, dva):
     H,rows,PT=p_ref.shape
     nch=PT//128
     tile=pl.program_id(0); last=pl.num_programs(0)-1
@@ -247,35 +253,82 @@
         hs=slice(hp*128,(hp+1)*128)
         kt=k_ref[:,hs].T
         o=[jnp.dot(kt[h*64:(h+1)*64],gs_ref[2*hp+h],preferred_element_type=f32) for h in range(2)]
-        dq_ref[:,hs]=(jnp.concatenate(o,0)*scale).T.astype(bf)
+        dq=(jnp.concatenate(o,0)*scale).T.astype(bf)
+        @pl.when(tile<last)
+        def _():
+            out_ref[pl.ds(pl.multiple_of(tile*PT,PT),PT),hs]=dq
+        @pl.when(tile==last)
+        def _():
+            left=rows-rows//PT*PT if rows%PT else PT
+            out_ref[rows-left:,hs]=dq[:left]
         qm=split(keep_rows(q_ref[:,hs],tile*PT,rows))
         dm=split(keep_rows(do_ref[:,hs],tile*PT,rows))
         dka[:,hs]+=jnp.dot(gs_ref[2*hp],qm[0],preferred_element_type=f32)+jnp.dot(gs_ref[2*hp+1],qm[1],preferred_element_type=f32)
         dva[:,hs]+=jnp.dot(p_ref[2*hp],dm[0],preferred_element_type=f32)+jnp.dot(p_ref[2*hp+1],dm[1],preferred_element_type=f32)
     @pl.when(tile==last)
     def _():
-        dk_ref[...]=(dka[...]*scale).astype(bf)
-        dv_ref[...]=dva[...].astype(bf)
-
-def attn_bwd(q, k, v, do, p, after=()):
-    rows, W = q.shape
+        W=dka.shape[1]
+        out_ref[:,W:2*W]=(dka[...]*scale).astype(bf)
+        out_ref[:,2*W:]=dva[...].astype(bf)
+
+def attn_bwd(q, k, v, W, do, p, after=()):
+    rows = do.shape[0]
     H = W // HEAD_DIM
     lanes = p.shape[2]
-    tilew = pl.BlockSpec((PT, W), lambda i: (i, 0))
-    whole = pl.BlockSpec((rows, W), lambda i: (0, 0))
+    column = lambda at: pl.BlockSpec((rows, W), lambda i: (0, at))
     big = pl.BlockSpec((H, rows, PT), lambda i: (0, 0, i))
-    o = jax.ShapeDtypeStruct((rows, W), bf)
     return pl.pallas_call(
         partial(skip_refs, bwd_kernel, 5, len(after)),
         grid=(lanes // PT,),
-        in_specs=[tilew, whole, whole, tilew, big] + [ANY] * len(after),
-        out_specs=(tilew, whole, whole, big),
-        out_shape=(o, o, o, jax.ShapeDtypeStruct((H, rows, lanes), bf)),
+        in_specs=[pl.BlockSpec((PT, W), lambda i: (i, q[1])), column(k[1]), column(v[1]), pl.BlockSpec((PT, W), lambda i: (i, 0)), big] + [ANY] * len(after),
+        out_specs=(pl.BlockSpec((rows, 3 * W), lambda i: (0, 0)), big),
+        out_shape=(jax.ShapeDtypeStruct((rows, 3 * W), bf), jax.ShapeDtypeStruct((H, rows, lanes), bf)),
         scratch_shapes=[pltpu.VMEM((H, rows, PT), f32), pltpu.VMEM((rows, W), f32), pltpu.VMEM((rows, W), f32)],
         compiler_params=pltpu.CompilerParams(vmem_limit_bytes=VM),
         name="attn_bwd",
-        cost_estimate=pl.CostEstimate(flops=H * rows * lanes * 4096, bytes_accessed=H * rows * lanes * 4, transcendentals=0),
-    )(q, k, v, do, p, *after)
+        cost_estimate=BRIEF,
+    )(q[0], k[0], v[0], do, p, *after)
+
+
+def finish_kernel(info_ref, mine_ref, theirs_ref, *refs, block, widths, turned):
+    rows = mine_ref.shape[0]
+    count = rows // block
+    n = len(widths)
+    outs, wide, sems = refs[:n], refs[n:2 * n], refs[2 * n]
+    copies = []
+    for p, src in enumerate((mine_ref, theirs_ref)):
+        for j in range(count):
+            rs = slice(j * block, (j + 1) * block)
+            place = pl.multiple_of((jnp.bitwise_xor(info_ref[0], p) * count + jnp.bitwise_xor(info_ref[1], j)) * block, block)
+            at = 0
+            for i in range(n):
+                part = src[rs, at:at + widths[i]].astype(f32)
+                at += widths[i]
+                if turned[i]:
+                    wide[i][p, :, rs] = part.T
+                    copy = pltpu.make_async_copy(wide[i].at[p, :, rs], outs[i].at[:, pl.ds(place, block)], sems.at[p, j, i])
+                else:
+                    wide[i][p, rs, :] = part
+                    copy = pltpu.make_async_copy(wide[i].at[p, rs, :], outs[i].at[pl.ds(place, block), :], sems.at[p, j, i])
+                copy.start()
+                copies.append(copy)
+    for copy in copies:
+        copy.wait()
+
+
+def finish(mine, theirs, core, base, block, widths, turned):
+    rows = mine.shape[0]
+    return pl.pallas_call(
+        partial(finish_kernel, block=block, widths=widths, turned=turned),
+        in_specs=[SMEM, VMEM, VMEM],
+        out_specs=[ANY] * len(widths),
+        out_shape=[jax.ShapeDtypeStruct((w, 2 * rows) if t else (2 * rows, w), f32) for w, t in zip(widths, turned)],
+        scratch_shapes=[pltpu.VMEM((2, w, rows) if t else (2, rows, w), f32) for w, t in zip(widths, turned)]
+        + [pltpu.SemaphoreType.DMA((2, rows // block, len(widths)))],
+        compiler_params=pltpu.CompilerParams(vmem_limit_bytes=VM),
+        name="finish",
+        cost_estimate=BRIEF,
+    )(jnp.stack([core, base]).astype(jnp.int32), mine, theirs)
 
 
 def hist_kernel(gs_ref, go_ref, idx_ref, out_ref, toep_ref, acc, accT, *, part):
@@ -346,11 +399,9 @@
             toep_ref[h, 7:8, :] = jnp.sum(accT[h, 512:640, :], axis=0, keepdims=True)
 
 
-def hist(gs, go, idx, part, parts, after=()):
+def hist(gs, go, idx, part, steps, after=()):
     H, rows, lanes = gs.shape
     SB = 48
-    steps = rows // SB // parts
-    part = part * steps
     near = BUCKETS_2D // 2
     big = pl.BlockSpec((H, SB, lanes), lambda i: (0, part + i, 0))
     return pl.pallas_call(
@@ -362,26 +413,110 @@
         scratch_shapes=[pltpu.VMEM((2, 8 * near, 2 * H * 16), f32), pltpu.VMEM((2 * H, 640, 128), f32)],
         compiler_params=pltpu.CompilerParams(vmem_limit_bytes=VM),
         name="table_sums",
-        cost_estimate=pl.CostEstimate(flops=steps * SB * 128 * lanes * 2 * H * 32, bytes_accessed=4 * H * steps * SB * lanes, transcendentals=0),
+        cost_estimate=BRIEF,
     )(gs, go, idx, *after)
 
 
-def tables_of(sums):
-    out = sum(s[0] for s in sums)
-    toep = sum(s[1] for s in sums)
-    heads = toep.shape[0]
-    xy = out.reshape(2, BUCKETS_2D // 2, heads, 2, 8).sum(4).transpose(0, 2, 3, 1)
-    xy = jnp.concatenate([xy[:, :, 0] - xy[:, :, 1], xy[:, :, 1]], 2)
-    line = toep.reshape(heads, 1024)
-    base = jnp.array([-128, 0, 0, 128, 128, 256, -MAX_DIST - 128, MAX_DIST + 256])
-    d = (base[:, None] - jnp.arange(128)).reshape(1024)
-    b = jnp.zeros_like(d)
-    for e in bucket_edges(BUCKETS, MAX_DIST):
-        b = b + (jnp.abs(d) >= e)
-    b = b + (d > 0) * (BUCKETS // 2)
-    seq = jnp.dot(line, (b[:, None] == jnp.arange(BUCKETS)).astype(f32), precision=lax.Precision.HIGHEST)
-    return seq, xy[0], xy[1]
-
+def tables_kernel(*refs, parts):
+    sums = refs[:2 * parts]
+    dqkv, dqkv_o, up, up_o = refs[2 * parts:2 * parts + 4]
+    shared = refs[2 * parts + 4:-1]
+    out_ref = refs[-1]
+    out = sums[0][...]
+    toep = sums[1][...]
+    for i in range(1, parts):
+        out = out + sums[2 * i][...]
+        toep = toep + sums[2 * i + 1][...]
+    both, rows_out, lanes_out = out_ref.shape
+    heads = toep.shape[0] // both
+    near = out.shape[1]
+    width = dqkv.shape[1] // 3
+    out_ref[...] = jnp.zeros_like(out_ref)
+    for o, (d, u) in enumerate(((dqkv, up), (dqkv_o, up_o))):
+        out_ref[o, 0:1, 0:u.shape[0]] = u[...][None]
+        for at in (0, 2 * width):
+            out_ref[o, 1:2, at:at + width] = jnp.sum(d[:, at:at + width].astype(f32), axis=0, keepdims=True)
+        for i, v in enumerate(shared):
+            out_ref[o, 2 + i:3 + i, 384:384 + v.shape[0]] = v[...][None]
+    exact = lax.Precision.HIGHEST
+    groups = lax.broadcasted_iota(jnp.int32, (4 * heads, out.shape[2]), 1) // 8
+    groups = jnp.where(groups == lax.broadcasted_iota(jnp.int32, groups.shape, 0), 1.0, 0.0)
+    for ax in range(2):
+        t = lax.dot_general(groups, out[ax], NT, precision=exact, preferred_element_type=f32)
+        for h in range(2 * heads):
+            line = jnp.concatenate([t[2 * h:2 * h + 1] - t[2 * h + 1:2 * h + 2], t[2 * h + 1:2 * h + 2]], 1)
+            out_ref[h // heads, 2 + h % heads:3 + h % heads, 128 * (ax + 1):128 * (ax + 1) + 2 * near] = line
+    seq = jnp.zeros((2 * heads, 128), f32)
+    m = lax.broadcasted_iota(jnp.int32, (128, 128), 0)
+    lane = lax.broadcasted_iota(jnp.int32, (128, 128), 1)
+    for i, base in enumerate((-128, 0, 0, 128, 128, 256, -MAX_DIST - 128, MAX_DIST + 256)):
+        d = base - m
+        b = jnp.where(d > 0, BUCKETS // 2, 0)
+        for e in bucket_edges(BUCKETS, MAX_DIST):
+            b = b + jnp.where(jnp.abs(d) >= e, 1, 0)
+        seq = seq + jnp.dot(toep[:, i, :], jnp.where(b == lane, 1.0, 0.0), precision=exact, preferred_element_type=f32)
+    for h in range(2 * heads):
+        out_ref[h // heads, 2 + h % heads:3 + h % heads, 0:128] = seq[h:h + 1]
+
+
+def pack_sums(sums, dqkv, dqkv_o, up, up_o, shared, rows, lanes, after=()):
+    flat = [x for s in sums for x in s]
+    return pl.pallas_call(
+        partial(skip_refs, partial(tables_kernel, parts=len(sums)), len(flat) + 4 + len(shared), len(after)),
+        out_shape=jax.ShapeDtypeStruct((2, rows, lanes), f32),
+        in_specs=[VMEM] * (len(flat) + 4 + len(shared)) + [ANY] * len(after),
+        out_specs=VMEM,
+        compiler_params=pltpu.CompilerParams(vmem_limit_bytes=VM),
+        name="pack_sums",
+        cost_estimate=BRIEF,
+    )(*flat, dqkv, dqkv_o, up, up_o, *shared, *after)
+
+
+def unpack_kernel(total_ref, *refs, width, heads):
+    bq, bv, bu, ts, tx, ty = refs[:6]
+    bq[...] = total_ref[1, 0:width]
+    bv[...] = total_ref[1, 2 * width:3 * width]
+    bu[...] = total_ref[0, 0:bu.shape[0]]
+    for i, t in enumerate((ts, tx, ty)):
+        t[...] = total_ref[2:2 + heads, 128 * i:128 * i + t.shape[1]]
+    for i, v in enumerate(refs[6:]):
+        v[...] = total_ref[2 + i, 384:384 + v.shape[0]]
+
+
+def unpack_sums(total, width, heads, shapes):
+    return pl.pallas_call(
+        partial(unpack_kernel, width=width, heads=heads),
+        out_shape=[jax.ShapeDtypeStruct(s, f32) for s in shapes],
+        in_specs=[VMEM],
+        out_specs=[VMEM] * len(shapes),
+        name="unpack_sums",
+        cost_estimate=BRIEF,
+    )(total)
+
+
+def tokens_kernel(first_ref, d_ref, do_ref, wq_ref, wk_ref, wv_ref, wo_ref, out_ref):
+    W = wq_ref.shape[1]
+    total = first_ref[...] + lax.dot_general(do_ref[...], wo_ref[...], NT, preferred_element_type=f32)
+    for i, w in enumerate((wq_ref, wk_ref, wv_ref)):
+        total = total + lax.dot_general(d_ref[:, i * W:(i + 1) * W], w[...], NT, preferred_element_type=f32)
+    out_ref[...] = total
+
+
+def grad_tokens_of(first, d, do, wq, wk, wv, wo, seq, after=()):
+    rows, width = first.shape
+    RB = 240
+    block = lambda n: pl.BlockSpec((RB, n), lambda i: (i, 0))
+    whole = lambda w: pl.BlockSpec(w.shape, lambda i: (0, 0))
+    return pl.pallas_call(
+        partial(skip_refs, tokens_kernel, 7, len(after)),
+        grid=(rows // RB,),
+        in_specs=[block(width), block(d.shape[1]), block(d.shape[1]), whole(wq), whole(wk), whole(wv), whole(wo)] + [ANY] * len(after),
+        out_specs=block(width),
+        out_shape=jax.ShapeDtypeStruct((seq, width), f32),
+        compiler_params=pltpu.CompilerParams(vmem_limit_bytes=VM),
+        name="grad_tokens",
+        cost_estimate=BRIEF,
+    )(first, d, do, wq, wk, wv, wo, *after)
 
 def swap(value, axis, bit=1):
     count = lax.axis_size(axis)
@@ -413,32 +548,34 @@
     return (a.astype(f32) + b.astype(f32)).astype(bf)
 
 
-def core_sum(own, other):
-    core = lax.axis_index("core")
-    both = jnp.stack([own, other])
-    return add_low(half_of(both, 1, core), swap(half_of(both, 1, 1 - core), "core"))
-
-
-def tensor_sum(both):
-    return add_low(both[0], swap(both[1], "tensor"))
-
-
-def far_halve(total, bit):
-    at = (lax.axis_index("far") // bit) % 2
-    return add_low(half_of(total, 0, at), swap(half_of(total, 0, 1 - at), "far", bit))
-
-
-def far_double(total, bit):
-    return join(total, swap(total, "far", bit), (lax.axis_index("far") // bit) % 2, 0)
-
-
-def core_join(total):
-    return join(total, swap(total, "core"), lax.axis_index("core"), 0).astype(f32)
-
-
-def reduce_small(own, other):
-    total = own + swap(other, "tensor")
-    total = total + swap(total, "core")
+def far_side(bit):
+    return (lax.axis_index("far") // bit) % 2
+
+
+def arrive(moment, *values):
+    return lax.optimization_barrier(values + (moment,))[:-1]
+
+
+def halve(total, bit):
+    at = far_side(bit)
+    return half_of(total, 0, at), swap(half_of(total, 0, 1 - at), "far", bit)
+
+
+def double(total, got, bit, base):
+    if total.shape[0] % 16:
+        return join(total, got, far_side(bit), 0), base
+    return jnp.concatenate([total, got], 0), base + [far_side(bit)]
+
+
+def spread(total, got, base, widths, turned):
+    place = 0
+    for side in base[::-1]:
+        place = 2 * place + side
+    block = total.shape[0] >> len(base)
+    return finish(total, got, lax.axis_index("core"), jnp.asarray(place), block, widths, turned)
+
+
+def reduce_small(total):
     for bit in far_bits():
         total = total + swap(total, "far", bit)
     return total
@@ -488,38 +625,41 @@
     heads = local // HEAD_DIM
     hidden = w_up.shape[1]
     core = lax.axis_index("core")
+    small_rows = -(-(2 + max(heads, 6)) // 8) * 8
 
     small, wide = pack(
         [b_query, b_value, b_up, table_seq, table_x, table_y],
         [b_out, gain_attn, shift_attn, b_down, gain_ffn, shift_ffn], width, hidden,
     )
     small_o = swap(small, "tensor")
+    halves, _ = lax.optimization_barrier((jnp.concatenate([half_of(w, 0, core) for w in (w_query, w_key, w_value)], 1), small))
+    qkv_half = swap(halves, "tensor")
     b_out, gain_attn, shift_attn, b_down, gain_ffn, shift_ffn = [wide[i:i + 1] for i in range(6)]
-
-    def fetch(mine):
-        got = swap(mine, "tensor")
-        return join(got, swap(got, "core"), core, mine.ndim - 2)
-
-    wqkv_o = fetch(jnp.stack([half_of(w, 0, core) for w in (w_query, w_key, w_value)]))
-    wq_o, wk_o, wv_o = wqkv_o[0], wqkv_o[1], wqkv_o[2]
-    wo_o, wu_o, wd_o = [fetch(half_of(w, 0, core)) for w in (w_out, w_up, w_down)]
 
     x = jnp.pad(tokens[0], ((0, rows - seq), (0, 0)))
     g = jnp.pad(cotangent[0], ((0, rows - seq), (0, 0)))
-
-    def project(wq, wk, wv, vectors):
-        bias = vectors[1:2].astype(f32)
-        return (
-            (mm(x, wq) + bias[:, :local]).astype(bf),
-            mm(x, wk).astype(bf),
-            (mm(x, wv) + bias[:, 2 * local:3 * local]).astype(bf),
-        )
-
+    bias = small[1:2].astype(f32)
+    q = ((mm(x, w_query) + bias[:, :local]).astype(bf), 0)
+    k = (mm(x, w_key).astype(bf), 0)
+    v = ((mm(x, w_value) + bias[:, 2 * local:3 * local]).astype(bf), 0)
     idx, toep, toep_o = prep(text_len, box_coords[0], small, small_o, heads, rows, lanes)
-    q, k, v = project(w_query, w_key, w_value, small)
-    ctx, prob = attn_fwd(q, k, v, idx, toep, small)
-    q_o, k_o, v_o = project(wq_o, wk_o, wv_o, small_o)
-    ctx_o, prob_o = attn_fwd(q_o, k_o, v_o, idx, toep_o, small_o)
+
+    def fetched(got):
+        return join(got, swap(got, "core"), core, 0)
+
+    out_half = swap(half_of(w_out, 0, core), "tensor")
+    up_half = swap(half_of(w_up, 0, core), "tensor")
+    ctx, prob = attn_fwd(q, k, v, local, idx, toep, small)
+    wqkv_o = fetched(qkv_half)
+    down_half, ctx = lax.optimization_barrier((half_of(w_down, 0, core), ctx))
+    down_half = swap(down_half, "tensor")
+    both = (mm(x, wqkv_o) + small_o[1:2, :3 * local].astype(f32)).astype(bf)
+    q_o, k_o, v_o = (both, 0), (both, 1), (both, 2)
+    wo_o = fetched(out_half)
+    ctx_o, prob_o = attn_fwd(q_o, k_o, v_o, local, idx, toep_o, small_o, (wo_o,))
+    wu_o = fetched(up_half)
+    down_half, ctx_o = lax.optimization_barrier((down_half, ctx_o))
+    wd_o = fetched(down_half)
 
     attn = mm(ctx, w_out) + mm(ctx_o, wo_o) + b_out
     n1, inv1 = norm_parts(x.astype(f32) + attn)
@@ -539,82 +679,139 @@
     grad_mid = norm_back(gf * gain_ffn, n2, inv2)
     gb = grad_mid.astype(bf)
     grad_b_down = jnp.sum(gb.astype(f32), axis=0)
-    down = core_sum(mm_tn(act, gb).astype(bf), mm_tn(act_o, gb).astype(bf))
+
+    def terms(left, right):
+        sent = swap(mm_tn(half_of(left, 1, 1 - core), right).astype(bf), "core")
+        return mm_tn(half_of(left, 1, core), right).astype(bf), sent
+
+    def add_three(a, b, c):
+        return (a.astype(f32) + b.astype(f32) + c.astype(f32)).astype(bf)
+
+    bits = far_bits()
+    down_o = add_low(*terms(act_o, gb))
+    down_x = swap(down_o, "tensor")
+    gh_o = (mm_nt(gb, wd_o) * slope_o.astype(f32)).astype(bf)
+    gb, down_o = lax.optimization_barrier((gb, down_o))
+    down = terms(act, gb)
     gh = (mm_nt(gb, w_down) * slope.astype(f32)).astype(bf)
-    gh_o = (mm_nt(gb, wd_o) * slope_o.astype(f32)).astype(bf)
     grad_b_up = jnp.sum(gh.astype(f32), axis=0)
     grad_b_up_o = jnp.sum(gh_o.astype(f32), axis=0)
+    up_o = terms(low, gh_o)
+    up = terms(low, gh)
     grad_normed = mm_nt(gh, w_up) + mm_nt(gh_o, wu_o) + grad_mid
     grad_gain_attn = jnp.sum(grad_normed * n1, axis=0)
     grad_shift_attn = jnp.sum(grad_normed, axis=0)
     grad_first = norm_back(grad_normed * gain_attn, n1, inv1)
     ga = grad_first.astype(bf)
     grad_b_out = jnp.sum(ga.astype(f32), axis=0)
+    out_o = terms(ga, ctx_o)
+    out = terms(ga, ctx)
+    gc_o = mm_nt(ga, wo_o).astype(bf)
     gc = mm_nt(ga, w_out).astype(bf)
-    gc_o = mm_nt(ga, wo_o).astype(bf)
-    bits = far_bits()
-
-    def wide_rows(first, second):
-        second = second.reshape(-1, first.shape[1])
-        extra = -(first.shape[0] + second.shape[0]) % (2 * lax.axis_size("far"))
-        return jnp.concatenate([first, second, jnp.zeros((extra, first.shape[1]), bf)], 0)
-
-    up = core_sum(
-        wide_rows(mm_tn(low, gh).astype(bf), mm_tn(ctx, ga).astype(bf)),
-        wide_rows(mm_tn(low, gh_o).astype(bf), mm_tn(ctx_o, ga).astype(bf)),
-    )
-    dq, dk, dv, gs = attn_bwd(q, k, v, gc, prob, (up,))
-    down = tensor_sum(down)
-    dq_o, dk_o, dv_o, gs_o = attn_bwd(q_o, k_o, v_o, gc_o, prob_o, (down,))
-    grads = [mm_tn(x, d).astype(bf) for d in (dq, dk, dv, dq_o, dk_o, dv_o)]
-    qkv = core_sum(jnp.concatenate(grads[:3], 1), jnp.concatenate(grads[3:], 1))
-    up = tensor_sum(up)
-    sums = [hist(gs, gs_o, idx, 0, 3, (qkv, up))]
-    up = far_halve(up, bits[0])
-    sums.append(hist(gs, gs_o, idx, 1, 3, (up,)))
-    up = far_halve(up, bits[1])
-    qkv = tensor_sum(qkv)
-    sums.append(hist(gs, gs_o, idx, 2, 3, (up, qkv)))
-    for bit in bits[2:]:
-        up = far_halve(up, bit)
-    for bit in bits[::-1]:
-        up = far_double(up, bit)
-    for bit in bits:
-        qkv = far_halve(qkv, bit)
-    for bit in bits[::-1]:
-        qkv = far_double(qkv, bit)
-    down = lax.psum(down, "far")
-    late = lax.optimization_barrier((sums[-1][0], down, dq, dk, dv, dq_o, dk_o, dv_o))
-    grad_w_down = core_join(late[1])
-    up = core_join(up)
-    grad_w_up = up[:width]
-    grad_w_out = up[width:width + w_out.size // hidden].reshape(w_out.shape)
-    qkv = core_join(qkv)
-    t_seq, t_x, t_y = tables_of(sums)
-    grad_tokens = grad_first
-    for d, w in zip(late[2:], (w_query, w_key, w_value, wq_o, wk_o, wv_o)):
-        grad_tokens = grad_tokens + mm_nt(d, w)
-    grad_tokens = grad_tokens[:seq][None]
-
-    bias_sums = [jnp.sum(d.astype(f32), axis=0) for d in (dq, dv, dq_o, dv_o)]
+    up_o = add_low(jnp.concatenate([up_o[0], out_o[0]], 1), jnp.concatenate([up_o[1], out_o[1]], 1))
+    up_x = swap(up_o, "tensor")
+    up = [jnp.concatenate([u, o], 1) for u, o in zip(up, out)]
+    dqkv_o, gs_o = attn_bwd(q_o, k_o, v_o, local, gc_o, prob_o, (up_o, output))
+    down_x, = arrive(gs_o, down_x)
+    down = add_three(*down, down_x)
+    down, down_in = halve(down, bits[0])
+    qkv_o = add_low(*terms(x, dqkv_o))
+    qkv_x = swap(qkv_o, "tensor")
+    dqkv, gs = attn_bwd(q, k, v, local, gc, prob, (down, qkv_o))
+
+    up_x, down_in = arrive(gs, up_x, down_in)
+    down, down_in = halve(add_low(down, down_in), bits[1])
+    up, up_in = halve(add_three(*up, up_x), bits[0])
+    qkv, qkv_core = terms(x, dqkv)
+    sums = [hist(gs, gs_o, idx, 0, 6, (up, down, qkv))]
+
+    down_in, up_in, qkv_core, qkv_x = arrive(sums[-1][0], down_in, up_in, qkv_core, qkv_x)
+    down = add_low(down, down_in)
+    up, up_in = halve(add_low(up, up_in), bits[1])
+    qkv, qkv_in = halve(add_three(qkv, qkv_core, qkv_x), bits[0])
+    for bit in bits[3:]:
+        keep, got = halve(down, bit)
+        down = add_low(keep, got)
+    down, down_in = halve(down, bits[2])
+    sums.append(hist(gs, gs_o, idx, 6, 3, (qkv, up, down)))
+
+    down_in, up_in, qkv_in = arrive(sums[-1][0], down_in, up_in, qkv_in)
+    down = add_low(down, down_in)
+    up = add_low(up, up_in)
+    qkv, qkv_in = halve(add_low(qkv, qkv_in), bits[1])
+    for bit in bits[3:]:
+        keep, got = halve(up, bit)
+        up = add_low(keep, got)
+    up, up_in = halve(up, bits[2])
+    down_base, up_base, base = [], [], []
+    for bit in bits[:2:-1]:
+        down, down_base = double(down, swap(down, "far", bit), bit, down_base)
+    down_in = swap(down, "far", bits[2])
+    sums.append(hist(gs, gs_o, idx, 9, 3, (up, qkv, down)))
+
+    down_in, up_in, qkv_in = arrive(sums[-1][0], down_in, up_in, qkv_in)
+    down, down_base = double(down, down_in, bits[2], down_base)
+    down_in = swap(down, "far", bits[1])
+    up = add_low(up, up_in)
+    for bit in bits[:2:-1]:
+        up, up_base = double(up, swap(up, "far", bit), bit, up_base)
+    up_in = swap(up, "far", bits[2])
+    qkv = add_low(qkv, qkv_in)
+    for bit in bits[3:]:
+        keep, got = halve(qkv, bit)
+        qkv = add_low(keep, got)
+    qkv, qkv_in = halve(qkv, bits[2])
+    sums.append(hist(gs, gs_o, idx, 12, 3, (up, qkv, down)))
+
+    down_in, up_in, qkv_in = arrive(sums[-1][0], down_in, up_in, qkv_in)
+    qkv = add_low(qkv, qkv_in)
+    for bit in bits[:2:-1]:
+        qkv, base = double(qkv, swap(qkv, "far", bit), bit, base)
+    qkv_in = swap(qkv, "far", bits[2])
+    up, up_base = double(up, up_in, bits[2], up_base)
+    up_in = swap(up, "far", bits[1])
+    down, down_base = double(down, down_in, bits[1], down_base)
+    down_in = swap(down, "far", bits[0])
     shared = [grad_b_out, grad_gain_attn, grad_shift_attn, grad_b_down, grad_gain_ffn, grad_shift_ffn]
-
-    def packed(query_sum, value_sum, up_sum, at):
-        tables = [t[at:at + heads].reshape(-1) for t in (t_seq, t_x, t_y)]
-        return jnp.concatenate([query_sum, value_sum, up_sum] + tables + shared)
-
-    totals = reduce_small(packed(*bias_sums[:2], grad_b_up, 0), packed(*bias_sums[2:], grad_b_up_o, heads))
+    payload = pack_sums(sums, dqkv, dqkv_o, grad_b_up, grad_b_up_o, shared, small_rows, hidden, (up, qkv, down))
+
+    up_in, qkv_in = arrive(payload, up_in, qkv_in)
+    qkv, base = double(qkv, qkv_in, bits[2], base)
+    qkv_in = swap(qkv, "far", bits[1])
+    up, up_base = double(up, up_in, bits[1], up_base)
+    up_in = swap(up, "far", bits[0])
+    total, total_in = payload[0], swap(payload[1], "tensor")
+    grad_tokens = grad_tokens_of(grad_first, dqkv, dqkv_o, w_query, w_key, w_value, wqkv_o, seq, (up, qkv))
+
+    qkv_in, total_in, down_in = arrive(grad_tokens, qkv_in, total_in, down_in)
+    qkv, base = double(qkv, qkv_in, bits[1], base)
+    qkv_in = swap(qkv, "far", bits[0])
+    total = total + total_in
+    total_in = swap(total, "core")
+    down, down_base = double(down, down_in, bits[0], down_base)
+    down_in = swap(down, "core")
+    grad_tokens, qkv, total, down = arrive(qkv, grad_tokens, qkv, total, down)
+    grad_tokens = grad_tokens[None]
+
+    total = total + total_in
+    grad_w_down, = spread(down, down_in, down_base, (width,), (False,))
+    up_in, qkv_in = arrive(grad_w_down, up_in, qkv_in)
+    up, up_base = double(up, up_in, bits[0], up_base)
+    up_in = swap(up, "core")
+    qkv, base = double(qkv, qkv_in, bits[0], base)
+    qkv_in = swap(qkv, "core")
+    totals = reduce_small(total)
+    grads_qkv = spread(qkv, qkv_in, base, (local,) * 3, (False,) * 3)
+    up_block = up.shape[0] >> len(up_base)
+    grad_w_up, grad_w_out = spread(up, up_in, up_base, (hidden, local), (False, up_block % 128 == 0))
+    if up_block % 128:
+        grad_w_out = grad_w_out.T
     shapes = [(local,), (local,), (hidden,), table_seq.shape, table_x.shape, table_y.shape] + [(width,)] * 6
-    pieces = []
-    at = 0
-    for shape in shapes:
-        size = math.prod(shape)
-        pieces.append(totals[at:at + size].reshape(shape))
-        at += size
+    pieces = unpack_sums(totals, local, heads, shapes)
     g_bq, g_bv, g_bu, g_ts, g_tx, g_ty, g_bo, g_ga, g_sa, g_bd, g_gf, g_sf = pieces
     return (
         output, grad_tokens,
-        qkv[:, :local], g_bq, qkv[:, local:2 * local], qkv[:, 2 * local:], g_bv,
+        grads_qkv[0], g_bq, grads_qkv[1], grads_qkv[2], g_bv,
         grad_w_out, g_bo, g_ts, g_tx, g_ty, g_ga, g_sa, grad_w_up, g_bu, grad_w_down, g_bd, g_gf, g_sf,
     )
 

time: 433 us -> 362 us (0.84)
  waiting for transfers between devices: 88 us -> 39 us
  Pallas kernels: 114 us -> 147 us
  other arithmetic: 60.9 us -> 35.3 us
  between operations: 16.3 us -> 2.4 us
  matrix products: 76.9 us -> 67.2 us
  local copies, waits for them, and re-layouts: 32.3 us -> 25.8 us
    ppermute x35 -> x46, waiting for transfers between devices: 85.4 us -> 39 us  [swap(): return lax.ppermute(value, axis, [(i, i ^ bit) for i in range(count)])]
    pallas_call x2 -> x8, Pallas kernels: 37.2 us -> 62.4 us  [the longest x2 37.2 us: attn_fwd(): pl.pallas_call(partial(skip_refs, fwd_kernel, 6, len(after)), grid=(lanes...]
    dot_general x12 -> x6, matrix products: 33.1 us -> 18.8 us  [mm_nt(): lax.dot_general(a, b, (((1,), (1,)), ((), ())), preferred_element_type=f32)]
    convert_element_type x12 -> x10, other arithmetic: 12.9 us -> 3.39 us  [add_low(): return (a.astype(f32) + b.astype(f32)).astype(bf)]
    dynamic_slice x9 -> x14, local copies, waits for them, and re-layouts: 4.51 us -> 12.6 us  [half_of(): return lax.dynamic_slice_in_dim(value, which * size, size, axis)]
    another operation x8 -> x1, other arithmetic: 8.04 us -> 0.58 us  [finish(): jnp.stack([core, base]).astype(jnp.int32)]
    broadcast_in_dim x1 -> x0, other arithmetic: 6.47 us -> none  [per_device(): grad_tokens = grad_tokens[:seq][None]]
    concatenate x0 -> x9, other arithmetic: none -> 6.27 us  [the longest x8 5.28 us: double(): return (jnp.concatenate([total, got], 0), base + [far_side(bit)])]
  transfers between devices with their start and end apart: 36 -> 46, of which waited for: 17 -> 12; matrix products, arithmetic and copies ran while one was open for 27% -> 30% of each run, Pallas kernels for 26% -> 39%
where the time goes in v3:
time: 362 us; the launch traced here: 358 us
  Pallas kernels  147 us (41%)
  matrix products  67.2 us (19%)
  starting transfers between devices  41.2 us (11%)
  waiting for transfers between devices  39 us (11%)
  other arithmetic  35.3 us (10%)
  local copies, waits for them, and re-layouts  25.8 us (7%)
    ppermute x46, starting transfers between devices, swap(): return lax.ppermute(value, axis, [(i, i ^ bit) for i in range(count)])  41.2 us
    pallas_call x4, Pallas kernels, hist(): pl.pallas_call(partial(skip_refs, partial(hist_kernel, part=part), 3, len...  39.1 us
    ppermute x46, waiting for transfers between devices, swap(): return lax.ppermute(value, axis, [(i, i ^ bit) for i in range(count)])  39 us
    pallas_call x2, Pallas kernels, attn_fwd(): pl.pallas_call(partial(skip_refs, fwd_kernel, 6, len(after)), grid=(lanes...  37.2 us
    pallas_call x2, Pallas kernels, attn_bwd(): pl.pallas_call(partial(skip_refs, bwd_kernel, 5, len(after)), grid=(lanes...  35.7 us
    dot_general x16, matrix products, mm_tn(): lax.dot_general(a, b, (((0,), (0,)), ((), ())), preferred_element_type=f32)  25.3 us
    dot_general x10, matrix products, mm(): return jnp.dot(a, b, preferred_element_type=f32)  23.1 us
    dot_general x6, matrix products, mm_nt(): lax.dot_general(a, b, (((1,), (1,)), ((), ())), preferred_element_type=f32)  18.8 us
  transfers between devices with their start and end apart: 46, of which 12 were waited for; matrix products, arithmetic and copies ran while one was open for 30% of the time, Pallas kernels for 39%

profile of v3, /device:TPU:0, one launch (start us, length us, event | category | flops | bytes accessed | tf_op | source)
XLA Modules:
  0.0 357.9 jit_solution(5690957951459594310)
XLA Ops:
  0.7 1.6 pack.1
  2.3 2.9 collective-permute-start
  8.4 2.0 collective-permute-start.4
  12.4 3.1 convolution_convert_fusion.14.refs_1_
  18.7 1.6 slice_reduce_fusion.1
  20.3 2.4 constant_dynamic-slice_fusion.23
  24.7 8.2 %buckets.1 = (s16[2,720,768]{2,1,0:T(8,128)(2,1)}, bf16[6,640,128]{2,1,0:T(8,128)(2,1)}, bf16[6,640,128]{2,1,0:T(8,128)(2,1)}) custom-call(s32[1]{0:T(128)S(6)} %copy.49.len_ref, s32[2,709]{1,0:T(2,128)} %bitcast.66, bf16[16,1536]{1,0:T(8,128)(2,1)} %get-tuple-element.91.own_ref.refs_5_, bf16[16,1536]{1,0:T(8,128)(2,1)} %collective-permute-done.oth_ref.refs_5_), custom_call_target="tpu_custom_call" | custom-call | flops 10000000000 | bytes 1 | tf_op jit(solution)/shard_map/buckets/pallas_call | solution.py:96
  32.9 18.5 %attn_fwd.2 = (bf16[720,384]{1,0:T(8,128)(2,1)}, bf16[6,720,768]{2,1,0:T(8,128)(2,1)}) custom-call(bf16[720,384]{1,0:T(8,128)(2,1)} %fusion.26.refs_0_, bf16[720,384]{1,0:T(8,128)(2,1)} %convolution_convert_fusion.14.refs_1_, bf16[720,384]{1,0:T(8,128)(2,1)} %fusion.27.refs_2_, s16[2,720,768]{2,1,0:T(8,128)(2,1)} %get-tuple-element.92.refs_3_.refs_2_, ...), custom_call_target="tpu_custom_call" | custom-call | flops 10000000000 | bytes 1 | tf_op jit(solution)/shard_map/attn_fwd/pallas_call | solution.py:201
  51.4 1.9 collective-permute-start.1
  55.5 1.8 fusion.88
  59.2 3.7 %collective-permute-done.6 = bf16[384,1536]{1,0:T(8,128)(2,1)} collective-permute-done((bf16[384,1536]{1,0:T(8,128)(2,1)}, bf16[384,1536]{1,0:T(8,128)(2,1)}, u32[]{:S(2)}, u32[]{:S(2)}) %collective-permute-start.6) | collective-permute-done | bytes 1179680 | tf_op jit(solution)/shard_map/ppermute | solution.py:523
  64.2 2.9 fusion.10.refs_0_.refs_1_.refs_2_
  67.0 18.7 %attn_fwd.3 = (bf16[720,384]{1,0:T(8,128)(2,1)}, bf16[6,720,768]{2,1,0:T(8,128)(2,1)}) custom-call(bf16[720,1152]{1,0:T(8,128)(2,1)} %fusion.10.refs_0_.refs_1_.refs_2_, bf16[720,1152]{1,0:T(8,128)(2,1)} %fusion.10.refs_0_.refs_1_.refs_2_, bf16[720,1152]{1,0:T(8,128)(2,1)} %fusion.10.refs_0_.refs_1_.refs_2_, ...), custom_call_target="tpu_custom_call" | custom-call | flops 10000000000 | bytes 1 | tf_op jit(solution)/shard_map/attn_fwd/pallas_call | solution.py:201
  86.6 2.3 fusion.86
  90.1 2.3 multiply_convert_fusion.3
  92.4 1.9 fusion.89
  95.7 1.8 broadcast_select_fusion.3
  97.4 3.4 multiply_convert_fusion.2
  100.9 2.4 broadcast_select_fusion.1
  103.3 2.3 fusion.87
  106.9 1.6 fusion.20
  111.4 6.0 %convert_reduce_fusion = (f32[1536]{0:T(1024)}, bf16[720,1536]{1,0:T(8,128)(2,1)S(1)}) fusion(f32[720,1536]{1,0:T(8,128)S(1)} %get-tuple-element.235, f32[1536]{0:T(1024)S(1)} %fusion.70, bf16[720,768]{1,0:T(8,128)(2,1)S(1)} %get-tuple-element.103, bf16[768,768]{1,0:T(8,128)(2,1)S(1)} %get-tuple-element.205, bf16[768,768]{1,0:T(8,128)(2,1)S(1)} %get-tuple-element.204), kind=kOutput, calls=%fused_computation.12 | convolution fusion | flops 1719998976 | bytes 10113024 | tf_op jit(solution)/shard_map/dot_general | solution.py:609
  121.5 2.2 add_convert_fusion.3
  123.6 4.3 %convert_reduce_fusion.1 = (f32[1536]{0:T(1024)}, bf16[720,1536]{1,0:T(8,128)(2,1)S(1)}) fusion(f32[720,1536]{1,0:T(8,128)S(1)} %get-tuple-element.233, f32[1536]{0:T(1024)S(1)} %copy-done.42, bf16[720,768]{1,0:T(8,128)(2,1)S(1)} %get-tuple-element.103, bf16[1536,768]{1,0:T(8,128)(2,1)S(1)} %copy-done.27), kind=kOutput, calls=%fused_computation.13 | convolution fusion | flops 1715280384 | bytes 10113024 | tf_op jit(solution)/shard_map/dot_general | solution.py:609
  127.9 1.9 fusion.90
  129.8 3.4 multiply_reduce_fusion
  133.2 2.4 convert_reduce_fusion.4
  136.1 1.6 convolution_convert_fusion.12.refs_3_
  140.5 2.1 convolution_convert_fusion.8
  145.3 2.1 convolution_convert_fusion.9
  149.0 18.0 %attn_bwd.2 = (bf16[720,1152]{1,0:T(8,128)(2,1)}, bf16[6,720,768]{2,1,0:T(8,128)(2,1)}) custom-call(bf16[720,1152]{1,0:T(8,128)(2,1)} %fusion.10.refs_0_.refs_1_.refs_2_, bf16[720,1152]{1,0:T(8,128)(2,1)} %fusion.10.refs_0_.refs_1_.refs_2_, bf16[720,1152]{1,0:T(8,128)(2,1)} %fusion.10.refs_0_.refs_1_.refs_2_, ...), custom_call_target="tpu_custom_call" | custom-call | flops 10000000000 | bytes 1 | tf_op jit(solution)/shard_map/attn_bwd/pallas_call | solution.py:280
  167.0 2.5 convolution_convert_fusion.6
  172.7 1.7 collective-permute-start.17
  174.4 2.1 add_convert_fusion.2
  179.0 1.9 fusion.16.refs_6_
  180.9 17.7 %attn_bwd.3 = (bf16[720,1152]{1,0:T(8,128)(2,1)}, bf16[6,720,768]{2,1,0:T(8,128)(2,1)}) custom-call(bf16[720,384]{1,0:T(8,128)(2,1)} %fusion.26.refs_0_, bf16[720,384]{1,0:T(8,128)(2,1)} %convolution_convert_fusion.14.refs_1_, bf16[720,384]{1,0:T(8,128)(2,1)} %fusion.27.refs_2_, bf16[720,384]{1,0:T(8,128)(2,1)} %convolution_convert_fusion.13.refs_3_, ...), custom_call_target="tpu_custom_call" | custom-call | flops 10000000000 | bytes 1 | tf_op jit(solution)/shard_map/attn_bwd/pallas_call | solution.py:280
  198.6 3.4 convolution_convert_fusion.4.refs_5_
  202.0 1.9 convolution_convert_fusion.5
  204.5 3.4 collective-permute-done.17
  209.1 1.9 add_convert_fusion
  212.0 1.7 collective-permute-start.20
  216.0 13.6 %table_sums.4 = (f32[2,32,192]{2,1,0:T(8,128)}, f32[12,8,128]{2,1,0:T(8,128)}) custom-call(bf16[6,720,768]{2,1,0:T(8,128)(2,1)} %get-tuple-element.110.refs_0_, bf16[6,720,768]{2,1,0:T(8,128)(2,1)} %get-tuple-element.106.refs_1_, s16[2,720,768]{2,1,0:T(8,128)(2,1)} %get-tuple-element.92.refs_3_.refs_2_, bf16[192,1920]{1,0:T(8,128)(2,1)} %get-tuple-element.210.refs_3_, ...), custom_call_target="tpu_custom_call" | custom-call | flops 10000000000 | bytes 1 | tf_op jit(solution)/shard_map/table_sums/pallas_call | solution.py:407
  235.6 2.6 collective-permute-start.23
  238.2 8.3 %table_sums.5 = (f32[2,32,192]{2,1,0:T(8,128)}, f32[12,8,128]{2,1,0:T(8,128)}) custom-call(bf16[6,720,768]{2,1,0:T(8,128)(2,1)} %get-tuple-element.110.refs_0_, bf16[6,720,768]{2,1,0:T(8,128)(2,1)} %get-tuple-element.106.refs_1_, s16[2,720,768]{2,1,0:T(8,128)(2,1)} %get-tuple-element.92.refs_3_.refs_2_, bf16[192,1152]{1,0:T(8,128)(2,1)} %get-tuple-element.214.refs_3_, ...), custom_call_target="tpu_custom_call" | custom-call | flops 10000000000 | bytes 1 | tf_op jit(solution)/shard_map/table_sums/pallas_call | solution.py:407
  249.1 1.6 collective-permute-start.27
  252.0 8.4 %table_sums.6 = (f32[2,32,192]{2,1,0:T(8,128)}, f32[12,8,128]{2,1,0:T(8,128)}) custom-call(bf16[6,720,768]{2,1,0:T(8,128)(2,1)} %get-tuple-element.110.refs_0_, bf16[6,720,768]{2,1,0:T(8,128)(2,1)} %get-tuple-element.106.refs_1_, s16[2,720,768]{2,1,0:T(8,128)(2,1)} %get-tuple-element.92.refs_3_.refs_2_, bf16[48,1920]{1,0:T(8,128)(2,1)} %get-tuple-element.224.refs_3_, ...), custom_call_target="tpu_custom_call" | custom-call | flops 10000000000 | bytes 1 | tf_op jit(solution)/shard_map/table_sums/pallas_call | solution.py:407
  260.4 3.3 collective-permute-done.26
  265.6 2.9 collective-permute-start.30
  268.6 8.7 %table_sums.7 = (f32[2,32,192]{2,1,0:T(8,128)}, f32[12,8,128]{2,1,0:T(8,128)}) custom-call(bf16[6,720,768]{2,1,0:T(8,128)(2,1)} %get-tuple-element.110.refs_0_, bf16[6,720,768]{2,1,0:T(8,128)(2,1)} %get-tuple-element.106.refs_1_, s16[2,720,768]{2,1,0:T(8,128)(2,1)} %get-tuple-element.92.refs_3_.refs_2_, bf16[48,1920]{1,0:T(8,128)(2,1)} %copy-done.4, ...), custom_call_target="tpu_custom_call" | custom-call | flops 10000000000 | bytes 1 | tf_op jit(solution)/shard_map/table_sums/pallas_call | solution.py:407
  277.4 2.1 collective-permute-done.30
  282.9 2.4 collective-permute-start.32
  285.3 3.5 pack_sums.1
  291.1 2.3 collective-permute-done.32
  296.1 7.9 %grad_tokens.1 = f32[709,768]{1,0:T(8,128)} custom-call(f32[720,768]{1,0:T(8,128)} %get-tuple-element.202.refs_0_, bf16[720,1152]{1,0:T(8,128)(2,1)} %get-tuple-element.109.refs_8_.refs_1_, bf16[720,1152]{1,0:T(8,128)(2,1)} %get-tuple-element.108.refs_9_.refs_2_, bf16[768,384]{1,0:T(8,128)(2,1)} %refs_3_.1, bf16[768,384]{1,0:T(8,128)(2,1)} %refs_4_.1, ...), custom_call_target="tpu_custom_call" | custom-call | flops 10000000000 | bytes 1 | tf_op jit(solution)/shard_map/grad_tokens/pallas_call | solution.py:510
  305.7 1.9 collective-permute-done.41
  307.7 4.1 %collective-permute-done.42 = f32[8,1536]{1,0:T(8,128)S(1)} collective-permute-done((f32[8,1536]{1,0:T(8,128)S(1)}, f32[8,1536]{1,0:T(8,128)S(1)}, u32[]{:S(2)}, u32[]{:S(2)}) %collective-permute-start.42) | collective-permute-done | bytes 49184 | tf_op jit(solution)/shard_map/ppermute | solution.py:523
  314.0 1.7 collective-permute-start.38
  318.2 3.6 %copy.44 = f32[1,709,768]{2,0,1:T(1,128)} copy(f32[1,709,768]{2,1,0:T(8,128)S(1)} %bitcast.55) | data formatting | bytes 4356096
  322.5 4.0 %finish.3 = f32[1536,768]{1,0:T(8,128)} custom-call(s32[2]{0:T(128)} %pad_add_fusion.info_ref, bf16[768,768]{1,0:T(8,128)(2,1)} %pad_maximum_fusion.10.mine_ref, bf16[768,768]{1,0:T(8,128)(2,1)} %collective-permute-done.39.theirs_ref), custom_call_target="tpu_custom_call" | custom-call | flops 10000000000 | bytes 1 | tf_op jit(solution)/shard_map/finish/pallas_call | solution.py:321
  326.4 14.3 %collective-permute-done.38 = bf16[192,1152]{1,0:T(8,128)(2,1)S(1)} collective-permute-done((bf16[192,1152]{1,0:T(8,128)(2,1)S(1)}, bf16[192,1152]{1,0:T(8,128)(2,1)S(1)}, u32[]{:S(2)}, u32[]{:S(2)}) %collective-permute-start.38) | collective-permute-done | bytes 442400 | tf_op jit(solution)/shard_map/ppermute | solution.py:523
  343.7 2.0 collective-permute-done.40.theirs_ref
  346.6 3.6 %finish.4 = (f32[768,384]{1,0:T(8,128)}, f32[768,384]{1,0:T(8,128)}, f32[768,384]{1,0:T(8,128)}) custom-call(s32[2]{0:T(128)} %pad_add_fusion.info_ref, bf16[384,1152]{1,0:T(8,128)(2,1)} %constant_dynamic-update-slice_fusion.mine_ref, bf16[384,1152]{1,0:T(8,128)(2,1)} %copy-done.44), custom_call_target="tpu_custom_call" | custom-call | flops 10000000000 | bytes 1 | tf_op jit(solution)/shard_map/finish/pallas_call | solution.py:321
  350.3 4.8 %finish.5 = (f32[768,1536]{1,0:T(8,128)}, f32[768,384]{1,0:T(8,128)}) custom-call(s32[2]{0:T(128)} %pad_add_fusion.info_ref, bf16[384,1920]{1,0:T(8,128)(2,1)} %copy-done.12, bf16[384,1920]{1,0:T(8,128)(2,1)} %collective-permute-done.45.theirs_ref), custom_call_target="tpu_custom_call" | custom-call | flops 10000000000 | bytes 1 | tf_op jit(solution)/shard_map/finish/pallas_call | solution.py:321
  355.1 2.7 copy.45
  (248 shorter events, 75.6 us)
Async XLA Ops:
  0.7 9.8 %copy-start = (bf16[768,1536]{1,0:T(8,128)(2,1)S(1)}, bf16[768,1536]{1,0:T(8,128)(2,1)}, u32[]{:S(2)}) copy-start(bf16[768,1536]{1,0:T(8,128)(2,1)} %param.37) | copy-start | bytes 7077892
  2.3 6.1 %copy-start.14 = (bf16[384,768]{1,0:T(8,128)(2,1)S(1)}, bf16[384,768]{1,0:T(8,128)(2,1)}, u32[]{:S(2)}) copy-start(bf16[384,768]{1,0:T(8,128)(2,1)} %param.30) | copy-start | bytes 1769476
  2.3 22.4 %collective-permute-start = (bf16[16,1536]{1,0:T(8,128)(2,1)}, bf16[16,1536]{1,0:T(8,128)(2,1)}, u32[]{:S(2)}, u32[]{:S(2)}) collective-permute-start(bf16[16,1536]{1,0:T(8,128)(2,1)} %get-tuple-element.91.own_ref.refs_5_), channel_id=1, source_target_pairs={{0,1},{1,0},{2,3},{3,2},{4,5},{5,4},{6,7},{7,6},{8,9},{9,8},{10,11... | collective-permute-start | bytes 147464 | tf_op jit(solution)/shard_map/ppermute | solution.py:523
  8.3 45.0 %collective-permute-start.2 = (bf16[384,1152]{1,0:T(8,128)(2,1)}, bf16[384,1152]{1,0:T(8,128)(2,1)}, u32[]{:S(2)}, u32[]{:S(2)}) collective-permute-start(bf16[384,1152]{1,0:T(8,128)(2,1)} %pad_maximum_fusion.11), channel_id=1, source_target_pairs={{0,1},{1,0},{2,3},{3,2},{4,5},{5,4},{6,7},{7,6},{8,9},{9,8},{10,11... | collective-permute-start | bytes 2654216 | tf_op jit(solution)/shard_map/ppermute | solution.py:523
  8.4 46.4 %collective-permute-start.4 = (bf16[192,768]{1,0:T(8,128)(2,1)S(1)}, bf16[192,768]{1,0:T(8,128)(2,1)S(1)}, u32[]{:S(2)}, u32[]{:S(2)}) collective-permute-start(bf16[192,768]{1,0:T(8,128)(2,1)S(1)} %constant_dynamic-slice_fusion.19), channel_id=1, source_target_pairs={{0,1},{1,0},{2,3},{3,2},{4,5},{5,4},{6,7},{7,6},{8,9},{9,8},{10,11... | collective-permute-start | bytes 884744 | tf_op jit(solution)/shard_map/ppermute | solution.py:523
  11.5 51.3 %collective-permute-start.6 = (bf16[384,1536]{1,0:T(8,128)(2,1)}, bf16[384,1536]{1,0:T(8,128)(2,1)}, u32[]{:S(2)}, u32[]{:S(2)}) collective-permute-start(bf16[384,1536]{1,0:T(8,128)(2,1)} %constant_dynamic-slice_fusion.18), channel_id=1, source_target_pairs={{0,1},{1,0},{2,3},{3,2},{4,5},{5,4},{6,7},{7,6},{8,9},{9,8},{10,11... | collective-permute-start | bytes 3538952 | tf_op jit(solution)/shard_map/ppermute | solution.py:523
  51.4 35.2 %collective-permute-start.1 = (bf16[768,768]{1,0:T(8,128)(2,1)}, bf16[768,768]{1,0:T(8,128)(2,1)}, u32[]{:S(2)}, u32[]{:S(2)}) collective-permute-start(bf16[768,768]{1,0:T(8,128)(2,1)} %constant_dynamic-slice_fusion.23), channel_id=1, source_target_pairs={{0,1},{1,0},{2,3},{3,2},{4,5},{5,4},{6,7},{7,6},{8,9},{9,8},{10,11... | collective-permute-start | bytes 3538952 | tf_op jit(solution)/shard_map/ppermute | solution.py:523
  53.4 9.5 %collective-permute-start.3 = (bf16[384,1152]{1,0:T(8,128)(2,1)}, bf16[384,1152]{1,0:T(8,128)(2,1)S(1)}, u32[]{:S(2)}, u32[]{:S(2)}) collective-permute-start(bf16[384,1152]{1,0:T(8,128)(2,1)} %collective-permute-done.2), channel_id=1, source_target_pairs={{0,2},{2,0},{1,3},{3,1},{4,6},{6,4},{5,7},{7,5},{8,10},{10,8},{9,1... | collective-permute-start | bytes 2654216 | tf_op jit(solution)/shard_map/ppermute | solution.py:523
  54.9 2.4 collective-permute-start.5
  58.3 5.9 %copy-start.20 = (bf16[1,709,768]{2,1,0:T(8,128)(2,1)S(1)}, bf16[1,709,768]{2,1,0:T(8,128)(2,1)}, u32[]{:S(2)}) copy-start(bf16[1,709,768]{2,1,0:T(8,128)(2,1)} %param.22) | copy-start | bytes 3267076
  62.8 32.8 %collective-permute-start.7 = (bf16[384,1536]{1,0:T(8,128)(2,1)}, bf16[384,1536]{1,0:T(8,128)(2,1)}, u32[]{:S(2)}, u32[]{:S(2)}) collective-permute-start(bf16[384,1536]{1,0:T(8,128)(2,1)} %collective-permute-done.6), channel_id=1, source_target_pairs={{0,2},{2,0},{1,3},{3,1},{4,6},{6,4},{5,7},{7,5},{8,10},{10,8},{9,1... | collective-permute-start | bytes 3538952 | tf_op jit(solution)/shard_map/ppermute | solution.py:523
  67.0 19.6 %copy-start.41 = (f32[768]{0:T(1024)S(1)}, f32[768]{0:T(1024)}, u32[]{:S(2)}) copy-start(f32[768]{0:T(1024)} %get-tuple-element.195) | copy-start | bytes 9220
  86.6 14.3 %collective-permute-start.8 = (bf16[768,768]{1,0:T(8,128)(2,1)}, bf16[768,768]{1,0:T(8,128)(2,1)S(1)}, u32[]{:S(2)}, u32[]{:S(2)}) collective-permute-start(bf16[768,768]{1,0:T(8,128)(2,1)} %collective-permute-done.1), channel_id=1, source_target_pairs={{0,2},{2,0},{1,3},{3,1},{4,6},{6,4},{5,7},{7,5},{8,10},{10,8},{9,1... | collective-permute-start | bytes 3538952 | tf_op jit(solution)/shard_map/ppermute | solution.py:523
  100.9 8.8 %copy-start.47 = (bf16[720,1536]{1,0:T(8,128)(2,1)}, bf16[720,1536]{1,0:T(8,128)(2,1)S(1)}, u32[]{:S(2)}) copy-start(bf16[720,1536]{1,0:T(8,128)(2,1)S(1)} %get-tuple-element.234) | copy-start | bytes 6635524
  110.8 10.1 %collective-permute-start.9 = (bf16[768,768]{1,0:T(8,128)(2,1)S(1)}, bf16[768,768]{1,0:T(8,128)(2,1)S(1)}, u32[]{:S(2)}, u32[]{:S(2)}) collective-permute-start(bf16[768,768]{1,0:T(8,128)(2,1)S(1)} %convolution_convert_fusion.10), channel_id=1, source_target_pairs={{0,2},{2,0},{1,3},{3,1},{4,6},{6,4},{5,7},{7,5},{8,10},{10,8},{9,1... | collective-permute-start | bytes 3538952 | tf_op jit(solution)/shard_map/ppermute | solution.py:523
  118.5 28.9 %collective-permute-start.12 = (bf16[384,1536]{1,0:T(8,128)(2,1)S(1)}, bf16[384,1536]{1,0:T(8,128)(2,1)S(1)}, u32[]{:S(2)}, u32[]{:S(2)}) collective-permute-start(bf16[384,1536]{1,0:T(8,128)(2,1)S(1)} %convolution_convert_fusion.2), channel_id=1, source_target_pairs={{0,2},{2,0},{1,3},{3,1},{4,6},{6,4},{5,7},{7,5},{8,10},{10,8},{9,1... | collective-permute-start | bytes 3538952 | tf_op jit(solution)/shard_map/ppermute | solution.py:523
  135.6 8.1 %copy-start.17 = (bf16[720,768]{1,0:T(8,128)(2,1)}, bf16[720,768]{1,0:T(8,128)(2,1)S(1)}, u32[]{:S(2)}) copy-start(bf16[720,768]{1,0:T(8,128)(2,1)S(1)} %get-tuple-element.201) | copy-start | bytes 3317764
  137.8 34.9 %collective-permute-start.11 = (bf16[768,768]{1,0:T(8,128)(2,1)}, bf16[768,768]{1,0:T(8,128)(2,1)}, u32[]{:S(2)}, u32[]{:S(2)}) collective-permute-start(bf16[768,768]{1,0:T(8,128)(2,1)} %add_convert_fusion.3), channel_id=1, source_target_pairs={{0,1},{1,0},{2,3},{3,2},{4,5},{5,4},{6,7},{7,6},{8,9},{9,8},{10,11... | collective-permute-start | bytes 3538952 | tf_op jit(solution)/shard_map/ppermute | solution.py:523
  140.2 7.2 %collective-permute-start.13 = (bf16[384,384]{1,0:T(8,128)(2,1)S(1)}, bf16[384,384]{1,0:T(8,128)(2,1)S(1)}, u32[]{:S(2)}, u32[]{:S(2)}) collective-permute-start(bf16[384,384]{1,0:T(8,128)(2,1)S(1)} %convolution_convert_fusion.17), channel_id=1, source_target_pairs={{0,2},{2,0},{1,3},{3,1},{4,6},{6,4},{5,7},{7,5},{8,10},{10,8},{9,1... | collective-permute-start | bytes 884744 | tf_op jit(solution)/shard_map/ppermute | solution.py:523
  145.0 29.4 %collective-permute-start.10 = (bf16[768,768]{1,0:T(8,128)(2,1)}, bf16[768,768]{1,0:T(8,128)(2,1)}, u32[]{:S(2)}, u32[]{:S(2)}) collective-permute-start(bf16[768,768]{1,0:T(8,128)(2,1)} %convolution_convert_fusion.8), channel_id=1, source_target_pairs={{0,2},{2,0},{1,3},{3,1},{4,6},{6,4},{5,7},{7,5},{8,10},{10,8},{9,1... | collective-permute-start | bytes 3538952 | tf_op jit(solution)/shard_map/ppermute | solution.py:523
  149.0 18.0 %copy-start.21 = (bf16[1,709,768]{2,1,0:T(8,128)(2,1)S(1)}, bf16[1,709,768]{2,1,0:T(8,128)(2,1)}, u32[]{:S(2)}) copy-start(bf16[1,709,768]{2,1,0:T(8,128)(2,1)} %param.22) | copy-start | bytes 3267076
  169.6 9.4 %collective-permute-start.14 = (bf16[384,1152]{1,0:T(8,128)(2,1)S(1)}, bf16[384,1152]{1,0:T(8,128)(2,1)S(1)}, u32[]{:S(2)}, u32[]{:S(2)}) collective-permute-start(bf16[384,1152]{1,0:T(8,128)(2,1)S(1)} %convolution_convert_fusion.6), channel_id=1, source_target_pairs={{0,2},{2,0},{1,3},{3,1},{4,6},{6,4},{5,7},{7,5},{8,10},{10,8},{9,1... | collective-permute-start | bytes 2654216 | tf_op jit(solution)/shard_map/ppermute | solution.py:523
  171.1 38.0 %collective-permute-start.15 = (bf16[384,1536]{1,0:T(8,128)(2,1)S(1)}, bf16[384,1536]{1,0:T(8,128)(2,1)}, u32[]{:S(2)}, u32[]{:S(2)}) collective-permute-start(bf16[384,1536]{1,0:T(8,128)(2,1)S(1)} %convolution_convert_fusion), channel_id=1, source_target_pairs={{0,2},{2,0},{1,3},{3,1},{4,6},{6,4},{5,7},{7,5},{8,10},{10,8},{9,1... | collective-permute-start | bytes 3538952 | tf_op jit(solution)/shard_map/ppermute | solution.py:523
  171.4 37.7 %collective-permute-start.16 = (bf16[384,384]{1,0:T(8,128)(2,1)}, bf16[384,384]{1,0:T(8,128)(2,1)}, u32[]{:S(2)}, u32[]{:S(2)}) collective-permute-start(bf16[384,384]{1,0:T(8,128)(2,1)} %convolution_convert_fusion.15), channel_id=1, source_target_pairs={{0,2},{2,0},{1,3},{3,1},{4,6},{6,4},{5,7},{7,5},{8,10},{10,8},{9,1... | collective-permute-start | bytes 884744 | tf_op jit(solution)/shard_map/ppermute | solution.py:523
  172.7 35.2 %collective-permute-start.17 = (bf16[384,1920]{1,0:T(8,128)(2,1)S(1)}, bf16[384,1920]{1,0:T(8,128)(2,1)S(1)}, u32[]{:S(2)}, u32[]{:S(2)}) collective-permute-start(bf16[384,1920]{1,0:T(8,128)(2,1)S(1)} %copy-done.11), channel_id=1, source_target_pairs={{0,1},{1,0},{2,3},{3,2},{4,5},{5,4},{6,7},{7,6},{8,9},{9,8},{10,11... | collective-permute-start | bytes 4423688 | tf_op jit(solution)/shard_map/ppermute | solution.py:523
  177.5 27.0 %collective-permute-start.18 = (bf16[384,768]{1,0:T(8,128)(2,1)S(1)}, bf16[384,768]{1,0:T(8,128)(2,1)}, u32[]{:S(2)}, u32[]{:S(2)}) collective-permute-start(bf16[384,768]{1,0:T(8,128)(2,1)S(1)} %get-tuple-element.212), channel_id=1, source_target_pairs={{0,4},{4,0},{8,12},{12,8},{16,20},{20,16},{24,28},{28,24},{1,5},{5... | collective-permute-start | bytes 1769480 | tf_op jit(solution)/shard_map/ppermute | solution.py:523
  202.0 7.1 %copy-start.34 = (bf16[384,384]{1,0:T(8,128)(2,1)S(1)}, bf16[384,384]{1,0:T(8,128)(2,1)}, u32[]{:S(2)}) copy-start(bf16[384,384]{1,0:T(8,128)(2,1)} %convolution_convert_fusion.16) | copy-start | bytes 884740
  203.9 25.7 %collective-permute-start.22 = (bf16[384,1152]{1,0:T(8,128)(2,1)}, bf16[384,1152]{1,0:T(8,128)(2,1)S(1)}, u32[]{:S(2)}, u32[]{:S(2)}) collective-permute-start(bf16[384,1152]{1,0:T(8,128)(2,1)} %fusion.16.refs_6_), channel_id=1, source_target_pairs={{0,1},{1,0},{2,3},{3,2},{4,5},{5,4},{6,7},{7,6},{8,9},{9,8},{10,11... | collective-permute-start | bytes 2654216 | tf_op jit(solution)/shard_map/ppermute | solution.py:523
  204.5 25.2 %collective-permute-start.21 = (bf16[384,1152]{1,0:T(8,128)(2,1)}, bf16[384,1152]{1,0:T(8,128)(2,1)S(1)}, u32[]{:S(2)}, u32[]{:S(2)}) collective-permute-start(bf16[384,1152]{1,0:T(8,128)(2,1)} %convolution_convert_fusion.5), channel_id=1, source_target_pairs={{0,2},{2,0},{1,3},{3,1},{4,6},{6,4},{5,7},{7,5},{8,10},{10,8},{9,1... | collective-permute-start | bytes 2654216 | tf_op jit(solution)/shard_map/ppermute | solution.py:523
  212.0 17.6 %collective-permute-start.20 = (bf16[192,1920]{1,0:T(8,128)(2,1)S(1)}, bf16[192,1920]{1,0:T(8,128)(2,1)S(1)}, u32[]{:S(2)}, u32[]{:S(2)}) collective-permute-start(bf16[192,1920]{1,0:T(8,128)(2,1)S(1)} %get-tuple-element.211), channel_id=1, source_target_pairs={{0,4},{4,0},{8,12},{12,8},{16,20},{20,16},{24,28},{28,24},{1,5},{5... | collective-permute-start | bytes 2211848 | tf_op jit(solution)/shard_map/ppermute | solution.py:523
  214.5 15.2 %collective-permute-start.19 = (bf16[192,768]{1,0:T(8,128)(2,1)S(1)}, bf16[192,768]{1,0:T(8,128)(2,1)S(1)}, u32[]{:S(2)}, u32[]{:S(2)}) collective-permute-start(bf16[192,768]{1,0:T(8,128)(2,1)S(1)} %get-tuple-element.219), channel_id=1, source_target_pairs={{0,8},{4,12},{8,0},{12,4},{16,24},{20,28},{24,16},{28,20},{1,9},{5... | collective-permute-start | bytes 884744 | tf_op jit(solution)/shard_map/ppermute | solution.py:523
  216.0 13.6 %copy-start.24 = (bf16[384,1152]{1,0:T(8,128)(2,1)S(1)}, bf16[384,1152]{1,0:T(8,128)(2,1)}, u32[]{:S(2)}) copy-start(bf16[384,1152]{1,0:T(8,128)(2,1)} %convolution_convert_fusion.4.refs_5_) | copy-start | bytes 2654212
  231.2 15.4 %collective-permute-start.25 = (bf16[192,1152]{1,0:T(8,128)(2,1)S(1)}, bf16[192,1152]{1,0:T(8,128)(2,1)S(1)}, u32[]{:S(2)}, u32[]{:S(2)}) collective-permute-start(bf16[192,1152]{1,0:T(8,128)(2,1)S(1)} %get-tuple-element.215), channel_id=1, source_target_pairs={{0,4},{4,0},{8,12},{12,8},{16,20},{20,16},{24,28},{28,24},{1,5},{5... | collective-permute-start | bytes 1327112 | tf_op jit(solution)/shard_map/ppermute | solution.py:523
  233.3 13.2 %collective-permute-start.24 = (bf16[96,1920]{1,0:T(8,128)(2,1)S(1)}, bf16[96,1920]{1,0:T(8,128)(2,1)S(1)}, u32[]{:S(2)}, u32[]{:S(2)}) collective-permute-start(bf16[96,1920]{1,0:T(8,128)(2,1)S(1)} %get-tuple-element.217), channel_id=1, source_target_pairs={{0,8},{4,12},{8,0},{12,4},{16,24},{20,28},{24,16},{28,20},{1,9},{5... | collective-permute-start | bytes 1105928 | tf_op jit(solution)/shard_map/ppermute | solution.py:523
  235.6 10.9 %collective-permute-start.23 = (bf16[96,768]{1,0:T(8,128)(2,1)S(1)}, bf16[96,768]{1,0:T(8,128)(2,1)S(1)}, u32[]{:S(2)}, u32[]{:S(2)}) collective-permute-start(bf16[96,768]{1,0:T(8,128)(2,1)S(1)} %get-tuple-element.227), channel_id=1, source_target_pairs={{0,16},{4,20},{8,24},{12,28},{16,0},{20,4},{24,8},{28,12},{1,17},{... | collective-permute-start | bytes 442376 | tf_op jit(solution)/shard_map/ppermute | solution.py:523
  238.2 8.4 %copy-start.10 = (bf16[192,1152]{1,0:T(8,128)(2,1)S(1)}, bf16[192,1152]{1,0:T(8,128)(2,1)}, u32[]{:S(2)}) copy-start(bf16[192,1152]{1,0:T(8,128)(2,1)} %get-tuple-element.214.refs_3_) | copy-start | bytes 1327108
  247.7 16.0 %collective-permute-start.28 = (bf16[96,1152]{1,0:T(8,128)(2,1)S(1)}, bf16[96,1152]{1,0:T(8,128)(2,1)S(1)}, u32[]{:S(2)}, u32[]{:S(2)}) collective-permute-start(bf16[96,1152]{1,0:T(8,128)(2,1)S(1)} %get-tuple-element.223), channel_id=1, source_target_pairs={{0,8},{4,12},{8,0},{12,4},{16,24},{20,28},{24,16},{28,20},{1,9},{5... | collective-permute-start | bytes 663560 | tf_op jit(solution)/shard_map/ppermute | solution.py:523
  249.1 14.6 %collective-permute-start.27 = (bf16[48,1920]{1,0:T(8,128)(2,1)S(1)}, bf16[48,1920]{1,0:T(8,128)(2,1)S(1)}, u32[]{:S(2)}, u32[]{:S(2)}) collective-permute-start(bf16[48,1920]{1,0:T(8,128)(2,1)S(1)} %get-tuple-element.225), channel_id=1, source_target_pairs={{0,16},{4,20},{8,24},{12,28},{16,0},{20,4},{24,8},{28,12},{1,17},{... | collective-permute-start | bytes 552968 | tf_op jit(solution)/shard_map/ppermute | solution.py:523
  250.7 13.0 %collective-permute-start.26 = (bf16[96,768]{1,0:T(8,128)(2,1)S(1)}, bf16[96,768]{1,0:T(8,128)(2,1)S(1)}, u32[]{:S(2)}, u32[]{:S(2)}) collective-permute-start(bf16[96,768]{1,0:T(8,128)(2,1)S(1)} %add_convert_fusion.12.refs_5_), channel_id=1, source_target_pairs={{0,16},{4,20},{8,24},{12,28},{16,0},{20,4},{24,8},{28,12},{1,17},{... | collective-permute-start | bytes 442376 | tf_op jit(solution)/shard_map/ppermute | solution.py:523
  252.0 11.7 %copy-start.25 = (bf16[96,1152]{1,0:T(8,128)(2,1)S(1)}, bf16[96,1152]{1,0:T(8,128)(2,1)}, u32[]{:S(2)}) copy-start(bf16[96,1152]{1,0:T(8,128)(2,1)} %get-tuple-element.222.refs_4_) | copy-start | bytes 663556
  252.0 12.4 %copy-start.26 = (bf16[48,1920]{1,0:T(8,128)(2,1)S(1)}, bf16[48,1920]{1,0:T(8,128)(2,1)}, u32[]{:S(2)}) copy-start(bf16[48,1920]{1,0:T(8,128)(2,1)} %get-tuple-element.224.refs_3_) | copy-start | bytes 552964
  265.5 11.8 %collective-permute-start.31 = (bf16[48,1152]{1,0:T(8,128)(2,1)S(1)}, bf16[48,1152]{1,0:T(8,128)(2,1)S(1)}, u32[]{:S(2)}, u32[]{:S(2)}) collective-permute-start(bf16[48,1152]{1,0:T(8,128)(2,1)S(1)} %get-tuple-element.229), channel_id=1, source_target_pairs={{0,16},{4,20},{8,24},{12,28},{16,0},{20,4},{24,8},{28,12},{1,17},{... | collective-permute-start | bytes 331784 | tf_op jit(solution)/shard_map/ppermute | solution.py:523
  265.6 13.9 %collective-permute-start.30 = (bf16[48,1920]{1,0:T(8,128)(2,1)S(1)}, bf16[48,1920]{1,0:T(8,128)(2,1)S(1)}, u32[]{:S(2)}, u32[]{:S(2)}) collective-permute-start(bf16[48,1920]{1,0:T(8,128)(2,1)S(1)} %add_convert_fusion.11.refs_3_), channel_id=1, source_target_pairs={{0,16},{4,20},{8,24},{12,28},{16,0},{20,4},{24,8},{28,12},{1,17},{... | collective-permute-start | bytes 552968 | tf_op jit(solution)/shard_map/ppermute | solution.py:523
  268.5 11.7 %collective-permute-start.29 = (bf16[192,768]{1,0:T(8,128)(2,1)S(1)}, bf16[192,768]{1,0:T(8,128)(2,1)S(1)}, u32[]{:S(2)}, u32[]{:S(2)}) collective-permute-start(bf16[192,768]{1,0:T(8,128)(2,1)S(1)} %pad_maximum_fusion.17.refs_5_), channel_id=1, source_target_pairs={{0,8},{4,12},{8,0},{12,4},{16,24},{20,28},{24,16},{28,20},{1,9},{5... | collective-permute-start | bytes 884744 | tf_op jit(solution)/shard_map/ppermute | solution.py:523
  268.6 11.6 %copy-start.7 = (bf16[96,768]{1,0:T(8,128)(2,1)S(1)}, bf16[96,768]{1,0:T(8,128)(2,1)}, u32[]{:S(2)}) copy-start(bf16[96,768]{1,0:T(8,128)(2,1)} %copy-done.6) | copy-start | bytes 442372
  268.6 11.6 %copy-start.32 = (bf16[48,1152]{1,0:T(8,128)(2,1)S(1)}, bf16[48,1152]{1,0:T(8,128)(2,1)}, u32[]{:S(2)}) copy-start(bf16[48,1152]{1,0:T(8,128)(2,1)} %get-tuple-element.228.refs_4_) | copy-start | bytes 331780
  281.5 9.6 %collective-permute-start.33 = (bf16[48,1152]{1,0:T(8,128)(2,1)S(1)}, bf16[48,1152]{1,0:T(8,128)(2,1)S(1)}, u32[]{:S(2)}, u32[]{:S(2)}) collective-permute-start(bf16[48,1152]{1,0:T(8,128)(2,1)S(1)} %add_convert_fusion.13.refs_19_), channel_id=1, source_target_pairs={{0,16},{4,20},{8,24},{12,28},{16,0},{20,4},{24,8},{28,12},{1,17},{... | collective-permute-start | bytes 331784 | tf_op jit(solution)/shard_map/ppermute | solution.py:523
  282.9 10.5 %collective-permute-start.32 = (bf16[96,1920]{1,0:T(8,128)(2,1)S(1)}, bf16[96,1920]{1,0:T(8,128)(2,1)S(1)}, u32[]{:S(2)}, u32[]{:S(2)}) collective-permute-start(bf16[96,1920]{1,0:T(8,128)(2,1)S(1)} %pad_maximum_fusion.16.refs_18_), channel_id=1, source_target_pairs={{0,8},{4,12},{8,0},{12,4},{16,24},{20,28},{24,16},{28,20},{1,9},{5... | collective-permute-start | bytes 1105928 | tf_op jit(solution)/shard_map/ppermute | solution.py:523
  285.3 18.7 %collective-permute-start.36 = (bf16[384,768]{1,0:T(8,128)(2,1)S(1)}, bf16[384,768]{1,0:T(8,128)(2,1)S(1)}, u32[]{:S(2)}, u32[]{:S(2)}) collective-permute-start(bf16[384,768]{1,0:T(8,128)(2,1)S(1)} %pad_maximum_fusion.14.refs_20_), channel_id=1, source_target_pairs={{0,4},{4,0},{8,12},{12,8},{16,20},{20,16},{24,28},{28,24},{1,5},{5... | collective-permute-start | bytes 1769480 | tf_op jit(solution)/shard_map/ppermute | solution.py:523
  285.3 9.0 %copy-start.5 = (bf16[48,1920]{1,0:T(8,128)(2,1)S(1)}, bf16[48,1920]{1,0:T(8,128)(2,1)}, u32[]{:S(2)}) copy-start(bf16[48,1920]{1,0:T(8,128)(2,1)} %copy-done.4) | copy-start | bytes 552964
  289.6 14.4 %collective-permute-start.35 = (f32[8,1536]{1,0:T(8,128)S(1)}, f32[8,1536]{1,0:T(8,128)S(1)}, u32[]{:S(2)}, u32[]{:S(2)}) collective-permute-start(f32[8,1536]{1,0:T(8,128)S(1)} %slice_bitcast_fusion.1), channel_id=1, source_target_pairs={{0,1},{1,0},{2,3},{3,2},{4,5},{5,4},{6,7},{7,6},{8,9},{9,8},{10,11... | collective-permute-start | bytes 147464 | tf_op jit(solution)/shard_map/ppermute | solution.py:523
  295.3 8.7 %collective-permute-start.34 = (bf16[96,1152]{1,0:T(8,128)(2,1)S(1)}, bf16[96,1152]{1,0:T(8,128)(2,1)S(1)}, u32[]{:S(2)}, u32[]{:S(2)}) collective-permute-start(bf16[96,1152]{1,0:T(8,128)(2,1)S(1)} %pad_maximum_fusion.18.refs_8_), channel_id=1, source_target_pairs={{0,8},{4,12},{8,0},{12,4},{16,24},{20,28},{24,16},{28,20},{1,9},{5... | collective-permute-start | bytes 663560 | tf_op jit(solution)/shard_map/ppermute | solution.py:523
  296.1 9.0 %copy-start.40 = (f32[2,8,1536]{2,1,0:T(8,128)S(1)}, f32[2,8,1536]{2,1,0:T(8,128)}, u32[]{:S(2)}) copy-start(f32[2,8,1536]{2,1,0:T(8,128)} %pack_sums.1) | copy-start | bytes 294916
  304.0 14.3 %copy-start.9 = (f32[709,768]{1,0:T(8,128)S(1)}, f32[709,768]{1,0:T(8,128)}, u32[]{:S(2)}) copy-start(f32[709,768]{1,0:T(8,128)} %grad_tokens.1) | copy-start | bytes 6534148
  305.1 17.3 %collective-permute-start.39 = (bf16[768,768]{1,0:T(8,128)(2,1)}, bf16[768,768]{1,0:T(8,128)(2,1)}, u32[]{:S(2)}, u32[]{:S(2)}) collective-permute-start(bf16[768,768]{1,0:T(8,128)(2,1)} %pad_maximum_fusion.10.mine_ref), channel_id=1, source_target_pairs={{0,2},{2,0},{1,3},{3,1},{4,6},{6,4},{5,7},{7,5},{8,10},{10,8},{9,1... | collective-permute-start | bytes 3538952 | tf_op jit(solution)/shard_map/ppermute | solution.py:523
  305.1 2.5 collective-permute-start.41
  307.7 4.1 %collective-permute-start.42 = (f32[8,1536]{1,0:T(8,128)S(1)}, f32[8,1536]{1,0:T(8,128)S(1)}, u32[]{:S(2)}, u32[]{:S(2)}) collective-permute-start(f32[8,1536]{1,0:T(8,128)S(1)} %add.413), channel_id=1, source_target_pairs={{0,4},{4,0},{8,12},{12,8},{16,20},{20,16},{24,28},{28,24},{1,5},{5... | collective-permute-start | bytes 147464 | tf_op jit(solution)/shard_map/ppermute | solution.py:523
  311.8 4.2 %collective-permute-start.43 = (f32[8,1536]{1,0:T(8,128)S(1)}, f32[8,1536]{1,0:T(8,128)S(1)}, u32[]{:S(2)}, u32[]{:S(2)}) collective-permute-start(f32[8,1536]{1,0:T(8,128)S(1)} %add.414), channel_id=1, source_target_pairs={{0,8},{4,12},{8,0},{12,4},{16,24},{20,28},{24,16},{28,20},{1,9},{5... | collective-permute-start | bytes 147464 | tf_op jit(solution)/shard_map/ppermute | solution.py:523
  313.6 27.1 %collective-permute-start.37 = (bf16[192,1920]{1,0:T(8,128)(2,1)}, bf16[192,1920]{1,0:T(8,128)(2,1)S(1)}, u32[]{:S(2)}, u32[]{:S(2)}) collective-permute-start(bf16[192,1920]{1,0:T(8,128)(2,1)} %pad_maximum_fusion.12.refs_7_), channel_id=1, source_target_pairs={{0,4},{4,0},{8,12},{12,8},{16,20},{20,16},{24,28},{28,24},{1,5},{5... | collective-permute-start | bytes 2211848 | tf_op jit(solution)/shard_map/ppermute | solution.py:523
  314.0 26.7 %collective-permute-start.38 = (bf16[192,1152]{1,0:T(8,128)(2,1)S(1)}, bf16[192,1152]{1,0:T(8,128)(2,1)S(1)}, u32[]{:S(2)}, u32[]{:S(2)}) collective-permute-start(bf16[192,1152]{1,0:T(8,128)(2,1)S(1)} %pad_maximum_fusion.15), channel_id=1, source_target_pairs={{0,4},{4,0},{8,12},{12,8},{16,20},{20,16},{24,28},{28,24},{1,5},{5... | collective-permute-start | bytes 1327112 | tf_op jit(solution)/shard_map/ppermute | solution.py:523
  315.9 5.9 %collective-permute-start.44 = (f32[8,1536]{1,0:T(8,128)S(1)}, f32[8,1536]{1,0:T(8,128)S(1)}, u32[]{:S(2)}, u32[]{:S(2)}) collective-permute-start(f32[8,1536]{1,0:T(8,128)S(1)} %add.415), channel_id=1, source_target_pairs={{0,16},{4,20},{8,24},{12,28},{16,0},{20,4},{24,8},{28,12},{1,17},{... | collective-permute-start | bytes 147464 | tf_op jit(solution)/shard_map/ppermute | solution.py:523
  340.9 9.4 %collective-permute-start.45 = (bf16[384,1920]{1,0:T(8,128)(2,1)S(1)}, bf16[384,1920]{1,0:T(8,128)(2,1)}, u32[]{:S(2)}, u32[]{:S(2)}) collective-permute-start(bf16[384,1920]{1,0:T(8,128)(2,1)S(1)} %pad_maximum_fusion.9.mine_ref), channel_id=1, source_target_pairs={{0,2},{2,0},{1,3},{3,1},{4,6},{6,4},{5,7},{7,5},{8,10},{10,8},{9,1... | collective-permute-start | bytes 4423688 | tf_op jit(solution)/shard_map/ppermute | solution.py:523
  341.9 3.8 %collective-permute-start.40 = (bf16[384,1152]{1,0:T(8,128)(2,1)}, bf16[384,1152]{1,0:T(8,128)(2,1)S(1)}, u32[]{:S(2)}, u32[]{:S(2)}) collective-permute-start(bf16[384,1152]{1,0:T(8,128)(2,1)} %constant_dynamic-update-slice_fusion.mine_ref), channel_id=1, source_target_pairs={{0,2},{2,0},{1,3},{3,1},{4,6},{6,4},{5,7},{7,5},{8,10},{10,8},{9,1... | collective-permute-start | bytes 2654216 | tf_op jit(solution)/shard_map/ppermute | solution.py:523
  350.3 7.5 %copy-start.1 = (bf16[768,1536]{1,0:T(8,128)(2,1)S(1)}, bf16[768,1536]{1,0:T(8,128)(2,1)}, u32[]{:S(2)}) copy-start(bf16[768,1536]{1,0:T(8,128)(2,1)} %param.37) | copy-start | bytes 7077892
  (31 other events, 78.6 us)
